TPU v7x, 128 devices: a whole 4x4x4 slice. The times are simulated.
128 devices in a mesh: ex: 32 (over x, y, core), layer: 4 (over z).
Axes of the slice: x: 4, y: 4, z: 4, core: 2. Of those that a mesh axis runs over, the one named last changes fastest.
Arguments:
- store: bfloat16 [131072, 8192], P('ex', 'layer'), as said below
- precond: bfloat16 [4, 2048, 2048], P('layer', 'ex'), as said below
- query_slots: bfloat16 [32, 2, 64, 8192], P('ex', None, None, 'layer'), may hold values from -6 to 6
- owners: int32 [2], replicated, may hold values from 0 to 31
Outputs:
- scores: float32 [131072, 128], P('ex', 'layer')
Inputs may be any that keep to these rules, and one draw needn't show every extreme that they name: `store`: training gradients with varying example and entry scales. `precond`: a dense preconditioner for each layer block.
All inputs are finite; a program needn't handle non-finite values.
Results may differ from a plain program's by a relative error of at most 0.0029.
Values may be sent and summed in bfloat16 or wider, within the bound.
No kernel may reach another device: no remote copies, remote signals or barrier semaphores. Data moves between devices by JAX's collectives and lax.ppermute only.
A program may use at most 128 MiB of HBM per device.

v0:
```python
import jax
import jax.numpy as jnp
from jax import lax
from jax.sharding import PartitionSpec as P


def broadcast(block, axis, source):
    block = jnp.where(lax.axis_index(axis) == source, block, jnp.zeros_like(block))
    return lax.psum(block, axis)


def shards(store, precond, query_slots, owners):
    local = query_slots[0]
    received = []
    for blocknum in range(local.shape[0]):
        received.append(broadcast(local[blocknum], "ex", owners[blocknum]))
    raw = jnp.concatenate(received, axis=0)
    weight = precond[0]
    summed = jnp.dot(
        raw, lax.all_gather(weight, "ex", axis=0, tiled=True), preferred_element_type=jnp.float32
    )
    pre = summed.astype(jnp.bfloat16)
    qnorm = jnp.sum(jnp.square(pre.astype(jnp.float32)), axis=1)
    gnorm = jnp.sum(jnp.square(store.astype(jnp.float32)), axis=1)
    dots = lax.dot_general(store, pre, (((1,), (1,)), ((), ())), preferred_element_type=jnp.float32)
    groups = lax.axis_size("layer")
    width = dots.shape[1] // groups
    factor = jnp.sqrt(jnp.float32(store.shape[1] * groups))
    first = lax.axis_index("layer") * width
    dots_all, gnorm_all, qnorm_all = lax.psum((dots, gnorm, qnorm), "layer")
    mine = lax.dynamic_slice_in_dim(dots_all, first, width, 1)
    qnorm_mine = lax.dynamic_slice_in_dim(qnorm_all, first, width, 0)
    return (
        mine
        * lax.rsqrt(gnorm_all + 1e-06)[:, None]
        * lax.rsqrt(qnorm_mine + 1e-06)[None, :]
        * factor
    )


def solution(mesh):
    return jax.shard_map(
        shards,
        mesh=mesh,
        in_specs=(P("ex", "layer"), P("layer", "ex", None), P("ex", None, None, "layer"), P()),
        out_specs=P("ex", "layer"),
        check_vma=False,
    )
```

profile of v0, /device:TPU:1, one launch (start us, length us, event | category | flops | bytes accessed | tf_op | source)
XLA Modules:
  0.0 257.9 jit_solution(1232442730883552394)
XLA Ops:
  6.5 0.0 all-reduce.7.cloned.1.call-start
  6.5 1.3 fusion.9
  9.1 1.9 select_bitcast_fusion.1
  10.9 0.0 all-reduce.7.cloned.1.call-update
  11.0 0.0 all-gather.3.cloned.1.call-start
  11.0 0.7 all-gather.3.cloned.1.call-update
  11.7 0.0 all-reduce.5.cloned.1.call-start
  11.8 105.9 %all-reduce.7.cloned.1.call-done = (bf16[64,2048]{1,0:T(8,128)(2,1)}, bf16[64,2048]{1,0:T(8,128)(2,1)}) async-done(((bf16[64,2048]{1,0:T(8,128)(2,1)}, bf16[64,2048]{1,0:T(8,128)(2,1)}), (bf16[64,2048]{1,0:T(8,128)(2,1)}, bf16[64,2048]{1,0:T(8,128)(2,1)})) %all-reduce.7.cloned.1.call-update) | async-done | bytes 524304 | tf_op jit(solution)/shard_map/psum | solution.py:9
  117.6 55.3 %all-gather.3.cloned.1.call-done = bf16[1,2048,2048]{2,1,0:T(8,128)(2,1)} async-done(((bf16[1,64,2048]{2,1,0:T(8,128)(2,1)}), bf16[1,2048,2048]{2,1,0:T(8,128)(2,1)}) %all-gather.3.cloned.1.call-update) | async-done | bytes 8388624 | tf_op jit(solution)/shard_map/all_gather | solution.py:20
  172.9 4.9 %multiply_reduce_fusion.1 = (f32[128]{0:T(128)S(1)}, bf16[128,2048]{1,0:T(8,128)(2,1)S(1)}) fusion(bf16[1,2048,2048]{2,1,0:T(8,128)(2,1)} %all-gather.3.cloned.1.call-done, bf16[64,2048]{1,0:T(8,128)(2,1)} %get-tuple-element.7, bf16[64,2048]{1,0:T(8,128)(2,1)} %get-tuple-element.8), kind=kOutput, calls=%fused_computation.5 | convolution fusion | flops 1075838848 | bytes 9437696 | tf_op jit(solution)/shard_map/dot_general | solution.py:19
  177.9 12.7 %convolution_bitcast_fusion = f32[4096,128]{0,1:T(8,128)} fusion(bf16[128,2048]{1,0:T(8,128)(2,1)S(1)} %get-tuple-element.14, bf16[4096,2048]{1,0:T(8,128)(2,1)} %param.4), kind=kOutput, calls=%fused_computation.3 | convolution fusion | flops 2147483648 | bytes 19398656 | tf_op jit(solution)/shard_map/dot_general | solution.py:25
  190.6 0.0 all-reduce.5.cloned.1.call-update
  190.6 7.2 %multiply_reduce_fusion = f32[4096]{0:T(1024)S(1)} fusion(bf16[4096,2048]{1,0:T(8,128)(2,1)} %param.4), kind=kLoop, calls=%fused_computation | loop fusion | flops 25161728 | bytes 16793600 | tf_op jit(solution)/shard_map/reduce_sum | solution.py:24
  197.8 15.6 %all-reduce = (f32[128]{0:T(128)S(1)}, f32[4096]{0:T(1024)S(1)}) all-reduce(f32[128]{0:T(128)S(1)} %get-tuple-element.13, f32[4096]{0:T(1024)S(1)} %multiply_reduce_fusion), channel_id=1, replica_groups=mesh['ex'=32,'layer'=4] {'layer'}, use_global_device_ids=true, to_apply=%region_6.7 | all-reduce | flops 4224 | bytes 33792 | tf_op jit(solution)/shard_map/psum | solution.py:30
  213.4 0.1 add_rsqrt_fusion.1
  213.5 35.9 %all-reduce.5.cloned.1.call-done = f32[4096,128]{0,1:T(8,128)} async-done(((f32[4096,128]{0,1:T(8,128)}), f32[4096,128]{0,1:T(8,128)}) %all-reduce.5.cloned.1.call-update) | async-done | bytes 2097168 | tf_op jit(solution)/shard_map/psum | solution.py:30
  249.4 1.9 multiply_multiply_fusion
  (1 shorter events, 0.0 us)
Async XLA Ops:
  6.5 111.1 %all-reduce.7.cloned.1.call-start = ((), (), s32[]{:S(2)}) async-start(), calls=%async_computation.2 | async-start | bytes 1048576 | tf_op jit(solution)/shard_map/psum | solution.py:9
  11.0 162.0 %all-gather.3.cloned.1.call-start = ((), (), s32[]{:S(2)}) async-start(), calls=%async_computation.1 | async-start | bytes 8650752 | tf_op jit(solution)/shard_map/all_gather | solution.py:20
  11.7 237.7 %all-reduce.5.cloned.1.call-start = ((), (), s32[]{:S(2)}) async-start(), calls=%async_computation | async-start | bytes 4194304 | tf_op jit(solution)/shard_map/psum | solution.py:30
Sparse Core Ops, SparseCore 0:
  11.1 106.5 all-reduce.6
  120.1 52.7 all-gather.2
  190.7 58.6 all-reduce.4
where the time goes:
time: 258 us
  waiting for transfers between devices  198 us (77%)
  matrix products  17.6 us (7%)
  blocking collectives  15.6 us (6%)
  between operations  14.3 us (6%)
  other arithmetic  11.1 us (4%)
    psum x1, waiting for transfers between devices, broadcast(): return lax.psum(block, axis)  106 us
    all_gather x1, waiting for transfers between devices, shards(): lax.all_gather(weight, 'ex', axis=0, tiled=True)  55.3 us
    psum x1, waiting for transfers between devices, shards(): dots_all, gnorm_all, qnorm_all = lax.psum((dots, gnorm, qnorm), 'layer')  35.9 us
    psum x1, blocking collectives, shards(): dots_all, gnorm_all, qnorm_all = lax.psum((dots, gnorm, qnorm), 'layer')  15.6 us
    dot_general x1, matrix products, shards(): lax.dot_general(store, pre, (((1,), (1,)), ((), ())), preferred_element_t...  12.7 us
    reduce_sum x1, other arithmetic, shards(): gnorm = jnp.sum(jnp.square(store.astype(jnp.float32)), axis=1)  7.19 us
  transfers between devices with their start and end apart: 3, of which 3 were waited for; matrix products, arithmetic and copies ran while one was open for 3% of the time, Pallas kernels for 0%

commit v1 on v0

v1 whole, which is shorter than its diff:
```python
import functools
import math

import jax
import jax.numpy as jnp
from jax import lax
from jax.experimental import pallas as pl
from jax.experimental.pallas import tpu as pltpu
from jax.sharding import PartitionSpec as P

BF16, F32 = jnp.bfloat16, jnp.float32
NT = (((1,), (1,)), ((), ()))
VMEM = pltpu.VMEM
NX = NY = 4
NZ = 4


def shape(dims, dtype):
    return jax.ShapeDtypeStruct(dims, dtype)


def place():
    e = lax.axis_index("ex")
    return e // 8, (e // 2) % 4, e % 2


def owner_place(owners_ref, block):
    o = owners_ref[block]
    return o // 8, (o // 2) % 4, o % 2


def at(start, size):
    return pl.ds(pl.multiple_of(start, size), size)


def call(body, name, ins, outs, scratch=(), limit=24 << 20, flops=0, moved=1 << 20):
    specs = []
    for a in ins:
        if a.dtype == jnp.int32:
            specs.append(pl.BlockSpec(memory_space=pltpu.SMEM))
        else:
            specs.append(pl.BlockSpec(memory_space=VMEM))
    return pl.pallas_call(
        body,
        name=name,
        in_specs=specs,
        out_specs=[pl.BlockSpec(memory_space=VMEM)] * len(outs),
        out_shape=outs,
        scratch_shapes=scratch,
        compiler_params=pltpu.CompilerParams(vmem_limit_bytes=limit),
        cost_estimate=pl.CostEstimate(flops=flops, bytes_accessed=moved, transcendentals=0),
    )(*ins)


def slices(owners, q, qo, p, po, a0, a1, a2, a3, b0, b1, b2, b3):
    x, y, c = place()
    for block in range(2):
        rows = slice(64 * block, 64 * block + 64)
        mine = owner_place(owners, block)[2] == c
        for d, a in enumerate((a0, a1, a2, a3)):
            columns = at(lax.rem(x + d, 4) * 512, 512)

            @pl.when(mine)
            def _():
                a[rows, :] = q[rows, columns]

            @pl.when(jnp.logical_not(mine))
            def _():
                a[rows, :] = qo[rows, columns]

    for d, b in enumerate((b0, b1, b2, b3)):
        columns = at(c * 1024 + lax.rem(y + d, 4) * 256, 256)
        b[at(c * 64, 64), :] = p[:, columns]
        b[at(64 - c * 64, 64), :] = po[:, columns]


def pack(owners, a0, a1, a2, a3, b1, b2, b3, r, t1, t2, t3):
    x, _, _ = place()
    for block in range(2):
        rows = slice(64 * block, 64 * block + 64)
        back = lax.rem(x - owner_place(owners, block)[0] + 4, 4)
        for d, a in enumerate((a0, a1, a2, a3)):

            @pl.when(back == d)
            def _():
                r[rows, :] = a[rows, :]

    for b, t in ((b1, t1), (b2, t2), (b3, t3)):
        t[:, 0:512] = r[...]
        t[:, 512:768] = b[...]


def product(owners, r, b0, u1, u2, u3, s, raw):
    _, y, _ = place()
    for block in range(2):
        rows = slice(64 * block, 64 * block + 64)
        back = lax.rem(y - owner_place(owners, block)[1] + 4, 4)
        for d, u in enumerate((r, u1, u2, u3)):

            @pl.when(back == d)
            def _():
                raw[rows, :] = u[rows, 0:512]

    total = None
    for d, u in enumerate((b0, u1, u2, u3)):
        piece = u[...] if d == 0 else u[:, 512:768]
        columns = at(lax.rem(y - d + 4, 4) * 128, 128)
        term = jnp.dot(raw[:, columns], piece, preferred_element_type=F32)
        total = term if total is None else total + term
    s[...] = total


def round_sum(s0, s1, s2, s3, w):
    w[...] = ((s0[...] + s2[...]) + (s1[...] + s3[...])).astype(BF16)


def join(w, wo, j):
    _, _, c = place()
    j[:, at(c * 256, 256)] = w[...]
    j[:, at(256 - c * 256, 256)] = wo[...]


ROWS = 512
CHUNKS = 8


def dots(j0, j1, j2, j3, store, own, gn_own, qn_own, z1, z2, z3, pre, half, gn, blocks, sems):
    _, y, _ = place()
    layer = lax.axis_index("layer")
    copies = []
    for i in range(CHUNKS):
        copy = pltpu.make_async_copy(store.at[pl.ds(ROWS * i, ROWS), :], blocks.at[i], sems.at[i])
        copy.start()
        copies.append(copy)
    for d, j in enumerate((j0, j1, j2, j3)):
        origin = lax.rem(y - d + 4, 4) * 256
        for c in range(2):
            pre[:, at(c * 1024 + origin, 256)] = j[:, 256 * c:256 * c + 256]
    q = jnp.square(pre[...].astype(F32))
    qsum = jnp.sum(q, axis=1, keepdims=True)
    qparts = jnp.broadcast_to(qsum, (128, 128))
    gn[...] = qparts
    zs = (None, z1, z2, z3)
    for d in range(4):
        rows = at(lax.rem(layer + d, 4) * 32, 32)
        half[32 * d:32 * d + 32, :] = pre[rows, :] * jnp.asarray(0.5, BF16)
        part = gn[rows, :]
        if d == 0:
            qn_own[...] = part * 0.5
        else:
            part = part * 0.5
            hi = part.astype(BF16)
            lo = (part - hi.astype(F32)).astype(BF16)
            lane = lax.broadcasted_iota(jnp.int32, (32, 128), 1)
            both = jnp.where(lane < 64, hi.astype(F32), lo.astype(F32))
            zs[d][:, 4352:4480] = both.astype(BF16)
    for i in range(CHUNKS):
        copies[i].wait()
        columns = slice(ROWS * i, ROWS * i + ROWS)
        s = blocks[i]
        out = lax.dot_general(s, half[...], NT, preferred_element_type=F32).T
        own[:, columns] = out[0:32, :]
        for d in range(1, 4):
            zs[d][:, columns] = out[32 * d:32 * d + 32, :].astype(BF16)
        squares = None
        for k in range(16):
            v = s[:, 128 * k:128 * k + 128].astype(F32)
            squares = v * v if squares is None else squares + v * v
        line = jnp.sum(squares.T, axis=0, keepdims=True) * 0.5
        for k in range(ROWS // 128):
            row = (ROWS // 128) * i + k
            gn_own[row:row + 1, :] = line[:, 128 * k:128 * k + 128]
    g = gn_own[...]
    hi = g.astype(BF16)
    lo = (g - hi.astype(F32)).astype(BF16)
    for d in range(1, 4):
        zs[d][:, 4096:4224] = hi
        zs[d][:, 4224:4352] = lo


def finish(own, gn_own, qn_own, z1, z2, z3, out):
    g = gn_own[...]
    q = qn_own[:, 0:1]
    for z in (z1, z2, z3):
        g = g + (z[:, 4096:4224].astype(F32) + z[:, 4224:4352].astype(F32))
        q = q + (z[:, 4352:4353].astype(F32) + z[:, 4416:4417].astype(F32))
    g = lax.rsqrt(g * 2.0 + 1e-06)
    q = lax.rsqrt(q * 2.0 + 1e-06) * (2.0 * math.sqrt(8192.0))
    for i in range(32):
        columns = slice(128 * i, 128 * i + 128)
        t = (own[:, columns] + z2[:, columns].astype(F32)) + (
            z1[:, columns].astype(F32) + z3[:, columns].astype(F32)
        )
        out[:, columns] = t * g[i:i + 1, :] * q


def moved(dx, dy, dc):
    pairs = []
    for x in range(4):
        for y in range(4):
            for c in range(2):
                to = ((x + dx) % 4 * 4 + (y + dy) % 4) * 2 + (c + dc) % 2
                pairs.append(((x * 4 + y) * 2 + c, to))
    return pairs


def send(a, dx=0, dy=0, dc=0):
    return lax.ppermute(a, "ex", moved(dx, dy, dc))


def send_layer(a, d):
    return lax.ppermute(a, "layer", [(i, (i + d) % 4) for i in range(4)])


def shards(store, precond, query_slots, owners):
    q = query_slots.reshape(128, 2048)
    p = precond.reshape(64, 2048)
    qo = send(q, dc=1)
    po = send(p, dc=1)
    piece = shape((128, 512), BF16)
    block = shape((128, 256), BF16)
    a0, a1, a2, a3, b0, b1, b2, b3 = call(
        slices, "slices", (owners, q, qo, p, po), [piece] * 4 + [block] * 4
    )
    a1, a2, a3 = send(a1, dx=1), send(a2, dx=2), send(a3, dx=3)
    r, t1, t2, t3 = call(
        pack, "pack", (owners, a0, a1, a2, a3, b1, b2, b3), [piece] + [shape((128, 768), BF16)] * 3
    )
    t1, t2, t3 = send(t1, dy=1), send(t2, dy=2), send(t3, dy=3)
    (s,) = call(
        product, "product", (owners, r, b0, t1, t2, t3), [shape((128, 256), F32)],
        scratch=[VMEM((128, 512), BF16)], flops=2 * 128 * 512 * 256,
    )
    s1, s2, s3 = send(s, dx=1), send(s, dx=2), send(s, dx=3)
    (w,) = call(round_sum, "round_sum", (s, s1, s2, s3), [block])
    wo = send(w, dc=1)
    (j,) = call(join, "join", (w, wo), [piece])
    j1, j2, j3 = send(j, dy=1), send(j, dy=2), send(j, dy=3)
    zshape = shape((32, 4480), BF16)
    vm = pl.BlockSpec(memory_space=VMEM)
    own, gn_own, qn_own, z1, z2, z3 = pl.pallas_call(
        dots,
        name="dots",
        in_specs=[vm] * 4 + [pl.BlockSpec(memory_space=pl.ANY)],
        out_specs=[vm] * 6,
        out_shape=[shape((32, 4096), F32), shape((32, 128), F32), shape((32, 128), F32)] + [zshape] * 3,
        scratch_shapes=[
            VMEM((128, 2048), BF16),
            VMEM((128, 2048), BF16),
            VMEM((128, 128), F32),
            VMEM((CHUNKS, ROWS, 2048), BF16),
            pltpu.SemaphoreType.DMA((CHUNKS,)),
        ],
        compiler_params=pltpu.CompilerParams(vmem_limit_bytes=40 << 20),
        cost_estimate=pl.CostEstimate(flops=2 * 128 * 2048 * 4096, bytes_accessed=17 << 20, transcendentals=0),
    )(j, j1, j2, j3, store)
    z1, z2, z3 = send_layer(z1, 1), send_layer(z2, 2), send_layer(z3, 3)
    (out,) = call(finish, "finish", (own, gn_own, qn_own, z1, z2, z3), [shape((32, 4096), F32)])
    return out.T


def solution(mesh):
    return jax.shard_map(
        shards,
        mesh=mesh,
        in_specs=(P("ex", "layer"), P("layer", "ex", None), P("ex", None, None, "layer"), P()),
        out_specs=P("ex", "layer"),
        check_vma=False,
    )
```

time: 258 us -> 87.4 us (0.34)
  waiting for transfers between devices: 198 us -> 41.6 us
  starting transfers between devices: 0.08 us -> 27.2 us
  matrix products: 17.6 us -> 0 us
  Pallas kernels: 0 us -> 15.8 us
  blocking collectives: 15.6 us -> 0 us
  between operations: 14.3 us -> 0.06 us
  other arithmetic: 11.1 us -> 0 us
    psum x2 -> x0, waiting for transfers between devices: 142 us -> none  [the longest x1 106 us: broadcast(): return lax.psum(block, axis)]
    all_gather x1 -> x0, waiting for transfers between devices: 55.3 us -> none  [shards(): lax.all_gather(weight, 'ex', axis=0, tiled=True)]
    ppermute x0 -> x18, waiting for transfers between devices: none -> 41.6 us  [the longest x15 29.7 us: send(): return lax.ppermute(a, 'ex', moved(dx, dy, dc))]
    ppermute x0 -> x18, starting transfers between devices: none -> 27.2 us  [the longest x15 21.5 us: send(): return lax.ppermute(a, 'ex', moved(dx, dy, dc))]
    dot_general x2 -> x0, matrix products: 17.6 us -> none  [the longest x1 12.7 us: shards(): lax.dot_general(store, pre, (((1,), (1,)), ((), ())), preferred_element_t...]
    pallas_call x0 -> x7, Pallas kernels: none -> 15.8 us  [the longest x1 12.5 us: shards(): pl.pallas_call(dots, name='dots', in_specs=[vm] * 4 + [pl.BlockSpec(memor...]
    psum x1 -> x0, blocking collectives: 15.6 us -> none  [shards(): dots_all, gnorm_all, qnorm_all = lax.psum((dots, gnorm, qnorm), 'layer')]
    reduce_sum x1 -> x0, other arithmetic: 7.19 us -> none  [shards(): gnorm = jnp.sum(jnp.square(store.astype(jnp.float32)), axis=1)]
  transfers between devices with their start and end apart: 3 -> 18, of which waited for: 3 -> 14; matrix products, arithmetic and copies ran while one was open for 3% -> 0% of each run, Pallas kernels for 0% -> 0%
where the time goes in v1:
time: 87.4 us; the launch traced here: 87.2 us
  waiting for transfers between devices  41.6 us (48%)
  starting transfers between devices  27.2 us (31%)
  Pallas kernels  15.8 us (18%)
  local copies, waits for them, and re-layouts  2.65 us (3%)
    ppermute x15, waiting for transfers between devices, send(): return lax.ppermute(a, 'ex', moved(dx, dy, dc))  29.7 us
    ppermute x15, starting transfers between devices, send(): return lax.ppermute(a, 'ex', moved(dx, dy, dc))  21.5 us
    pallas_call x1, Pallas kernels, shards(): pl.pallas_call(dots, name='dots', in_specs=[vm] * 4 + [pl.BlockSpec(memor...  12.5 us
    ppermute x3, waiting for transfers between devices, send_layer(): return lax.ppermute(a, 'layer', [(i, (i + d) % 4) for i in range(4)])  11.8 us
    ppermute x3, starting transfers between devices, send_layer(): return lax.ppermute(a, 'layer', [(i, (i + d) % 4) for i in range(4)])  5.66 us
    pallas_call x6, Pallas kernels, call(): pl.pallas_call(body, name=name, in_specs=specs, out_specs=[pl.BlockSpec(m...  3.29 us
    unnamed x6, local copies, waits for them, and re-layouts  2.65 us
  transfers between devices with their start and end apart: 18, of which 14 were waited for; matrix products, arithmetic and copies ran while one was open for 0% of the time, Pallas kernels for 0%

profile of v1, /device:TPU:1, one launch (start us, length us, event | category | flops | bytes accessed | tf_op | source)
XLA Modules:
  0.0 87.2 jit_solution(5800585580049911479)
XLA Ops:
  0.0 1.4 %collective-permute-start = (bf16[128,2048]{1,0:T(8,128)(2,1)}, bf16[128,2048]{1,0:T(8,128)(2,1)S(1)}, u32[]{:S(2)}, u32[]{:S(2)}) collective-permute-start(bf16[128,2048]{1,0:T(8,128)(2,1)} %bitcast.3), channel_id=1, source_target_pairs={{0,4},{4,0},{8,12},{12,8},{16,20},{20,16},{24,28},{28,24},{32,36},... | collective-permute-start | bytes 1572872 | tf_op jit(solution)/shard_map/ppermute | solution.py:208
  1.4 0.0 collective-permute-start.1
  1.4 2.1 %collective-permute-done.1.po = bf16[64,2048]{1,0:T(8,128)(2,1)S(1)} collective-permute-done((bf16[64,2048]{1,0:T(8,128)(2,1)}, bf16[64,2048]{1,0:T(8,128)(2,1)S(1)}, u32[]{:S(2)}, u32[]{:S(2)}) %collective-permute-start.1) | collective-permute-done | bytes 262176 | tf_op jit(solution)/shard_map/ppermute | solution.py:208
  3.5 0.0 collective-permute-done.qo
  3.5 0.0 copy-start
  3.6 1.0 %copy-done = bf16[1,2,64,2048]{3,2,1,0:T(8,128)(2,1)S(1)} copy-done((bf16[1,2,64,2048]{3,2,1,0:T(8,128)(2,1)S(1)}, bf16[1,2,64,2048]{3,2,1,0:T(8,128)(2,1)}, u32[]{:S(2)}) %copy-start) | copy-done | bytes 524312
  4.6 0.0 copy-start.1
  4.6 0.9 %copy-done.1 = bf16[1,64,2048]{2,1,0:T(8,128)(2,1)S(1)} copy-done((bf16[1,64,2048]{2,1,0:T(8,128)(2,1)S(1)}, bf16[1,64,2048]{2,1,0:T(8,128)(2,1)}, u32[]{:S(2)}) %copy-start.1) | copy-done | bytes 262168
  5.5 0.0 copy-start.2
  5.5 0.7 copy-done.2
  6.2 0.7 slices.1
  6.9 1.4 %collective-permute-start.2 = (bf16[128,512]{1,0:T(8,128)(2,1)S(1)}, bf16[128,512]{1,0:T(8,128)(2,1)S(1)}, u32[]{:S(2)}, u32[]{:S(2)}) collective-permute-start(bf16[128,512]{1,0:T(8,128)(2,1)S(1)} %get-tuple-element.24), channel_id=1, source_target_pairs={{0,32},{4,36},{8,40},{12,44},{16,48},{20,52},{24,56},{28,60},{32,6... | collective-permute-start | bytes 393224 | tf_op jit(solution)/shard_map/ppermute | solution.py:208
  8.3 2.5 %collective-permute-start.3 = (bf16[128,512]{1,0:T(8,128)(2,1)S(1)}, bf16[128,512]{1,0:T(8,128)(2,1)S(1)}, u32[]{:S(2)}, u32[]{:S(2)}) collective-permute-start(bf16[128,512]{1,0:T(8,128)(2,1)S(1)} %get-tuple-element.25), channel_id=1, source_target_pairs={{0,64},{4,68},{8,72},{12,76},{16,80},{20,84},{24,88},{28,92},{32,9... | collective-permute-start | bytes 393224 | tf_op jit(solution)/shard_map/ppermute | solution.py:208
  10.7 1.2 %collective-permute-start.4 = (bf16[128,512]{1,0:T(8,128)(2,1)S(1)}, bf16[128,512]{1,0:T(8,128)(2,1)S(1)}, u32[]{:S(2)}, u32[]{:S(2)}) collective-permute-start(bf16[128,512]{1,0:T(8,128)(2,1)S(1)} %get-tuple-element.26), channel_id=1, source_target_pairs={{0,96},{4,100},{8,104},{12,108},{16,112},{20,116},{24,120},{28,124... | collective-permute-start | bytes 393224 | tf_op jit(solution)/shard_map/ppermute | solution.py:208
  11.9 1.0 %collective-permute-done.2.a1 = bf16[128,512]{1,0:T(8,128)(2,1)S(1)} collective-permute-done((bf16[128,512]{1,0:T(8,128)(2,1)S(1)}, bf16[128,512]{1,0:T(8,128)(2,1)S(1)}, u32[]{:S(2)}, u32[]{:S(2)}) %collective-permute-start.2) | collective-permute-done | bytes 131104 | tf_op jit(solution)/shard_map/ppermute | solution.py:208
  12.9 3.9 %collective-permute-done.3.a2 = bf16[128,512]{1,0:T(8,128)(2,1)S(1)} collective-permute-done((bf16[128,512]{1,0:T(8,128)(2,1)S(1)}, bf16[128,512]{1,0:T(8,128)(2,1)S(1)}, u32[]{:S(2)}, u32[]{:S(2)}) %collective-permute-start.3) | collective-permute-done | bytes 131104 | tf_op jit(solution)/shard_map/ppermute | solution.py:208
  16.8 0.0 collective-permute-done.4.a3
  16.8 0.7 pack.1
  17.5 1.4 %collective-permute-start.5 = (bf16[128,768]{1,0:T(8,128)(2,1)S(1)}, bf16[128,768]{1,0:T(8,128)(2,1)S(1)}, u32[]{:S(2)}, u32[]{:S(2)}) collective-permute-start(bf16[128,768]{1,0:T(8,128)(2,1)S(1)} %get-tuple-element.32), channel_id=1, source_target_pairs={{0,8},{4,12},{8,16},{12,20},{16,24},{20,28},{24,0},{28,4},{32,40},... | collective-permute-start | bytes 589832 | tf_op jit(solution)/shard_map/ppermute | solution.py:208
  18.8 2.6 %collective-permute-start.6 = (bf16[128,768]{1,0:T(8,128)(2,1)S(1)}, bf16[128,768]{1,0:T(8,128)(2,1)S(1)}, u32[]{:S(2)}, u32[]{:S(2)}) collective-permute-start(bf16[128,768]{1,0:T(8,128)(2,1)S(1)} %get-tuple-element.33), channel_id=1, source_target_pairs={{0,16},{4,20},{8,24},{12,28},{16,0},{20,4},{24,8},{28,12},{32,48},... | collective-permute-start | bytes 589832 | tf_op jit(solution)/shard_map/ppermute | solution.py:208
  21.4 1.1 %collective-permute-start.7 = (bf16[128,768]{1,0:T(8,128)(2,1)S(1)}, bf16[128,768]{1,0:T(8,128)(2,1)S(1)}, u32[]{:S(2)}, u32[]{:S(2)}) collective-permute-start(bf16[128,768]{1,0:T(8,128)(2,1)S(1)} %get-tuple-element.34), channel_id=1, source_target_pairs={{0,24},{4,28},{8,0},{12,4},{16,8},{20,12},{24,16},{28,20},{32,56},... | collective-permute-start | bytes 589832 | tf_op jit(solution)/shard_map/ppermute | solution.py:208
  22.5 1.6 %collective-permute-done.5.u1 = bf16[128,768]{1,0:T(8,128)(2,1)S(1)} collective-permute-done((bf16[128,768]{1,0:T(8,128)(2,1)S(1)}, bf16[128,768]{1,0:T(8,128)(2,1)S(1)}, u32[]{:S(2)}, u32[]{:S(2)}) %collective-permute-start.5) | collective-permute-done | bytes 196640 | tf_op jit(solution)/shard_map/ppermute | solution.py:208
  24.1 5.3 %collective-permute-done.6.u2 = bf16[128,768]{1,0:T(8,128)(2,1)S(1)} collective-permute-done((bf16[128,768]{1,0:T(8,128)(2,1)S(1)}, bf16[128,768]{1,0:T(8,128)(2,1)S(1)}, u32[]{:S(2)}, u32[]{:S(2)}) %collective-permute-start.6) | collective-permute-done | bytes 196640 | tf_op jit(solution)/shard_map/ppermute | solution.py:208
  29.4 0.0 collective-permute-done.7.u3
  29.4 0.8 product.1.s0
  30.2 2.1 %collective-permute-start.10 = (f32[128,256]{1,0:T(8,128)S(1)}, f32[128,256]{1,0:T(8,128)S(1)}, u32[]{:S(2)}, u32[]{:S(2)}) collective-permute-start(f32[128,256]{1,0:T(8,128)S(1)} %product.1.s0), channel_id=1, source_target_pairs={{0,96},{4,100},{8,104},{12,108},{16,112},{20,116},{24,120},{28,124... | collective-permute-start | bytes 393224 | tf_op jit(solution)/shard_map/ppermute | solution.py:208
  32.4 0.7 collective-permute-start.9
  33.1 0.0 collective-permute-start.8
  33.1 2.7 %collective-permute-done.10.s3 = f32[128,256]{1,0:T(8,128)S(1)} collective-permute-done((f32[128,256]{1,0:T(8,128)S(1)}, f32[128,256]{1,0:T(8,128)S(1)}, u32[]{:S(2)}, u32[]{:S(2)}) %collective-permute-start.10) | collective-permute-done | bytes 131104 | tf_op jit(solution)/shard_map/ppermute | solution.py:208
  35.8 2.0 %collective-permute-done.9.s2 = f32[128,256]{1,0:T(8,128)S(1)} collective-permute-done((f32[128,256]{1,0:T(8,128)S(1)}, f32[128,256]{1,0:T(8,128)S(1)}, u32[]{:S(2)}, u32[]{:S(2)}) %collective-permute-start.9) | collective-permute-done | bytes 131104 | tf_op jit(solution)/shard_map/ppermute | solution.py:208
  37.8 1.3 %collective-permute-done.8.s1 = f32[128,256]{1,0:T(8,128)S(1)} collective-permute-done((f32[128,256]{1,0:T(8,128)S(1)}, f32[128,256]{1,0:T(8,128)S(1)}, u32[]{:S(2)}, u32[]{:S(2)}) %collective-permute-start.8) | collective-permute-done | bytes 131104 | tf_op jit(solution)/shard_map/ppermute | solution.py:208
  39.1 3.6 %collective-permute-start.11 = (bf16[128,256]{1,0:T(8,128)(2,1)S(1)}, bf16[128,256]{1,0:T(8,128)(2,1)S(1)}, u32[]{:S(2)}, u32[]{:S(2)}) collective-permute-start(bf16[128,256]{1,0:T(8,128)(2,1)S(1)} %round_sum.1.w), channel_id=1, source_target_pairs={{0,4},{4,0},{8,12},{12,8},{16,20},{20,16},{24,28},{28,24},{32,36},... | collective-permute-start | bytes 196616 | tf_op jit(solution)/shard_map/ppermute | solution.py:208
  42.7 0.9 %collective-permute-done.11.wo = bf16[128,256]{1,0:T(8,128)(2,1)S(1)} collective-permute-done((bf16[128,256]{1,0:T(8,128)(2,1)S(1)}, bf16[128,256]{1,0:T(8,128)(2,1)S(1)}, u32[]{:S(2)}, u32[]{:S(2)}) %collective-permute-start.11) | collective-permute-done | bytes 65568 | tf_op jit(solution)/shard_map/ppermute | solution.py:208
  43.7 2.8 %collective-permute-start.14 = (bf16[128,512]{1,0:T(8,128)(2,1)S(1)}, bf16[128,512]{1,0:T(8,128)(2,1)S(1)}, u32[]{:S(2)}, u32[]{:S(2)}) collective-permute-start(bf16[128,512]{1,0:T(8,128)(2,1)S(1)} %join.1.j0), channel_id=1, source_target_pairs={{0,24},{4,28},{8,0},{12,4},{16,8},{20,12},{24,16},{28,20},{32,56},... | collective-permute-start | bytes 393224 | tf_op jit(solution)/shard_map/ppermute | solution.py:208
  46.4 0.8 collective-permute-start.13
  47.3 0.0 collective-permute-start.12
  47.3 2.0 %collective-permute-done.14.j3 = bf16[128,512]{1,0:T(8,128)(2,1)S(1)} collective-permute-done((bf16[128,512]{1,0:T(8,128)(2,1)S(1)}, bf16[128,512]{1,0:T(8,128)(2,1)S(1)}, u32[]{:S(2)}, u32[]{:S(2)}) %collective-permute-start.14) | collective-permute-done | bytes 131104 | tf_op jit(solution)/shard_map/ppermute | solution.py:208
  49.3 3.1 %collective-permute-done.13.j2 = bf16[128,512]{1,0:T(8,128)(2,1)S(1)} collective-permute-done((bf16[128,512]{1,0:T(8,128)(2,1)S(1)}, bf16[128,512]{1,0:T(8,128)(2,1)S(1)}, u32[]{:S(2)}, u32[]{:S(2)}) %collective-permute-start.13) | collective-permute-done | bytes 131104 | tf_op jit(solution)/shard_map/ppermute | solution.py:208
  52.4 3.8 %collective-permute-done.12.j1 = bf16[128,512]{1,0:T(8,128)(2,1)S(1)} collective-permute-done((bf16[128,512]{1,0:T(8,128)(2,1)S(1)}, bf16[128,512]{1,0:T(8,128)(2,1)S(1)}, u32[]{:S(2)}, u32[]{:S(2)}) %collective-permute-start.12) | collective-permute-done | bytes 131104 | tf_op jit(solution)/shard_map/ppermute | solution.py:208
  56.2 12.5 %dots.1 = (f32[32,4096]{1,0:T(8,128)S(1)}, f32[32,128]{1,0:T(8,128)S(1)}, f32[32,128]{1,0:T(8,128)S(1)}, bf16[32,4480]{1,0:T(8,128)(2,1)S(1)}, bf16[32,4480]{1,0...) custom-call(bf16[128,512]{1,0:T(8,128)(2,1)S(1)} %join.1.j0, bf16[128,512]{1,0:T(8,128)(2,1)S(1)} %collective-permute-done.12.j1, ...), custom_call_target="tpu_custom_call" | custom-call | flops 2147483648 | bytes 17825792 | tf_op jit(solution)/shard_map/dots/pallas_call | solution.py:241
  68.7 1.6 %collective-permute-start.15 = (bf16[32,4480]{1,0:T(8,128)(2,1)S(1)}, bf16[32,4480]{1,0:T(8,128)(2,1)S(1)}, u32[]{:S(2)}, u32[]{:S(2)}) collective-permute-start(bf16[32,4480]{1,0:T(8,128)(2,1)S(1)} %get-tuple-element.38), channel_id=1, source_target_pairs={{0,1},{1,2},{2,3},{3,0},{4,5},{5,6},{6,7},{7,4},{8,9},{9,10},{10,1... | collective-permute-start | bytes 860168 | tf_op jit(solution)/shard_map/ppermute | solution.py:212
  70.3 3.3 %collective-permute-start.16 = (bf16[32,4480]{1,0:T(8,128)(2,1)S(1)}, bf16[32,4480]{1,0:T(8,128)(2,1)S(1)}, u32[]{:S(2)}, u32[]{:S(2)}) collective-permute-start(bf16[32,4480]{1,0:T(8,128)(2,1)S(1)} %get-tuple-element.39), channel_id=1, source_target_pairs={{0,2},{1,3},{2,0},{3,1},{4,6},{5,7},{6,4},{7,5},{8,10},{9,11},{10,... | collective-permute-start | bytes 860168 | tf_op jit(solution)/shard_map/ppermute | solution.py:212
  73.6 0.7 collective-permute-start.17
  74.3 4.8 %collective-permute-done.15.z1 = bf16[32,4480]{1,0:T(8,128)(2,1)S(1)} collective-permute-done((bf16[32,4480]{1,0:T(8,128)(2,1)S(1)}, bf16[32,4480]{1,0:T(8,128)(2,1)S(1)}, u32[]{:S(2)}, u32[]{:S(2)}) %collective-permute-start.15) | collective-permute-done | bytes 286752 | tf_op jit(solution)/shard_map/ppermute | solution.py:212
  79.2 7.0 %collective-permute-done.16.z2 = bf16[32,4480]{1,0:T(8,128)(2,1)S(1)} collective-permute-done((bf16[32,4480]{1,0:T(8,128)(2,1)S(1)}, bf16[32,4480]{1,0:T(8,128)(2,1)S(1)}, u32[]{:S(2)}, u32[]{:S(2)}) %collective-permute-start.16) | collective-permute-done | bytes 286752 | tf_op jit(solution)/shard_map/ppermute | solution.py:212
  86.2 0.0 collective-permute-done.17.z3
  86.2 1.0 %finish.1 = f32[32,4096]{1,0:T(8,128)} custom-call(f32[32,4096]{1,0:T(8,128)S(1)} %get-tuple-element.35.own, f32[32,128]{1,0:T(8,128)S(1)} %get-tuple-element.36.gn_own, f32[32,128]{1,0:T(8,128)S(1)} %get-tuple-element.37.qn_own, bf16[32,4480]{1,0:T(8,128)(2,1)S(1)} %collective-permute-done.15.z1, bf16[32,4480]{1,0:T(8,128)(2,1)S(1)} %collective-permute-done.16.z2, ...), custom_call_target="tpu_custom_call" | custom-call | bytes 1048576 | tf_op jit(solution)/shard_map/finish/pallas_call | solution.py:43
  (2 shorter events, 0.1 us)
Async XLA Ops:
  0.0 3.5 %collective-permute-start = (bf16[128,2048]{1,0:T(8,128)(2,1)}, bf16[128,2048]{1,0:T(8,128)(2,1)S(1)}, u32[]{:S(2)}, u32[]{:S(2)}) collective-permute-start(bf16[128,2048]{1,0:T(8,128)(2,1)} %bitcast.3), channel_id=1, source_target_pairs={{0,4},{4,0},{8,12},{12,8},{16,20},{20,16},{24,28},{28,24},{32,36},... | collective-permute-start | bytes 1572872 | tf_op jit(solution)/shard_map/ppermute | solution.py:208
  1.4 2.1 %collective-permute-start.1 = (bf16[64,2048]{1,0:T(8,128)(2,1)}, bf16[64,2048]{1,0:T(8,128)(2,1)S(1)}, u32[]{:S(2)}, u32[]{:S(2)}) collective-permute-start(bf16[64,2048]{1,0:T(8,128)(2,1)} %bitcast.5), channel_id=1, source_target_pairs={{0,4},{4,0},{8,12},{12,8},{16,20},{20,16},{24,28},{28,24},{32,36},... | collective-permute-start | bytes 786440 | tf_op jit(solution)/shard_map/ppermute | solution.py:208
  3.5 1.0 %copy-start = (bf16[1,2,64,2048]{3,2,1,0:T(8,128)(2,1)S(1)}, bf16[1,2,64,2048]{3,2,1,0:T(8,128)(2,1)}, u32[]{:S(2)}) copy-start(bf16[1,2,64,2048]{3,2,1,0:T(8,128)(2,1)} %param.6) | copy-start | bytes 1572868
  4.6 0.9 %copy-start.1 = (bf16[1,64,2048]{2,1,0:T(8,128)(2,1)S(1)}, bf16[1,64,2048]{2,1,0:T(8,128)(2,1)}, u32[]{:S(2)}) copy-start(bf16[1,64,2048]{2,1,0:T(8,128)(2,1)} %param.5) | copy-start | bytes 786436
  5.5 0.7 copy-start.2
  6.9 6.0 %collective-permute-start.2 = (bf16[128,512]{1,0:T(8,128)(2,1)S(1)}, bf16[128,512]{1,0:T(8,128)(2,1)S(1)}, u32[]{:S(2)}, u32[]{:S(2)}) collective-permute-start(bf16[128,512]{1,0:T(8,128)(2,1)S(1)} %get-tuple-element.24), channel_id=1, source_target_pairs={{0,32},{4,36},{8,40},{12,44},{16,48},{20,52},{24,56},{28,60},{32,6... | collective-permute-start | bytes 393224 | tf_op jit(solution)/shard_map/ppermute | solution.py:208
  8.3 8.5 %collective-permute-start.3 = (bf16[128,512]{1,0:T(8,128)(2,1)S(1)}, bf16[128,512]{1,0:T(8,128)(2,1)S(1)}, u32[]{:S(2)}, u32[]{:S(2)}) collective-permute-start(bf16[128,512]{1,0:T(8,128)(2,1)S(1)} %get-tuple-element.25), channel_id=1, source_target_pairs={{0,64},{4,68},{8,72},{12,76},{16,80},{20,84},{24,88},{28,92},{32,9... | collective-permute-start | bytes 393224 | tf_op jit(solution)/shard_map/ppermute | solution.py:208
  10.7 6.1 %collective-permute-start.4 = (bf16[128,512]{1,0:T(8,128)(2,1)S(1)}, bf16[128,512]{1,0:T(8,128)(2,1)S(1)}, u32[]{:S(2)}, u32[]{:S(2)}) collective-permute-start(bf16[128,512]{1,0:T(8,128)(2,1)S(1)} %get-tuple-element.26), channel_id=1, source_target_pairs={{0,96},{4,100},{8,104},{12,108},{16,112},{20,116},{24,120},{28,124... | collective-permute-start | bytes 393224 | tf_op jit(solution)/shard_map/ppermute | solution.py:208
  17.5 6.6 %collective-permute-start.5 = (bf16[128,768]{1,0:T(8,128)(2,1)S(1)}, bf16[128,768]{1,0:T(8,128)(2,1)S(1)}, u32[]{:S(2)}, u32[]{:S(2)}) collective-permute-start(bf16[128,768]{1,0:T(8,128)(2,1)S(1)} %get-tuple-element.32), channel_id=1, source_target_pairs={{0,8},{4,12},{8,16},{12,20},{16,24},{20,28},{24,0},{28,4},{32,40},... | collective-permute-start | bytes 589832 | tf_op jit(solution)/shard_map/ppermute | solution.py:208
  18.8 10.6 %collective-permute-start.6 = (bf16[128,768]{1,0:T(8,128)(2,1)S(1)}, bf16[128,768]{1,0:T(8,128)(2,1)S(1)}, u32[]{:S(2)}, u32[]{:S(2)}) collective-permute-start(bf16[128,768]{1,0:T(8,128)(2,1)S(1)} %get-tuple-element.33), channel_id=1, source_target_pairs={{0,16},{4,20},{8,24},{12,28},{16,0},{20,4},{24,8},{28,12},{32,48},... | collective-permute-start | bytes 589832 | tf_op jit(solution)/shard_map/ppermute | solution.py:208
  21.4 8.0 %collective-permute-start.7 = (bf16[128,768]{1,0:T(8,128)(2,1)S(1)}, bf16[128,768]{1,0:T(8,128)(2,1)S(1)}, u32[]{:S(2)}, u32[]{:S(2)}) collective-permute-start(bf16[128,768]{1,0:T(8,128)(2,1)S(1)} %get-tuple-element.34), channel_id=1, source_target_pairs={{0,24},{4,28},{8,0},{12,4},{16,8},{20,12},{24,16},{28,20},{32,56},... | collective-permute-start | bytes 589832 | tf_op jit(solution)/shard_map/ppermute | solution.py:208
  30.2 5.5 %collective-permute-start.10 = (f32[128,256]{1,0:T(8,128)S(1)}, f32[128,256]{1,0:T(8,128)S(1)}, u32[]{:S(2)}, u32[]{:S(2)}) collective-permute-start(f32[128,256]{1,0:T(8,128)S(1)} %product.1.s0), channel_id=1, source_target_pairs={{0,96},{4,100},{8,104},{12,108},{16,112},{20,116},{24,120},{28,124... | collective-permute-start | bytes 393224 | tf_op jit(solution)/shard_map/ppermute | solution.py:208
  32.4 5.4 %collective-permute-start.9 = (f32[128,256]{1,0:T(8,128)S(1)}, f32[128,256]{1,0:T(8,128)S(1)}, u32[]{:S(2)}, u32[]{:S(2)}) collective-permute-start(f32[128,256]{1,0:T(8,128)S(1)} %product.1.s0), channel_id=1, source_target_pairs={{0,64},{4,68},{8,72},{12,76},{16,80},{20,84},{24,88},{28,92},{32,9... | collective-permute-start | bytes 393224 | tf_op jit(solution)/shard_map/ppermute | solution.py:208
  33.1 6.0 %collective-permute-start.8 = (f32[128,256]{1,0:T(8,128)S(1)}, f32[128,256]{1,0:T(8,128)S(1)}, u32[]{:S(2)}, u32[]{:S(2)}) collective-permute-start(f32[128,256]{1,0:T(8,128)S(1)} %product.1.s0), channel_id=1, source_target_pairs={{0,32},{4,36},{8,40},{12,44},{16,48},{20,52},{24,56},{28,60},{32,6... | collective-permute-start | bytes 393224 | tf_op jit(solution)/shard_map/ppermute | solution.py:208
  39.1 4.5 %collective-permute-start.11 = (bf16[128,256]{1,0:T(8,128)(2,1)S(1)}, bf16[128,256]{1,0:T(8,128)(2,1)S(1)}, u32[]{:S(2)}, u32[]{:S(2)}) collective-permute-start(bf16[128,256]{1,0:T(8,128)(2,1)S(1)} %round_sum.1.w), channel_id=1, source_target_pairs={{0,4},{4,0},{8,12},{12,8},{16,20},{20,16},{24,28},{28,24},{32,36},... | collective-permute-start | bytes 196616 | tf_op jit(solution)/shard_map/ppermute | solution.py:208
  43.7 5.7 %collective-permute-start.14 = (bf16[128,512]{1,0:T(8,128)(2,1)S(1)}, bf16[128,512]{1,0:T(8,128)(2,1)S(1)}, u32[]{:S(2)}, u32[]{:S(2)}) collective-permute-start(bf16[128,512]{1,0:T(8,128)(2,1)S(1)} %join.1.j0), channel_id=1, source_target_pairs={{0,24},{4,28},{8,0},{12,4},{16,8},{20,12},{24,16},{28,20},{32,56},... | collective-permute-start | bytes 393224 | tf_op jit(solution)/shard_map/ppermute | solution.py:208
  46.4 5.9 %collective-permute-start.13 = (bf16[128,512]{1,0:T(8,128)(2,1)S(1)}, bf16[128,512]{1,0:T(8,128)(2,1)S(1)}, u32[]{:S(2)}, u32[]{:S(2)}) collective-permute-start(bf16[128,512]{1,0:T(8,128)(2,1)S(1)} %join.1.j0), channel_id=1, source_target_pairs={{0,16},{4,20},{8,24},{12,28},{16,0},{20,4},{24,8},{28,12},{32,48},... | collective-permute-start | bytes 393224 | tf_op jit(solution)/shard_map/ppermute | solution.py:208
  47.3 8.9 %collective-permute-start.12 = (bf16[128,512]{1,0:T(8,128)(2,1)S(1)}, bf16[128,512]{1,0:T(8,128)(2,1)S(1)}, u32[]{:S(2)}, u32[]{:S(2)}) collective-permute-start(bf16[128,512]{1,0:T(8,128)(2,1)S(1)} %join.1.j0), channel_id=1, source_target_pairs={{0,8},{4,12},{8,16},{12,20},{16,24},{20,28},{24,0},{28,4},{32,40},... | collective-permute-start | bytes 393224 | tf_op jit(solution)/shard_map/ppermute | solution.py:208
  68.7 10.5 %collective-permute-start.15 = (bf16[32,4480]{1,0:T(8,128)(2,1)S(1)}, bf16[32,4480]{1,0:T(8,128)(2,1)S(1)}, u32[]{:S(2)}, u32[]{:S(2)}) collective-permute-start(bf16[32,4480]{1,0:T(8,128)(2,1)S(1)} %get-tuple-element.38), channel_id=1, source_target_pairs={{0,1},{1,2},{2,3},{3,0},{4,5},{5,6},{6,7},{7,4},{8,9},{9,10},{10,1... | collective-permute-start | bytes 860168 | tf_op jit(solution)/shard_map/ppermute | solution.py:212
  70.3 15.9 %collective-permute-start.16 = (bf16[32,4480]{1,0:T(8,128)(2,1)S(1)}, bf16[32,4480]{1,0:T(8,128)(2,1)S(1)}, u32[]{:S(2)}, u32[]{:S(2)}) collective-permute-start(bf16[32,4480]{1,0:T(8,128)(2,1)S(1)} %get-tuple-element.39), channel_id=1, source_target_pairs={{0,2},{1,3},{2,0},{3,1},{4,6},{5,7},{6,4},{7,5},{8,10},{9,11},{10,... | collective-permute-start | bytes 860168 | tf_op jit(solution)/shard_map/ppermute | solution.py:212
  73.6 12.6 %collective-permute-start.17 = (bf16[32,4480]{1,0:T(8,128)(2,1)S(1)}, bf16[32,4480]{1,0:T(8,128)(2,1)S(1)}, u32[]{:S(2)}, u32[]{:S(2)}) collective-permute-start(bf16[32,4480]{1,0:T(8,128)(2,1)S(1)} %get-tuple-element.40), channel_id=1, source_target_pairs={{0,3},{1,0},{2,1},{3,2},{4,7},{5,4},{6,5},{7,6},{8,11},{9,8},{10,9... | collective-permute-start | bytes 860168 | tf_op jit(solution)/shard_map/ppermute | solution.py:212

commit v2 on v0

v2 whole, which is shorter than its diff:
```python
import math

import jax
import jax.numpy as jnp
from jax import lax
from jax.experimental import pallas as pl
from jax.experimental.pallas import tpu as pltpu
from jax.sharding import PartitionSpec as P

BF16, F32 = jnp.bfloat16, jnp.float32
NT = (((1,), (1,)), ((), ()))
VMEM, HBM = pltpu.VMEM, pltpu.HBM
PART = 1024
PARTS = 4


def shape(dims, dtype=BF16):
    return jax.ShapeDtypeStruct(dims, dtype)


def place():
    e = lax.axis_index("ex")
    return e // 8, (e // 2) % 4, e % 2


def at(start, size):
    return pl.ds(pl.multiple_of(start, size), size)


def call(body, name, ins, outs, spaces=None, scratch=(), limit=8 << 20, flops=0, moved=1 << 20, alias=None):
    spaces = spaces or {}
    ins = [pltpu.with_memory_space_constraint(a, HBM) if spaces.get(i) is HBM else a for i, a in enumerate(ins)]
    return pl.pallas_call(
        body,
        name=name,
        in_specs=[pl.BlockSpec(memory_space=spaces.get(i, VMEM)) for i in range(len(ins))],
        out_specs=[pl.BlockSpec(memory_space=VMEM)] * len(outs),
        out_shape=outs,
        scratch_shapes=scratch,
        input_output_aliases=alias or {},
        compiler_params=pltpu.CompilerParams(vmem_limit_bytes=limit),
        cost_estimate=pl.CostEstimate(flops=flops, bytes_accessed=moved, transcendentals=0),
    )(*ins)


def fetch(owners, q, p, w, qc, pv, sems):
    x, y, c = place()
    one = pltpu.make_async_copy(q.at[at(c * 64, 64), :], qc, sems.at[0])
    two = pltpu.make_async_copy(p, pv, sems.at[1])
    one.start()
    two.start()
    o = owners[c]
    xback = lax.rem(x - o // 8 + 4, 4)
    yback = lax.rem(y - (o // 2) % 4 + 4, 4)
    tests = [o % 2 == c, o % 2 != c] + [xback == d for d in range(4)] + [yback == d for d in range(4)]
    for i, test in enumerate(tests):
        w[i, :, :] = jnp.full((16, 128), jnp.where(test, 1.0, 0.0), F32).astype(BF16)
    one.wait()
    two.wait()


def weigh(w, first, refs, columns):
    total = None
    for d, ref in enumerate(refs):
        term = ref(columns) * w[first + d, 0:1, :]
        total = term if total is None else total + term
    return total


def slices(w, qc, qo, pv, po, a0, a1, a2, a3, b0, b1, b2, b3):
    x, y, c = place()
    for d, a in enumerate((a0, a1, a2, a3)):
        for k in range(4):
            columns = at(lax.rem(x + d, 4) * 512 + 128 * k, 128)
            a[:, 128 * k:128 * k + 128] = weigh(
                w, 0, (lambda s: qc[:, s], lambda s: qo[at(c * 64, 64), s]), columns
            )
    for d, b in enumerate((b0, b1, b2, b3)):
        columns = at(c * 1024 + lax.rem(y + d, 4) * 256, 256)
        b[at(c * 64, 64), :] = pv[:, columns]
        b[at(64 - c * 64, 64), :] = po[:, columns]


def pack(w, a0, a1, a2, a3, b1, b2, b3, g0, g1, r, t1, t2, t3):
    for k in range(4):
        columns = slice(128 * k, 128 * k + 128)
        got = weigh(w, 2, [lambda s, a=a: a[:, s] for a in (a0, a1, a2, a3)], columns)
        for t in (r, t1, t2, t3):
            t[:, columns] = got
    for b, t in ((b1, t1), (b2, t2), (b3, t3)):
        t[:, 512:768] = b[0:64, :]
        t[:, 768:1024] = b[64:128, :]


def pick(w, r, u1, u2, u3, g2, g3, rc):
    for k in range(4):
        columns = slice(128 * k, 128 * k + 128)
        rc[:, columns] = weigh(w, 6, [lambda s, u=u: u[:, s] for u in (r, u1, u2, u3)], columns)


def product(rc, ro, b0, u1, u2, u3, s, raw, block):
    _, y, c = place()
    raw[at(c * 64, 64), :] = rc[...]
    raw[at(64 - c * 64, 64), :] = ro[...]
    block[at(y * 128, 128), :] = b0[...]
    for d, u in enumerate((u1, u2, u3)):
        first = lax.rem(y - (d + 1) + 4, 4) * 128
        block[at(first, 64), :] = u[:, 512:768]
        block[at(first + 64, 64), :] = u[:, 768:1024]
    s[...] = jnp.dot(raw[...], block[...], preferred_element_type=F32)


def round_sum(s0, s1, s2, s3, w):
    w[...] = ((s0[...] + s2[...]) + (s1[...] + s3[...])).astype(BF16)


def join(w, wo, j):
    _, _, c = place()
    layer = lax.axis_index("layer")
    for d in range(4):
        rows = at(lax.rem(layer + d, 4) * 32, 32)
        j[32 * d:32 * d + 32, at(c * 256, 256)] = w[rows, :] * jnp.asarray(0.5, BF16)
        j[32 * d:32 * d + 32, at(256 - c * 256, 256)] = wo[rows, :] * jnp.asarray(0.5, BF16)


SUB = 256


def load(part, store, after, sv, gn, sems):
    copies = []
    for i in range(PART // SUB):
        rows = pl.ds(SUB * i, SUB)
        copies.append(pltpu.make_async_copy(store.at[pl.ds(PART * part + SUB * i, SUB), :], sv.at[rows, :], sems.at[i]))
        copies[-1].start()
    for i in range(PART // SUB):
        copies[i].wait()
        squares = None
        for k in range(16):
            v = sv[SUB * i:SUB * i + SUB, 128 * k:128 * k + 128].astype(F32)
            squares = v * v if squares is None else squares + v * v
        line = jnp.sum(squares.T, axis=0, keepdims=True) * 0.5
        for k in range(SUB // 128):
            row = SUB // 128 * i + k
            gn[row:row + 1, :] = line[:, 128 * k:128 * k + 128]


def term(d, j, sv):
    _, y, _ = place()
    origin = lax.rem(y - d + 4, 4) * 256
    return lax.dot_general(sv[:, at(origin, 256)], j[:, 0:256], NT, preferred_element_type=F32) + lax.dot_general(
        sv[:, at(origin + 1024, 256)], j[:, 256:512], NT, preferred_element_type=F32
    )


def dots_first(j, v0, v1, v2, v3, acc):
    for i, v in enumerate((v0, v1, v2, v3)):
        acc[PART * i:PART * i + PART, :] = term(0, j, v)


def dots_next(d, j, v0, v1, v2, v3, old, acc):
    for i, v in enumerate((v0, v1, v2, v3)):
        rows = slice(PART * i, PART * i + PART)
        acc[rows, :] = old[rows, :] + term(d, j, v)


def dots_last(d, j, j0, ja, jb, v0, v1, v2, v3, old, g0, g1, g2, g3, own, gn, qn, z1, z2, z3):
    zs = (None, z1, z2, z3)
    for i, v in enumerate((v0, v1, v2, v3)):
        rows = slice(PART * i, PART * i + PART)
        out = (old[rows, :] + term(d, j, v)).T
        own[:, rows] = out[0:32, :]
        for e in range(1, 4):
            zs[e][:, rows] = out[32 * e:32 * e + 32, :].astype(BF16)
    total = None
    for piece in (j, j0, ja, jb):
        for k in range(4):
            v = piece[:, 128 * k:128 * k + 128].astype(F32)
            total = v * v if total is None else total + v * v
    qsum = jnp.broadcast_to(jnp.sum(total, axis=1, keepdims=True), (128, 128))
    qn[...] = qsum[0:32, :]
    lane = lax.broadcasted_iota(jnp.int32, (32, 128), 1)
    for e in range(1, 4):
        part = qsum[32 * e:32 * e + 32, :]
        hi = part.astype(BF16).astype(F32)
        zs[e][:, 4352:4480] = jnp.where(lane < 64, hi, part - hi).astype(BF16)
    for i, g in enumerate((g0, g1, g2, g3)):
        gn[8 * i:8 * i + 8, :] = g[...]
    g = gn[...]
    hi = g.astype(BF16)
    lo = (g - hi.astype(F32)).astype(BF16)
    for e in range(1, 4):
        zs[e][:, 4096:4224] = hi
        zs[e][:, 4224:4352] = lo


def finish(own, gn, qn, z1, z2, z3, out):
    g = gn[...]
    q = qn[:, 0:1]
    for z in (z1, z2, z3):
        g = g + (z[:, 4096:4224].astype(F32) + z[:, 4224:4352].astype(F32))
        q = q + (z[:, 4352:4353].astype(F32) + z[:, 4416:4417].astype(F32))
    g = lax.rsqrt(g * 2.0 + 1e-06)
    q = lax.rsqrt(q * 4.0 + 1e-06) * (2.0 * math.sqrt(8192.0))
    for i in range(32):
        columns = slice(128 * i, 128 * i + 128)
        t = (own[:, columns] + z2[:, columns].astype(F32)) + (
            z1[:, columns].astype(F32) + z3[:, columns].astype(F32)
        )
        out[:, columns] = t * g[i:i + 1, :] * q


def moved(dx, dy, dc):
    pairs = []
    for x in range(4):
        for y in range(4):
            for c in range(2):
                to = ((x + dx) % 4 * 4 + (y + dy) % 4) * 2 + (c + dc) % 2
                pairs.append(((x * 4 + y) * 2 + c, to))
    return pairs


def send(a, dx=0, dy=0, dc=0):
    return lax.ppermute(a, "ex", moved(dx, dy, dc))


def send_layer(a, d):
    return lax.ppermute(a, "layer", [(i, (i + d) % 4) for i in range(4)])


def load_part(part, store, after):
    return call(
        lambda *refs: load(part, *refs), "load%d" % part, (store, after),
        [shape((PART, 2048)), shape((8, 128), F32)], spaces={0: HBM, 1: pl.ANY},
        scratch=[pltpu.SemaphoreType.DMA((PART // SUB,))], flops=3 * PART * 2048, moved=8 << 20,
    )


def shards(store, precond, query_slots, owners):
    q = query_slots.reshape(128, 2048)
    p = precond.reshape(64, 2048)
    qo = send(q, dc=1)
    po = send(p, dc=1)
    piece = shape((64, 512))
    block = shape((128, 256))
    w, qc, pv = call(
        fetch, "fetch", (owners, q, p), [shape((10, 16, 128)), shape((64, 2048)), shape((64, 2048))],
        spaces={0: pltpu.SMEM, 1: HBM, 2: HBM}, scratch=[pltpu.SemaphoreType.DMA((2,))],
    )
    a0, a1, a2, a3, b0, b1, b2, b3 = call(slices, "slices", (w, qc, qo, pv, po), [piece] * 4 + [block] * 4)
    v0, g0 = load_part(0, store, a0)
    v1, g1 = load_part(1, store, a0)
    a1, a2, a3 = send(a1, dx=1), send(a2, dx=2), send(a3, dx=3)
    r, t1, t2, t3 = call(
        pack, "pack", (w, a0, a1, a2, a3, b1, b2, b3, g0, g1), [piece] + [shape((64, 1024))] * 3,
        spaces={8: pl.ANY, 9: pl.ANY},
    )
    v2, g2 = load_part(2, store, r)
    v3, g3 = load_part(3, store, r)
    t1, t2, t3 = send(t1, dy=1), send(t2, dy=2), send(t3, dy=3)
    (rc,) = call(pick, "pick", (w, r, t1, t2, t3, g2, g3), [piece], spaces={5: pl.ANY, 6: pl.ANY})
    ro = send(rc, dc=1)
    (s,) = call(
        product, "product", (rc, ro, b0, t1, t2, t3), [shape((128, 256), F32)],
        scratch=[VMEM((128, 512), BF16), VMEM((512, 256), BF16)], flops=2 * 128 * 512 * 256,
    )
    s1, s2, s3 = send(s, dx=1), send(s, dx=2), send(s, dx=3)
    (h,) = call(round_sum, "round_sum", (s, s1, s2, s3), [block])
    ho = send(h, dc=1)
    (j,) = call(join, "join", (h, ho), [shape((128, 512))])
    j1, j2, j3 = send(j, dy=1), send(j, dy=2), send(j, dy=3)
    accs = [shape((4096, 128), F32)]
    work = 2 * 128 * 512 * 4096
    (acc,) = call(dots_first, "dots_first", (j, v0, v1, v2, v3), accs, flops=work)
    for d, piece in ((1, j1), (3, j3)):
        (acc,) = call(
            lambda *refs, d=d: dots_next(d, *refs), "dots_next%d" % d, (piece, v0, v1, v2, v3, acc), accs,
            flops=work, alias={5: 0},
        )
    own, gn, qn, z1, z2, z3 = call(
        lambda *refs: dots_last(2, *refs), "dots_last", (j2, j, j1, j3, v0, v1, v2, v3, acc, g0, g1, g2, g3),
        [shape((32, 4096), F32), shape((32, 128), F32), shape((32, 128), F32)] + [shape((32, 4480))] * 3, flops=work,
    )
    z1, z2, z3 = send_layer(z1, 1), send_layer(z2, 2), send_layer(z3, 3)
    (out,) = call(finish, "finish", (own, gn, qn, z1, z2, z3), [shape((32, 4096), F32)])
    return out.T


def solution(mesh):
    return jax.shard_map(
        shards,
        mesh=mesh,
        in_specs=(P("ex", "layer"), P("layer", "ex", None), P("ex", None, None, "layer"), P()),
        out_specs=P("ex", "layer"),
        check_vma=False,
    )
```

time: 258 us -> 69.2 us (0.27)
  the two profiles are of different devices: /device:TPU:1 before, /device:TPU:24 now
where the time goes in v2:
time: 69.2 us; the launch traced here: 69 us
  waiting for transfers between devices  26.5 us (38%)
  starting transfers between devices  23.1 us (33%)
  Pallas kernels  18.6 us (27%)
    pallas_call x16, Pallas kernels, call(): pl.pallas_call(body, name=name, in_specs=[pl.BlockSpec(memory_space=space...  18.6 us
    ppermute x16, starting transfers between devices, send(): return lax.ppermute(a, 'ex', moved(dx, dy, dc))  16.5 us
    ppermute x16, waiting for transfers between devices, send(): return lax.ppermute(a, 'ex', moved(dx, dy, dc))  15.4 us
    ppermute x3, waiting for transfers between devices, send_layer(): return lax.ppermute(a, 'layer', [(i, (i + d) % 4) for i in range(4)])  11.1 us
    ppermute x3, starting transfers between devices, send_layer(): return lax.ppermute(a, 'layer', [(i, (i + d) % 4) for i in range(4)])  6.56 us
  transfers between devices with their start and end apart: 19, of which 10 were waited for; matrix products, arithmetic and copies ran while one was open for 0% of the time, Pallas kernels for 23%

profile of v2, /device:TPU:24, one launch (start us, length us, event | category | flops | bytes accessed | tf_op | source)
XLA Modules:
  0.0 69.0 jit_solution(14790236463698582562)
XLA Ops:
  0.0 0.0 collective-permute-start
  0.0 0.5 collective-permute-start.1
  0.5 0.0 copy-start
  0.5 0.7 copy-done
  1.2 1.6 %fetch.1 = (bf16[10,16,128]{2,1,0:T(8,128)(2,1)S(1)}, bf16[64,2048]{1,0:T(8,128)(2,1)S(1)}, bf16[64,2048]{1,0:T(8,128)(2,1)S(1)}) custom-call(s32[2]{0:T(128)S(1)} %copy-done, bf16[128,2048]{1,0:T(8,128)(2,1)} %bitcast.4, bf16[64,2048]{1,0:T(8,128)(2,1)} %bitcast.6), custom_call_target="tpu_custom_call" | custom-call | bytes 1048576 | tf_op jit(solution)/shard_map/fetch/pallas_call | solution.py:33
  2.8 0.0 collective-permute-done.1.po
  2.8 0.0 collective-permute-done.qo
  2.8 0.2 slices.1
  3.0 1.6 %collective-permute-start.2 = (bf16[64,512]{1,0:T(8,128)(2,1)S(1)}, bf16[64,512]{1,0:T(8,128)(2,1)S(1)}, u32[]{:S(2)}, u32[]{:S(2)}) collective-permute-start(bf16[64,512]{1,0:T(8,128)(2,1)S(1)} %get-tuple-element.38), channel_id=1, source_target_pairs={{0,32},{4,36},{8,40},{12,44},{16,48},{20,52},{24,56},{28,60},{32,6... | collective-permute-start | bytes 196616 | tf_op jit(solution)/shard_map/ppermute | solution.py:223
  4.6 2.7 %collective-permute-start.3 = (bf16[64,512]{1,0:T(8,128)(2,1)S(1)}, bf16[64,512]{1,0:T(8,128)(2,1)S(1)}, u32[]{:S(2)}, u32[]{:S(2)}) collective-permute-start(bf16[64,512]{1,0:T(8,128)(2,1)S(1)} %get-tuple-element.39), channel_id=1, source_target_pairs={{0,64},{4,68},{8,72},{12,76},{16,80},{20,84},{24,88},{28,92},{32,9... | collective-permute-start | bytes 196616 | tf_op jit(solution)/shard_map/ppermute | solution.py:223
  7.3 1.4 %collective-permute-start.4 = (bf16[64,512]{1,0:T(8,128)(2,1)S(1)}, bf16[64,512]{1,0:T(8,128)(2,1)S(1)}, u32[]{:S(2)}, u32[]{:S(2)}) collective-permute-start(bf16[64,512]{1,0:T(8,128)(2,1)S(1)} %get-tuple-element.40), channel_id=1, source_target_pairs={{0,96},{4,100},{8,104},{12,108},{16,112},{20,116},{24,120},{28,124... | collective-permute-start | bytes 196616 | tf_op jit(solution)/shard_map/ppermute | solution.py:223
  8.7 2.5 %load0.1 = (bf16[1024,2048]{1,0:T(8,128)(2,1)S(1)}, f32[8,128]{1,0:T(8,128)S(1)}) custom-call(bf16[4096,2048]{1,0:T(8,128)(2,1)} %refs_0_.7, bf16[64,512]{1,0:T(8,128)(2,1)S(1)} %get-tuple-element.37.refs_1_.a0), custom_call_target="tpu_custom_call" | custom-call | flops 6291456 | bytes 8388608 | tf_op jit(solution)/shard_map/load0/pallas_call | solution.py:33
  11.2 2.5 %load1.1 = (bf16[1024,2048]{1,0:T(8,128)(2,1)S(1)}, f32[8,128]{1,0:T(8,128)S(1)}) custom-call(bf16[4096,2048]{1,0:T(8,128)(2,1)} %refs_0_.7, bf16[64,512]{1,0:T(8,128)(2,1)S(1)} %get-tuple-element.37.refs_1_.a0), custom_call_target="tpu_custom_call" | custom-call | flops 6291456 | bytes 8388608 | tf_op jit(solution)/shard_map/load1/pallas_call | solution.py:33
  13.7 0.0 collective-permute-done.2.a1
  13.8 0.0 collective-permute-done.3.a2
  13.8 0.0 collective-permute-done.4.a3
  13.8 0.1 pack.1
  13.9 0.3 collective-permute-start.5
  14.2 2.6 %collective-permute-start.6 = (bf16[64,1024]{1,0:T(8,128)(2,1)S(1)}, bf16[64,1024]{1,0:T(8,128)(2,1)S(1)}, u32[]{:S(2)}, u32[]{:S(2)}) collective-permute-start(bf16[64,1024]{1,0:T(8,128)(2,1)S(1)} %get-tuple-element.48), channel_id=1, source_target_pairs={{0,16},{4,20},{8,24},{12,28},{16,0},{20,4},{24,8},{28,12},{32,48},... | collective-permute-start | bytes 393224 | tf_op jit(solution)/shard_map/ppermute | solution.py:223
  16.7 0.0 collective-permute-start.7
  16.7 2.5 %load2.1 = (bf16[1024,2048]{1,0:T(8,128)(2,1)S(1)}, f32[8,128]{1,0:T(8,128)S(1)}) custom-call(bf16[4096,2048]{1,0:T(8,128)(2,1)} %refs_0_.7, bf16[64,512]{1,0:T(8,128)(2,1)S(1)} %get-tuple-element.46.refs_1_.r), custom_call_target="tpu_custom_call" | custom-call | flops 6291456 | bytes 8388608 | tf_op jit(solution)/shard_map/load2/pallas_call | solution.py:33
  19.2 2.5 %load3.1 = (bf16[1024,2048]{1,0:T(8,128)(2,1)S(1)}, f32[8,128]{1,0:T(8,128)S(1)}) custom-call(bf16[4096,2048]{1,0:T(8,128)(2,1)} %refs_0_.7, bf16[64,512]{1,0:T(8,128)(2,1)S(1)} %get-tuple-element.46.refs_1_.r), custom_call_target="tpu_custom_call" | custom-call | flops 6291456 | bytes 8388608 | tf_op jit(solution)/shard_map/load3/pallas_call | solution.py:33
  21.7 0.0 collective-permute-done.5.u1
  21.7 0.2 collective-permute-done.6.u2
  22.0 1.3 %collective-permute-done.7.u3 = bf16[64,1024]{1,0:T(8,128)(2,1)S(1)} collective-permute-done((bf16[64,1024]{1,0:T(8,128)(2,1)S(1)}, bf16[64,1024]{1,0:T(8,128)(2,1)S(1)}, u32[]{:S(2)}, u32[]{:S(2)}) %collective-permute-start.7) | collective-permute-done | bytes 131104 | tf_op jit(solution)/shard_map/ppermute | solution.py:223
  23.4 0.1 collective-permute-start.8
  23.5 1.2 %collective-permute-done.8.ro = bf16[64,512]{1,0:T(8,128)(2,1)S(1)} collective-permute-done((bf16[64,512]{1,0:T(8,128)(2,1)S(1)}, bf16[64,512]{1,0:T(8,128)(2,1)S(1)}, u32[]{:S(2)}, u32[]{:S(2)}) %collective-permute-start.8) | collective-permute-done | bytes 65568 | tf_op jit(solution)/shard_map/ppermute | solution.py:223
  24.7 0.2 product.1.s0
  25.0 0.6 collective-permute-start.10
  25.5 2.8 %collective-permute-start.11 = (f32[128,256]{1,0:T(8,128)S(1)}, f32[128,256]{1,0:T(8,128)S(1)}, u32[]{:S(2)}, u32[]{:S(2)}) collective-permute-start(f32[128,256]{1,0:T(8,128)S(1)} %product.1.s0), channel_id=1, source_target_pairs={{0,96},{4,100},{8,104},{12,108},{16,112},{20,116},{24,120},{28,124... | collective-permute-start | bytes 393224 | tf_op jit(solution)/shard_map/ppermute | solution.py:223
  28.3 0.0 collective-permute-start.9
  28.3 4.6 %collective-permute-done.10.s2 = f32[128,256]{1,0:T(8,128)S(1)} collective-permute-done((f32[128,256]{1,0:T(8,128)S(1)}, f32[128,256]{1,0:T(8,128)S(1)}, u32[]{:S(2)}, u32[]{:S(2)}) %collective-permute-start.10) | collective-permute-done | bytes 131104 | tf_op jit(solution)/shard_map/ppermute | solution.py:223
  32.9 0.0 collective-permute-done.11.s3
  32.9 2.2 %collective-permute-done.9.s1 = f32[128,256]{1,0:T(8,128)S(1)} collective-permute-done((f32[128,256]{1,0:T(8,128)S(1)}, f32[128,256]{1,0:T(8,128)S(1)}, u32[]{:S(2)}, u32[]{:S(2)}) %collective-permute-start.9) | collective-permute-done | bytes 131104 | tf_op jit(solution)/shard_map/ppermute | solution.py:223
  35.1 0.1 collective-permute-start.12
  35.2 1.2 %collective-permute-done.12.wo = bf16[128,256]{1,0:T(8,128)(2,1)S(1)} collective-permute-done((bf16[128,256]{1,0:T(8,128)(2,1)S(1)}, bf16[128,256]{1,0:T(8,128)(2,1)S(1)}, u32[]{:S(2)}, u32[]{:S(2)}) %collective-permute-start.12) | collective-permute-done | bytes 65568 | tf_op jit(solution)/shard_map/ppermute | solution.py:223
  36.5 1.7 %collective-permute-start.14 = (bf16[128,512]{1,0:T(8,128)(2,1)S(1)}, bf16[128,512]{1,0:T(8,128)(2,1)S(1)}, u32[]{:S(2)}, u32[]{:S(2)}) collective-permute-start(bf16[128,512]{1,0:T(8,128)(2,1)S(1)} %join.1.j.refs_1_), channel_id=1, source_target_pairs={{0,8},{4,12},{8,16},{12,20},{16,24},{20,28},{24,0},{28,4},{32,40},... | collective-permute-start | bytes 393224 | tf_op jit(solution)/shard_map/ppermute | solution.py:223
  38.2 0.4 collective-permute-start.15
  38.6 1.8 %collective-permute-start.13 = (bf16[128,512]{1,0:T(8,128)(2,1)S(1)}, bf16[128,512]{1,0:T(8,128)(2,1)S(1)}, u32[]{:S(2)}, u32[]{:S(2)}) collective-permute-start(bf16[128,512]{1,0:T(8,128)(2,1)S(1)} %join.1.j.refs_1_), channel_id=1, source_target_pairs={{0,16},{4,20},{8,24},{12,28},{16,0},{20,4},{24,8},{28,12},{32,48},... | collective-permute-start | bytes 393224 | tf_op jit(solution)/shard_map/ppermute | solution.py:223
  40.4 1.2 %dots_first.1.refs_5_ = f32[4096,128]{1,0:T(8,128)S(1)} custom-call(bf16[128,512]{1,0:T(8,128)(2,1)S(1)} %join.1.j.refs_1_, bf16[1024,2048]{1,0:T(8,128)(2,1)S(1)} %get-tuple-element.53.v0.refs_1_.refs_4_, bf16[1024,2048]{1,0:T(8,128)(2,1)S(1)} %get-tuple-element.54.v1.refs_2_.refs_5_, bf16[1024,2048]{1,0:T(8,128)(2,1)S(1)} %get-tuple-element.55.v2.refs_3_.refs_6_, ...), custom_call_target="tpu_custom_call" | custom-call | flops 536870912 | bytes 1048576 | tf_op jit(solution)/shard_map/dots_first/pallas_call | solution.py:33
  41.6 0.5 collective-permute-done.14.refs_0_.refs_2_
  42.1 1.4 %dots_next1.1.refs_5_ = f32[4096,128]{1,0:T(8,128)S(1)} custom-call(bf16[128,512]{1,0:T(8,128)(2,1)S(1)} %collective-permute-done.14.refs_0_.refs_2_, bf16[1024,2048]{1,0:T(8,128)(2,1)S(1)} %get-tuple-element.53.v0.refs_1_.refs_4_, bf16[1024,2048]{1,0:T(8,128)(2,1)S(1)} %get-tuple-element.54.v1.refs_2_.refs_5_, ...), custom_call_target="tpu_custom_call", output_to_operand_aliasing={{}: (5, {})} | custom-call | flops 536870912 | bytes 1048576 | tf_op jit(solution)/shard_map/dots_next1/pallas_call | solution.py:33
  43.5 4.0 %collective-permute-done.15.refs_0_.refs_3_ = bf16[128,512]{1,0:T(8,128)(2,1)S(1)} collective-permute-done((bf16[128,512]{1,0:T(8,128)(2,1)S(1)}, bf16[128,512]{1,0:T(8,128)(2,1)S(1)}, u32[]{:S(2)}, u32[]{:S(2)}) %collective-permute-start.15) | collective-permute-done | bytes 131104 | tf_op jit(solution)/shard_map/ppermute | solution.py:223
  47.5 1.4 %dots_next3.1.refs_8_ = f32[4096,128]{1,0:T(8,128)S(1)} custom-call(bf16[128,512]{1,0:T(8,128)(2,1)S(1)} %collective-permute-done.15.refs_0_.refs_3_, bf16[1024,2048]{1,0:T(8,128)(2,1)S(1)} %get-tuple-element.53.v0.refs_1_.refs_4_, bf16[1024,2048]{1,0:T(8,128)(2,1)S(1)} %get-tuple-element.54.v1.refs_2_.refs_5_, ...), custom_call_target="tpu_custom_call", output_to_operand_aliasing={{}: (5, {})} | custom-call | flops 536870912 | bytes 1048576 | tf_op jit(solution)/shard_map/dots_next3/pallas_call | solution.py:33
  48.9 0.0 collective-permute-done.13.refs_0_
  48.9 1.4 %dots_last.1 = (f32[32,4096]{1,0:T(8,128)S(1)}, f32[32,128]{1,0:T(8,128)S(1)}, f32[32,128]{1,0:T(8,128)S(1)}, bf16[32,4480]{1,0:T(8,128)(2,1)S(1)}, bf16[32,4480...) custom-call(bf16[128,512]{1,0:T(8,128)(2,1)S(1)} %collective-permute-done.13.refs_0_, bf16[128,512]{1,0:T(8,128)(2,1)S(1)} %join.1.j.refs_1_, ...), custom_call_target="tpu_custom_call" | custom-call | flops 536870912 | bytes 1048576 | tf_op jit(solution)/shard_map/dots_last/pallas_call | solution.py:33
  50.3 2.0 %collective-permute-start.16 = (bf16[32,4480]{1,0:T(8,128)(2,1)S(1)}, bf16[32,4480]{1,0:T(8,128)(2,1)S(1)}, u32[]{:S(2)}, u32[]{:S(2)}) collective-permute-start(bf16[32,4480]{1,0:T(8,128)(2,1)S(1)} %get-tuple-element.60), channel_id=1, source_target_pairs={{0,1},{1,2},{2,3},{3,0},{4,5},{5,6},{6,7},{7,4},{8,9},{9,10},{10,1... | collective-permute-start | bytes 860168 | tf_op jit(solution)/shard_map/ppermute | solution.py:227
  52.3 3.6 %collective-permute-start.17 = (bf16[32,4480]{1,0:T(8,128)(2,1)S(1)}, bf16[32,4480]{1,0:T(8,128)(2,1)S(1)}, u32[]{:S(2)}, u32[]{:S(2)}) collective-permute-start(bf16[32,4480]{1,0:T(8,128)(2,1)S(1)} %get-tuple-element.61), channel_id=1, source_target_pairs={{0,2},{1,3},{2,0},{3,1},{4,6},{5,7},{6,4},{7,5},{8,10},{9,11},{10,... | collective-permute-start | bytes 860168 | tf_op jit(solution)/shard_map/ppermute | solution.py:227
  55.9 1.0 %collective-permute-start.18 = (bf16[32,4480]{1,0:T(8,128)(2,1)S(1)}, bf16[32,4480]{1,0:T(8,128)(2,1)S(1)}, u32[]{:S(2)}, u32[]{:S(2)}) collective-permute-start(bf16[32,4480]{1,0:T(8,128)(2,1)S(1)} %get-tuple-element.62), channel_id=1, source_target_pairs={{0,3},{1,0},{2,1},{3,2},{4,7},{5,4},{6,5},{7,6},{8,11},{9,8},{10,9... | collective-permute-start | bytes 860168 | tf_op jit(solution)/shard_map/ppermute | solution.py:227
  56.9 4.4 %collective-permute-done.16.z1 = bf16[32,4480]{1,0:T(8,128)(2,1)S(1)} collective-permute-done((bf16[32,4480]{1,0:T(8,128)(2,1)S(1)}, bf16[32,4480]{1,0:T(8,128)(2,1)S(1)}, u32[]{:S(2)}, u32[]{:S(2)}) %collective-permute-start.16) | collective-permute-done | bytes 286752 | tf_op jit(solution)/shard_map/ppermute | solution.py:227
  61.2 6.7 %collective-permute-done.17.z2 = bf16[32,4480]{1,0:T(8,128)(2,1)S(1)} collective-permute-done((bf16[32,4480]{1,0:T(8,128)(2,1)S(1)}, bf16[32,4480]{1,0:T(8,128)(2,1)S(1)}, u32[]{:S(2)}, u32[]{:S(2)}) %collective-permute-start.17) | collective-permute-done | bytes 286752 | tf_op jit(solution)/shard_map/ppermute | solution.py:227
  68.0 0.0 collective-permute-done.18.z3
  68.0 1.0 %finish.1 = f32[32,4096]{1,0:T(8,128)} custom-call(f32[32,4096]{1,0:T(8,128)S(1)} %get-tuple-element.57.own, f32[32,128]{1,0:T(8,128)S(1)} %get-tuple-element.58.gn, f32[32,128]{1,0:T(8,128)S(1)} %get-tuple-element.59.qn, bf16[32,4480]{1,0:T(8,128)(2,1)S(1)} %collective-permute-done.16.z1, bf16[32,4480]{1,0:T(8,128)(2,1)S(1)} %collective-permute-done.17.z2, ...), custom_call_target="tpu_custom_call" | custom-call | bytes 1048576 | tf_op jit(solution)/shard_map/finish/pallas_call | solution.py:33
  (3 shorter events, 0.1 us)
Async XLA Ops:
  0.0 2.8 %collective-permute-start = (bf16[128,2048]{1,0:T(8,128)(2,1)}, bf16[128,2048]{1,0:T(8,128)(2,1)S(1)}, u32[]{:S(2)}, u32[]{:S(2)}) collective-permute-start(bf16[128,2048]{1,0:T(8,128)(2,1)} %bitcast.3), channel_id=1, source_target_pairs={{0,4},{4,0},{8,12},{12,8},{16,20},{20,16},{24,28},{28,24},{32,36},... | collective-permute-start | bytes 1572872 | tf_op jit(solution)/shard_map/ppermute | solution.py:223
  0.0 2.8 %collective-permute-start.1 = (bf16[64,2048]{1,0:T(8,128)(2,1)}, bf16[64,2048]{1,0:T(8,128)(2,1)S(1)}, u32[]{:S(2)}, u32[]{:S(2)}) collective-permute-start(bf16[64,2048]{1,0:T(8,128)(2,1)} %bitcast.5), channel_id=1, source_target_pairs={{0,4},{4,0},{8,12},{12,8},{16,20},{20,16},{24,28},{28,24},{32,36},... | collective-permute-start | bytes 786440 | tf_op jit(solution)/shard_map/ppermute | solution.py:223
  0.5 0.7 copy-start
  3.0 10.7 %collective-permute-start.2 = (bf16[64,512]{1,0:T(8,128)(2,1)S(1)}, bf16[64,512]{1,0:T(8,128)(2,1)S(1)}, u32[]{:S(2)}, u32[]{:S(2)}) collective-permute-start(bf16[64,512]{1,0:T(8,128)(2,1)S(1)} %get-tuple-element.38), channel_id=1, source_target_pairs={{0,32},{4,36},{8,40},{12,44},{16,48},{20,52},{24,56},{28,60},{32,6... | collective-permute-start | bytes 196616 | tf_op jit(solution)/shard_map/ppermute | solution.py:223
  4.6 9.2 %collective-permute-start.3 = (bf16[64,512]{1,0:T(8,128)(2,1)S(1)}, bf16[64,512]{1,0:T(8,128)(2,1)S(1)}, u32[]{:S(2)}, u32[]{:S(2)}) collective-permute-start(bf16[64,512]{1,0:T(8,128)(2,1)S(1)} %get-tuple-element.39), channel_id=1, source_target_pairs={{0,64},{4,68},{8,72},{12,76},{16,80},{20,84},{24,88},{28,92},{32,9... | collective-permute-start | bytes 196616 | tf_op jit(solution)/shard_map/ppermute | solution.py:223
  7.3 6.5 %collective-permute-start.4 = (bf16[64,512]{1,0:T(8,128)(2,1)S(1)}, bf16[64,512]{1,0:T(8,128)(2,1)S(1)}, u32[]{:S(2)}, u32[]{:S(2)}) collective-permute-start(bf16[64,512]{1,0:T(8,128)(2,1)S(1)} %get-tuple-element.40), channel_id=1, source_target_pairs={{0,96},{4,100},{8,104},{12,108},{16,112},{20,116},{24,120},{28,124... | collective-permute-start | bytes 196616 | tf_op jit(solution)/shard_map/ppermute | solution.py:223
  13.9 7.9 %collective-permute-start.5 = (bf16[64,1024]{1,0:T(8,128)(2,1)S(1)}, bf16[64,1024]{1,0:T(8,128)(2,1)S(1)}, u32[]{:S(2)}, u32[]{:S(2)}) collective-permute-start(bf16[64,1024]{1,0:T(8,128)(2,1)S(1)} %get-tuple-element.47), channel_id=1, source_target_pairs={{0,8},{4,12},{8,16},{12,20},{16,24},{20,28},{24,0},{28,4},{32,40},... | collective-permute-start | bytes 393224 | tf_op jit(solution)/shard_map/ppermute | solution.py:223
  14.2 7.8 %collective-permute-start.6 = (bf16[64,1024]{1,0:T(8,128)(2,1)S(1)}, bf16[64,1024]{1,0:T(8,128)(2,1)S(1)}, u32[]{:S(2)}, u32[]{:S(2)}) collective-permute-start(bf16[64,1024]{1,0:T(8,128)(2,1)S(1)} %get-tuple-element.48), channel_id=1, source_target_pairs={{0,16},{4,20},{8,24},{12,28},{16,0},{20,4},{24,8},{28,12},{32,48},... | collective-permute-start | bytes 393224 | tf_op jit(solution)/shard_map/ppermute | solution.py:223
  16.7 6.6 %collective-permute-start.7 = (bf16[64,1024]{1,0:T(8,128)(2,1)S(1)}, bf16[64,1024]{1,0:T(8,128)(2,1)S(1)}, u32[]{:S(2)}, u32[]{:S(2)}) collective-permute-start(bf16[64,1024]{1,0:T(8,128)(2,1)S(1)} %get-tuple-element.49), channel_id=1, source_target_pairs={{0,24},{4,28},{8,0},{12,4},{16,8},{20,12},{24,16},{28,20},{32,56},... | collective-permute-start | bytes 393224 | tf_op jit(solution)/shard_map/ppermute | solution.py:223
  23.4 1.3 %collective-permute-start.8 = (bf16[64,512]{1,0:T(8,128)(2,1)S(1)}, bf16[64,512]{1,0:T(8,128)(2,1)S(1)}, u32[]{:S(2)}, u32[]{:S(2)}) collective-permute-start(bf16[64,512]{1,0:T(8,128)(2,1)S(1)} %pick.1.rc), channel_id=1, source_target_pairs={{0,4},{4,0},{8,12},{12,8},{16,20},{20,16},{24,28},{28,24},{32,36},... | collective-permute-start | bytes 196616 | tf_op jit(solution)/shard_map/ppermute | solution.py:223
  25.0 7.9 %collective-permute-start.10 = (f32[128,256]{1,0:T(8,128)S(1)}, f32[128,256]{1,0:T(8,128)S(1)}, u32[]{:S(2)}, u32[]{:S(2)}) collective-permute-start(f32[128,256]{1,0:T(8,128)S(1)} %product.1.s0), channel_id=1, source_target_pairs={{0,64},{4,68},{8,72},{12,76},{16,80},{20,84},{24,88},{28,92},{32,9... | collective-permute-start | bytes 393224 | tf_op jit(solution)/shard_map/ppermute | solution.py:223
  25.5 7.3 %collective-permute-start.11 = (f32[128,256]{1,0:T(8,128)S(1)}, f32[128,256]{1,0:T(8,128)S(1)}, u32[]{:S(2)}, u32[]{:S(2)}) collective-permute-start(f32[128,256]{1,0:T(8,128)S(1)} %product.1.s0), channel_id=1, source_target_pairs={{0,96},{4,100},{8,104},{12,108},{16,112},{20,116},{24,120},{28,124... | collective-permute-start | bytes 393224 | tf_op jit(solution)/shard_map/ppermute | solution.py:223
  28.3 6.8 %collective-permute-start.9 = (f32[128,256]{1,0:T(8,128)S(1)}, f32[128,256]{1,0:T(8,128)S(1)}, u32[]{:S(2)}, u32[]{:S(2)}) collective-permute-start(f32[128,256]{1,0:T(8,128)S(1)} %product.1.s0), channel_id=1, source_target_pairs={{0,32},{4,36},{8,40},{12,44},{16,48},{20,52},{24,56},{28,60},{32,6... | collective-permute-start | bytes 393224 | tf_op jit(solution)/shard_map/ppermute | solution.py:223
  35.1 1.3 %collective-permute-start.12 = (bf16[128,256]{1,0:T(8,128)(2,1)S(1)}, bf16[128,256]{1,0:T(8,128)(2,1)S(1)}, u32[]{:S(2)}, u32[]{:S(2)}) collective-permute-start(bf16[128,256]{1,0:T(8,128)(2,1)S(1)} %round_sum.1.w), channel_id=1, source_target_pairs={{0,4},{4,0},{8,12},{12,8},{16,20},{20,16},{24,28},{28,24},{32,36},... | collective-permute-start | bytes 196616 | tf_op jit(solution)/shard_map/ppermute | solution.py:223
  36.5 5.6 %collective-permute-start.14 = (bf16[128,512]{1,0:T(8,128)(2,1)S(1)}, bf16[128,512]{1,0:T(8,128)(2,1)S(1)}, u32[]{:S(2)}, u32[]{:S(2)}) collective-permute-start(bf16[128,512]{1,0:T(8,128)(2,1)S(1)} %join.1.j.refs_1_), channel_id=1, source_target_pairs={{0,8},{4,12},{8,16},{12,20},{16,24},{20,28},{24,0},{28,4},{32,40},... | collective-permute-start | bytes 393224 | tf_op jit(solution)/shard_map/ppermute | solution.py:223
  38.2 9.3 %collective-permute-start.15 = (bf16[128,512]{1,0:T(8,128)(2,1)S(1)}, bf16[128,512]{1,0:T(8,128)(2,1)S(1)}, u32[]{:S(2)}, u32[]{:S(2)}) collective-permute-start(bf16[128,512]{1,0:T(8,128)(2,1)S(1)} %join.1.j.refs_1_), channel_id=1, source_target_pairs={{0,24},{4,28},{8,0},{12,4},{16,8},{20,12},{24,16},{28,20},{32,56},... | collective-permute-start | bytes 393224 | tf_op jit(solution)/shard_map/ppermute | solution.py:223
  38.6 10.3 %collective-permute-start.13 = (bf16[128,512]{1,0:T(8,128)(2,1)S(1)}, bf16[128,512]{1,0:T(8,128)(2,1)S(1)}, u32[]{:S(2)}, u32[]{:S(2)}) collective-permute-start(bf16[128,512]{1,0:T(8,128)(2,1)S(1)} %join.1.j.refs_1_), channel_id=1, source_target_pairs={{0,16},{4,20},{8,24},{12,28},{16,0},{20,4},{24,8},{28,12},{32,48},... | collective-permute-start | bytes 393224 | tf_op jit(solution)/shard_map/ppermute | solution.py:223
  50.3 10.9 %collective-permute-start.16 = (bf16[32,4480]{1,0:T(8,128)(2,1)S(1)}, bf16[32,4480]{1,0:T(8,128)(2,1)S(1)}, u32[]{:S(2)}, u32[]{:S(2)}) collective-permute-start(bf16[32,4480]{1,0:T(8,128)(2,1)S(1)} %get-tuple-element.60), channel_id=1, source_target_pairs={{0,1},{1,2},{2,3},{3,0},{4,5},{5,6},{6,7},{7,4},{8,9},{9,10},{10,1... | collective-permute-start | bytes 860168 | tf_op jit(solution)/shard_map/ppermute | solution.py:227
  52.3 15.7 %collective-permute-start.17 = (bf16[32,4480]{1,0:T(8,128)(2,1)S(1)}, bf16[32,4480]{1,0:T(8,128)(2,1)S(1)}, u32[]{:S(2)}, u32[]{:S(2)}) collective-permute-start(bf16[32,4480]{1,0:T(8,128)(2,1)S(1)} %get-tuple-element.61), channel_id=1, source_target_pairs={{0,2},{1,3},{2,0},{3,1},{4,6},{5,7},{6,4},{7,5},{8,10},{9,11},{10,... | collective-permute-start | bytes 860168 | tf_op jit(solution)/shard_map/ppermute | solution.py:227
  55.9 12.1 %collective-permute-start.18 = (bf16[32,4480]{1,0:T(8,128)(2,1)S(1)}, bf16[32,4480]{1,0:T(8,128)(2,1)S(1)}, u32[]{:S(2)}, u32[]{:S(2)}) collective-permute-start(bf16[32,4480]{1,0:T(8,128)(2,1)S(1)} %get-tuple-element.62), channel_id=1, source_target_pairs={{0,3},{1,0},{2,1},{3,2},{4,7},{5,4},{6,5},{7,6},{8,11},{9,8},{10,9... | collective-permute-start | bytes 860168 | tf_op jit(solution)/shard_map/ppermute | solution.py:227

commit v3 on v2

v3 whole, which is shorter than its diff:
```python
import math

import jax
import jax.numpy as jnp
from jax import lax
from jax.experimental import pallas as pl
from jax.experimental.pallas import tpu as pltpu
from jax.sharding import PartitionSpec as P

BF16, F32 = jnp.bfloat16, jnp.float32
NT = (((1,), (1,)), ((), ()))
VMEM, HBM = pltpu.VMEM, pltpu.HBM
PART = 1024
PARTS = 4


def shape(dims, dtype=BF16):
    return jax.ShapeDtypeStruct(dims, dtype)


def place():
    e = lax.axis_index("ex")
    return e // 8, (e // 2) % 4, e % 2


def at(start, size):
    return pl.ds(pl.multiple_of(start, size), size)


def call(body, name, ins, outs, spaces=None, scratch=(), limit=24 << 20, flops=0, moved=1 << 20, alias=None):
    spaces = spaces or {}
    ins = [
        pltpu.with_memory_space_constraint(a, HBM) if spaces.get(i) in (HBM, pltpu.SMEM) else a
        for i, a in enumerate(ins)
    ]
    return pl.pallas_call(
        body,
        name=name,
        in_specs=[pl.BlockSpec(memory_space=spaces.get(i, VMEM)) for i in range(len(ins))],
        out_specs=[pl.BlockSpec(memory_space=VMEM)] * len(outs),
        out_shape=outs,
        scratch_shapes=scratch,
        input_output_aliases=alias or {},
        compiler_params=pltpu.CompilerParams(vmem_limit_bytes=limit),
        cost_estimate=pl.CostEstimate(flops=flops, bytes_accessed=moved, transcendentals=0),
    )(*ins)


def fetch(owners, q, p, _, w, qc, pv, sems):
    x, y, c = place()
    one = pltpu.make_async_copy(q.at[at(c * 64, 64), :], qc, sems.at[0])
    two = pltpu.make_async_copy(p, pv, sems.at[1])
    one.start()
    two.start()
    o = owners[c]
    xback = lax.rem(x - o // 8 + 4, 4)
    yback = lax.rem(y - (o // 2) % 4 + 4, 4)
    tests = [o % 2 == c, o % 2 != c] + [xback == d for d in range(4)] + [yback == d for d in range(4)]
    for i, test in enumerate(tests):
        w[i, :, :] = jnp.full((16, 128), jnp.where(test, 1.0, 0.0), F32).astype(BF16)
    one.wait()
    two.wait()


def weigh(w, first, refs, columns):
    total = None
    for d, ref in enumerate(refs):
        term = ref(columns) * w[first + d, 0:1, :]
        total = term if total is None else total + term
    return total


def slices(w, qc, qo, pv, po, a0, a1, a2, a3, b0, b1, b2, b3):
    x, y, c = place()
    for d, a in enumerate((a0, a1, a2, a3)):
        for k in range(4):
            columns = at(lax.rem(x + d, 4) * 512 + 128 * k, 128)
            a[:, 128 * k:128 * k + 128] = weigh(
                w, 0, (lambda s: qc[:, s], lambda s: qo[at(c * 64, 64), s]), columns
            )
    for d, b in enumerate((b0, b1, b2, b3)):
        columns = at(c * 1024 + lax.rem(y + d, 4) * 256, 256)
        b[at(c * 64, 64), :] = pv[:, columns]
        b[at(64 - c * 64, 64), :] = po[:, columns]


def pack(w, a0, a1, a2, a3, b1, b2, b3, r, t1, t2, t3):
    for k in range(4):
        columns = slice(128 * k, 128 * k + 128)
        got = weigh(w, 2, [lambda s, a=a: a[:, s] for a in (a0, a1, a2, a3)], columns)
        for t in (r, t1, t2, t3):
            t[:, columns] = got
    for b, t in ((b1, t1), (b2, t2), (b3, t3)):
        t[:, 512:768] = b[0:64, :]
        t[:, 768:1024] = b[64:128, :]


def pick(w, r, u1, u2, u3, g0, rc):
    for k in range(4):
        columns = slice(128 * k, 128 * k + 128)
        rc[:, columns] = weigh(w, 6, [lambda s, u=u: u[:, s] for u in (r, u1, u2, u3)], columns)


def product(rc, ro, b0, u1, u2, u3, s, raw, block):
    _, y, c = place()
    raw[at(c * 64, 64), :] = rc[...]
    raw[at(64 - c * 64, 64), :] = ro[...]
    block[at(y * 128, 128), :] = b0[...]
    for d, u in enumerate((u1, u2, u3)):
        first = lax.rem(y - (d + 1) + 4, 4) * 128
        block[at(first, 64), :] = u[:, 512:768]
        block[at(first + 64, 64), :] = u[:, 768:1024]
    s[...] = jnp.dot(raw[...], block[...], preferred_element_type=F32)


def round_sum(s0, s1, s2, s3, g1, h):
    layer = lax.axis_index("layer")
    for d in range(4):
        rows = at(lax.rem(layer + d, 4) * 32, 32)
        total = ((s0[rows, :] + s2[rows, :]) + (s1[rows, :] + s3[rows, :])).astype(BF16)
        h[32 * d:32 * d + 32, :] = total * jnp.asarray(0.5, BF16)


def join(h, o, _, j):
    _, _, c = place()
    j[:, at(c * 256, 256)] = h[...]
    j[:, at(256 - c * 256, 256)] = o[...]


def norms(part, v, after, gn):
    for i in range(8):
        rows = slice(2048 * part + 256 * i, 2048 * part + 256 * i + 256)
        squares = None
        for k in range(16):
            t = v[rows, 128 * k:128 * k + 128].astype(F32)
            squares = t * t if squares is None else squares + t * t
        line = jnp.sum(squares.T, axis=0, keepdims=True) * 0.5
        for k in range(2):
            gn[2 * i + k:2 * i + k + 1, :] = line[:, 128 * k:128 * k + 128]


def term(d, half, h, v, rows):
    _, y, _ = place()
    columns = at(half * 1024 + lax.rem(y - d + 4, 4) * 256, 256)
    return lax.dot_general(v[rows, columns], h, NT, preferred_element_type=F32)


def both(d, j, v, rows):
    return term(d, 0, j[:, 0:256], v, rows) + term(d, 1, j[:, 256:512], v, rows)


def dots_own(h, v, acc):
    _, _, c = place()
    for i in range(PARTS):
        rows = slice(PART * i, PART * i + PART)
        acc[rows, :] = term(0, c, h[...], v, rows)


def dots_other(h, v, old, acc):
    _, _, c = place()
    for i in range(PARTS):
        rows = slice(PART * i, PART * i + PART)
        acc[rows, :] = old[rows, :] + term(0, 1 - c, h[...], v, rows)


def dots_next(d, j, v, old, acc):
    for i in range(PARTS):
        rows = slice(PART * i, PART * i + PART)
        acc[rows, :] = old[rows, :] + both(d, j, v, rows)


def dots_half(d, first, j, v, old, own, z1, z2, z3):
    for i in range(2):
        rows = slice(first + PART * i, first + PART * i + PART)
        columns = slice(PART * i, PART * i + PART)
        out = (old[rows, :] + both(d, j, v, rows)).T
        own[:, columns] = out[0:32, :]
        for e, z in ((1, z1), (2, z2), (3, z3)):
            z[:, columns] = out[32 * e:32 * e + 32, :].astype(BF16)


def extras(pieces, gs, gn, qn, z1, z2, z3):
    total = None
    for piece in pieces:
        for k in range(4):
            v = piece[:, 128 * k:128 * k + 128].astype(F32)
            total = v * v if total is None else total + v * v
    qsum = jnp.broadcast_to(jnp.sum(total, axis=1, keepdims=True), (128, 128))
    qn[...] = qsum[0:32, :]
    for i, g in enumerate(gs):
        gn[16 * i:16 * i + 16, :] = g[...]
    g = gn[...]
    hi = g.astype(BF16)
    lo = (g - hi.astype(F32)).astype(BF16)
    lane = lax.broadcasted_iota(jnp.int32, (32, 128), 1)
    for e, z in ((1, z1), (2, z2), (3, z3)):
        part = qsum[32 * e:32 * e + 32, :]
        top = part.astype(BF16).astype(F32)
        z[:, 2048:2176] = hi
        z[:, 2176:2304] = lo
        z[:, 2304:2432] = jnp.where(lane < 64, top, part - top).astype(BF16)


def scales(gn, qn, z1, z2, z3, g_ref, q_ref):
    g = gn[...]
    q = qn[:, 0:1]
    for z in (z1, z2, z3):
        g = g + (z[:, 2048:2176].astype(F32) + z[:, 2176:2304].astype(F32))
        q = q + (z[:, 2304:2305].astype(F32) + z[:, 2368:2369].astype(F32))
    g_ref[...] = lax.rsqrt(g * 2.0 + 1e-06)
    q = lax.rsqrt(q * 4.0 + 1e-06) * (2.0 * math.sqrt(8192.0))
    q_ref[...] = jnp.broadcast_to(q, (32, 128))


def finish(first, own, g, q, z1, z2, z3, out, part, sem):
    scale = q[...]
    for i in range(16):
        columns = slice(128 * i, 128 * i + 128)
        t = (own[:, columns] + z2[:, columns].astype(F32)) + (
            z1[:, columns].astype(F32) + z3[:, columns].astype(F32)
        )
        row = first // 128 + i
        part[:, columns] = t * g[row:row + 1, :] * scale
    copy = pltpu.make_async_copy(part, out.at[:, pl.ds(first, 2048)], sem)
    copy.start()
    copy.wait()


def finish_first(own, gn, qn, z1, z2, z3, out, g, q, part, sem):
    scales(gn, qn, z1, z2, z3, g, q)
    finish(0, own, g, q, z1, z2, z3, out, part, sem)


def finish_second(own, g, q, z1, z2, z3, _, out, part, sem):
    finish(2048, own, g, q, z1, z2, z3, out, part, sem)


def moved(dx, dy, dc):
    pairs = []
    for x in range(4):
        for y in range(4):
            for c in range(2):
                to = ((x + dx) % 4 * 4 + (y + dy) % 4) * 2 + (c + dc) % 2
                pairs.append(((x * 4 + y) * 2 + c, to))
    return pairs


def send(a, dx=0, dy=0, dc=0):
    return lax.ppermute(a, "ex", moved(dx, dy, dc))


def send_layer(a, d):
    return lax.ppermute(a, "layer", [(i, (i + d) % 4) for i in range(4)])


def norms_part(part, store, after):
    return call(
        lambda *refs: norms(part, *refs), "norms%d" % part, (store, after), [shape((16, 128), F32)],
        spaces={1: pl.ANY}, flops=3 * 2048 * 2048, moved=8 << 20,
    )[0]


def shards(store, precond, query_slots, owners):

    q = query_slots.reshape(128, 2048)
    p = precond.reshape(64, 2048)
    qo = send(q, dc=1)
    po = send(p, dc=1)
    piece = shape((64, 512))
    block = shape((128, 256))
    w, qc, pv = call(
        fetch, "fetch", (owners, q, p, store), [shape((10, 16, 128)), shape((64, 2048)), shape((64, 2048))],
        spaces={0: pltpu.SMEM, 1: HBM, 2: HBM, 3: HBM}, scratch=[pltpu.SemaphoreType.DMA((2,))],
    )
    a0, a1, a2, a3, b0, b1, b2, b3 = call(slices, "slices", (w, qc, qo, pv, po), [piece] * 4 + [block] * 4)
    a1, a2, a3 = send(a1, dx=1), send(a2, dx=2), send(a3, dx=3)
    r, t1, t2, t3 = call(
        pack, "pack", (w, a0, a1, a2, a3, b1, b2, b3), [piece] + [shape((64, 1024))] * 3,
    )
    g0 = norms_part(0, store, r)
    t1, t2, t3 = send(t1, dy=1), send(t2, dy=2), send(t3, dy=3)
    (rc,) = call(pick, "pick", (w, r, t1, t2, t3, g0), [piece], spaces={5: pl.ANY})
    ro = send(rc, dc=1)
    (s,) = call(
        product, "product", (rc, ro, b0, t1, t2, t3), [shape((128, 256), F32)],
        scratch=[VMEM((128, 512), BF16), VMEM((512, 256), BF16)], flops=2 * 128 * 512 * 256,
    )
    g1 = norms_part(1, store, s)
    s1, s2, s3 = send(s, dx=1), send(s, dx=2), send(s, dx=3)
    (h,) = call(round_sum, "round_sum", (s, s1, s2, s3, g1), [block], spaces={4: pl.ANY})
    o = send(h, dc=1)
    accs = [shape((4096, 128), F32)]
    (acc,) = call(dots_own, "dots_own", (h, store), accs, flops=2 * 128 * 256 * 4096)
    (j,) = call(join, "join", (h, o, acc), [shape((128, 512))], spaces={2: pl.ANY})
    j1, j2, j3 = send(j, dy=1), send(j, dy=2), send(j, dy=3)
    (acc,) = call(dots_other, "dots_other", (o, store, acc), accs, flops=2 * 128 * 256 * 4096, alias={2: 0})
    for d, piece in ((1, j1), (3, j3)):
        (acc,) = call(
            lambda *f, d=d: dots_next(d, *f), "dots_next%d" % d, (piece, store, acc), accs,
            flops=2 * 128 * 512 * 4096, alias={2: 0},
        )
    half = shape((32, 2048), F32)

    def first_half(k, j0, ja, jb, v, old, g0, g1, own, gn, qn, z1, z2, z3):
        dots_half(2, 0, k, v, old, own, z1, z2, z3)
        extras((k, j0, ja, jb), (g0, g1), gn, qn, z1, z2, z3)

    own_a, gn, qn, a1, a2, a3 = call(
        first_half, "dots_first_half", (j2, j, j1, j3, store, acc, g0, g1),
        [half, shape((32, 128), F32), shape((32, 128), F32)] + [shape((32, 2432))] * 3, flops=128 * 512 * 4096,
    )

    def second_half(k, v, old, _, own, z1, z2, z3):
        dots_half(2, 2048, k, v, old, own, z1, z2, z3)

    own_b, b1, b2, b3 = call(
        second_half, "dots_second_half", (j2, store, acc, gn), [half] + [shape((32, 2048))] * 3,
        spaces={3: pl.ANY}, flops=128 * 512 * 4096,
    )
    a1, a3, a2 = send_layer(a1, 1), send_layer(a3, 3), send_layer(a2, 2)
    b1, b3, b2 = send_layer(b1, 1), send_layer(b3, 3), send_layer(b2, 2)
    params = pltpu.CompilerParams(vmem_limit_bytes=24 << 20)
    vm, hbm = pl.BlockSpec(memory_space=VMEM), pl.BlockSpec(memory_space=pl.ANY)
    scratch = [VMEM((32, 2048), F32), pltpu.SemaphoreType.DMA(())]
    full = shape((32, 4096), F32)
    out, g, q = pl.pallas_call(
        finish_first, name="finish_first", in_specs=[vm] * 6, out_specs=[hbm, vm, vm],
        out_shape=[full, shape((32, 128), F32), shape((32, 128), F32)], scratch_shapes=scratch, compiler_params=params,
    )(own_a, gn, qn, a1, a2, a3)
    out = pl.pallas_call(
        finish_second, name="finish_second", in_specs=[vm] * 6 + [hbm], out_specs=hbm, out_shape=full,
        scratch_shapes=scratch, compiler_params=params, input_output_aliases={6: 0},
    )(own_b, g, q, b1, b2, b3, out)
    return out.T


def solution(mesh):
    return jax.shard_map(
        shards,
        mesh=mesh,
        in_specs=(P("ex", "layer"), P("layer", "ex", None), P("ex", None, None, "layer"), P()),
        out_specs=P("ex", "layer"),
        check_vma=False,
    )
```

time: 69.2 us -> 66.3 us (0.958)
  the two profiles are of different devices: /device:TPU:24 before, /device:TPU:1 now
where the time goes in v3:
time: 66.3 us; the launch traced here: 65.2 us
  starting transfers between devices  30.4 us (46%)
  waiting for transfers between devices  20.8 us (31%)
  Pallas kernels  13.7 us (21%)
    ppermute x16, starting transfers between devices, send(): return lax.ppermute(a, 'ex', moved(dx, dy, dc))  21.4 us
    ppermute x16, waiting for transfers between devices, send(): return lax.ppermute(a, 'ex', moved(dx, dy, dc))  15 us
    pallas_call x15, Pallas kernels, call(): pl.pallas_call(body, name=name, in_specs=[pl.BlockSpec(memory_space=space...  12 us
    ppermute x6, starting transfers between devices, send_layer(): return lax.ppermute(a, 'layer', [(i, (i + d) % 4) for i in range(4)])  9.02 us
    ppermute x6, waiting for transfers between devices, send_layer(): return lax.ppermute(a, 'layer', [(i, (i + d) % 4) for i in range(4)])  5.81 us
  transfers between devices with their start and end apart: 22, of which 15 were waited for; matrix products, arithmetic and copies ran while one was open for 0% of the time, Pallas kernels for 18%

profile of v3, /device:TPU:1, one launch (start us, length us, event | category | flops | bytes accessed | tf_op | source)
XLA Modules:
  0.0 65.2 jit_solution(1824905124878855743)
XLA Ops:
  0.0 1.4 %collective-permute-start = (bf16[128,2048]{1,0:T(8,128)(2,1)}, bf16[128,2048]{1,0:T(8,128)(2,1)S(1)}, u32[]{:S(2)}, u32[]{:S(2)}) collective-permute-start(bf16[128,2048]{1,0:T(8,128)(2,1)} %bitcast.3), channel_id=1, source_target_pairs={{0,4},{4,0},{8,12},{12,8},{16,20},{20,16},{24,28},{28,24},{32,36},... | collective-permute-start | bytes 1572872 | tf_op jit(solution)/shard_map/ppermute | solution.py:249
  1.4 0.0 collective-permute-start.1
  1.4 0.0 copy-start
  1.4 2.2 %fetch.1 = (bf16[10,16,128]{2,1,0:T(8,128)(2,1)S(1)}, bf16[64,2048]{1,0:T(8,128)(2,1)S(1)}, bf16[64,2048]{1,0:T(8,128)(2,1)S(1)}) custom-call(s32[2]{0:T(128)} %owners.1, bf16[128,2048]{1,0:T(8,128)(2,1)} %bitcast.4, bf16[64,2048]{1,0:T(8,128)(2,1)} %bitcast.6, bf16[4096,2048]{1,0:T(8,128)(2,1)} %v.7), custom_call_target="tpu_custom_call" | custom-call | bytes 1048576 | tf_op jit(solution)/shard_map/fetch/pallas_call | solution.py:36
  3.6 0.0 collective-permute-done.1.po
  3.6 0.0 collective-permute-done.qo
  3.6 0.2 slices.1
  3.9 1.4 %collective-permute-start.2 = (bf16[64,512]{1,0:T(8,128)(2,1)S(1)}, bf16[64,512]{1,0:T(8,128)(2,1)S(1)}, u32[]{:S(2)}, u32[]{:S(2)}) collective-permute-start(bf16[64,512]{1,0:T(8,128)(2,1)S(1)} %get-tuple-element.37), channel_id=1, source_target_pairs={{0,32},{4,36},{8,40},{12,44},{16,48},{20,52},{24,56},{28,60},{32,6... | collective-permute-start | bytes 196616 | tf_op jit(solution)/shard_map/ppermute | solution.py:249
  5.2 2.5 %collective-permute-start.3 = (bf16[64,512]{1,0:T(8,128)(2,1)S(1)}, bf16[64,512]{1,0:T(8,128)(2,1)S(1)}, u32[]{:S(2)}, u32[]{:S(2)}) collective-permute-start(bf16[64,512]{1,0:T(8,128)(2,1)S(1)} %get-tuple-element.38), channel_id=1, source_target_pairs={{0,64},{4,68},{8,72},{12,76},{16,80},{20,84},{24,88},{28,92},{32,9... | collective-permute-start | bytes 196616 | tf_op jit(solution)/shard_map/ppermute | solution.py:249
  7.7 1.2 %collective-permute-start.4 = (bf16[64,512]{1,0:T(8,128)(2,1)S(1)}, bf16[64,512]{1,0:T(8,128)(2,1)S(1)}, u32[]{:S(2)}, u32[]{:S(2)}) collective-permute-start(bf16[64,512]{1,0:T(8,128)(2,1)S(1)} %get-tuple-element.39), channel_id=1, source_target_pairs={{0,96},{4,100},{8,104},{12,108},{16,112},{20,116},{24,120},{28,124... | collective-permute-start | bytes 196616 | tf_op jit(solution)/shard_map/ppermute | solution.py:249
  8.8 0.0 collective-permute-done.2.a1
  8.8 1.6 %collective-permute-done.3.a2 = bf16[64,512]{1,0:T(8,128)(2,1)S(1)} collective-permute-done((bf16[64,512]{1,0:T(8,128)(2,1)S(1)}, bf16[64,512]{1,0:T(8,128)(2,1)S(1)}, u32[]{:S(2)}, u32[]{:S(2)}) %collective-permute-start.3) | collective-permute-done | bytes 65568 | tf_op jit(solution)/shard_map/ppermute | solution.py:249
  10.5 0.6 collective-permute-done.4.a3
  11.1 0.1 pack.1
  11.2 1.4 %collective-permute-start.5 = (bf16[64,1024]{1,0:T(8,128)(2,1)S(1)}, bf16[64,1024]{1,0:T(8,128)(2,1)S(1)}, u32[]{:S(2)}, u32[]{:S(2)}) collective-permute-start(bf16[64,1024]{1,0:T(8,128)(2,1)S(1)} %get-tuple-element.44), channel_id=1, source_target_pairs={{0,8},{4,12},{8,16},{12,20},{16,24},{20,28},{24,0},{28,4},{32,40},... | collective-permute-start | bytes 393224 | tf_op jit(solution)/shard_map/ppermute | solution.py:249
  12.6 2.6 %collective-permute-start.6 = (bf16[64,1024]{1,0:T(8,128)(2,1)S(1)}, bf16[64,1024]{1,0:T(8,128)(2,1)S(1)}, u32[]{:S(2)}, u32[]{:S(2)}) collective-permute-start(bf16[64,1024]{1,0:T(8,128)(2,1)S(1)} %get-tuple-element.45), channel_id=1, source_target_pairs={{0,16},{4,20},{8,24},{12,28},{16,0},{20,4},{24,8},{28,12},{32,48},... | collective-permute-start | bytes 393224 | tf_op jit(solution)/shard_map/ppermute | solution.py:249
  15.2 1.1 %collective-permute-start.7 = (bf16[64,1024]{1,0:T(8,128)(2,1)S(1)}, bf16[64,1024]{1,0:T(8,128)(2,1)S(1)}, u32[]{:S(2)}, u32[]{:S(2)}) collective-permute-start(bf16[64,1024]{1,0:T(8,128)(2,1)S(1)} %get-tuple-element.46), channel_id=1, source_target_pairs={{0,24},{4,28},{8,0},{12,4},{16,8},{20,12},{24,16},{28,20},{32,56},... | collective-permute-start | bytes 393224 | tf_op jit(solution)/shard_map/ppermute | solution.py:249
  16.3 0.0 copy-done
  16.3 1.7 %norms0.1.g0 = f32[16,128]{1,0:T(8,128)S(1)} custom-call(bf16[4096,2048]{1,0:T(8,128)(2,1)S(1)} %copy-done, bf16[64,512]{1,0:T(8,128)(2,1)S(1)} %get-tuple-element.43.refs_1_.r), custom_call_target="tpu_custom_call" | custom-call | flops 12582912 | bytes 8388608 | tf_op jit(solution)/shard_map/norms0/pallas_call | solution.py:36
  18.0 0.0 collective-permute-done.5.u1
  18.0 1.5 %collective-permute-done.6.u2 = bf16[64,1024]{1,0:T(8,128)(2,1)S(1)} collective-permute-done((bf16[64,1024]{1,0:T(8,128)(2,1)S(1)}, bf16[64,1024]{1,0:T(8,128)(2,1)S(1)}, u32[]{:S(2)}, u32[]{:S(2)}) %collective-permute-start.6) | collective-permute-done | bytes 131104 | tf_op jit(solution)/shard_map/ppermute | solution.py:249
  19.5 0.9 %collective-permute-done.7.u3 = bf16[64,1024]{1,0:T(8,128)(2,1)S(1)} collective-permute-done((bf16[64,1024]{1,0:T(8,128)(2,1)S(1)}, bf16[64,1024]{1,0:T(8,128)(2,1)S(1)}, u32[]{:S(2)}, u32[]{:S(2)}) %collective-permute-start.7) | collective-permute-done | bytes 131104 | tf_op jit(solution)/shard_map/ppermute | solution.py:249
  20.4 2.3 %collective-permute-start.8 = (bf16[64,512]{1,0:T(8,128)(2,1)S(1)}, bf16[64,512]{1,0:T(8,128)(2,1)S(1)}, u32[]{:S(2)}, u32[]{:S(2)}) collective-permute-start(bf16[64,512]{1,0:T(8,128)(2,1)S(1)} %pick.1.rc), channel_id=1, source_target_pairs={{0,4},{4,0},{8,12},{12,8},{16,20},{20,16},{24,28},{28,24},{32,36},... | collective-permute-start | bytes 196616 | tf_op jit(solution)/shard_map/ppermute | solution.py:249
  22.7 0.9 %collective-permute-done.8.ro = bf16[64,512]{1,0:T(8,128)(2,1)S(1)} collective-permute-done((bf16[64,512]{1,0:T(8,128)(2,1)S(1)}, bf16[64,512]{1,0:T(8,128)(2,1)S(1)}, u32[]{:S(2)}, u32[]{:S(2)}) %collective-permute-start.8) | collective-permute-done | bytes 65568 | tf_op jit(solution)/shard_map/ppermute | solution.py:249
  23.6 0.2 product.1.refs_1_.s0
  23.9 2.4 %collective-permute-start.11 = (f32[128,256]{1,0:T(8,128)S(1)}, f32[128,256]{1,0:T(8,128)S(1)}, u32[]{:S(2)}, u32[]{:S(2)}) collective-permute-start(f32[128,256]{1,0:T(8,128)S(1)} %product.1.refs_1_.s0), channel_id=1, source_target_pairs={{0,96},{4,100},{8,104},{12,108},{16,112},{20,116},{24,120},{28,124... | collective-permute-start | bytes 393224 | tf_op jit(solution)/shard_map/ppermute | solution.py:249
  26.3 0.0 collective-permute-start.10
  26.3 0.7 %collective-permute-start.9 = (f32[128,256]{1,0:T(8,128)S(1)}, f32[128,256]{1,0:T(8,128)S(1)}, u32[]{:S(2)}, u32[]{:S(2)}) collective-permute-start(f32[128,256]{1,0:T(8,128)S(1)} %product.1.refs_1_.s0), channel_id=1, source_target_pairs={{0,32},{4,36},{8,40},{12,44},{16,48},{20,52},{24,56},{28,60},{32,6... | collective-permute-start | bytes 393224 | tf_op jit(solution)/shard_map/ppermute | solution.py:249
  27.0 1.7 %norms1.1.g1 = f32[16,128]{1,0:T(8,128)S(1)} custom-call(bf16[4096,2048]{1,0:T(8,128)(2,1)S(1)} %copy-done, f32[128,256]{1,0:T(8,128)S(1)} %product.1.refs_1_.s0), custom_call_target="tpu_custom_call" | custom-call | flops 12582912 | bytes 8388608 | tf_op jit(solution)/shard_map/norms1/pallas_call | solution.py:36
  28.7 0.8 %collective-permute-done.11.s3 = f32[128,256]{1,0:T(8,128)S(1)} collective-permute-done((f32[128,256]{1,0:T(8,128)S(1)}, f32[128,256]{1,0:T(8,128)S(1)}, u32[]{:S(2)}, u32[]{:S(2)}) %collective-permute-start.11) | collective-permute-done | bytes 131104 | tf_op jit(solution)/shard_map/ppermute | solution.py:249
  29.5 2.8 %collective-permute-done.10.s2 = f32[128,256]{1,0:T(8,128)S(1)} collective-permute-done((f32[128,256]{1,0:T(8,128)S(1)}, f32[128,256]{1,0:T(8,128)S(1)}, u32[]{:S(2)}, u32[]{:S(2)}) %collective-permute-start.10) | collective-permute-done | bytes 131104 | tf_op jit(solution)/shard_map/ppermute | solution.py:249
  32.3 3.1 %collective-permute-done.9.s1 = f32[128,256]{1,0:T(8,128)S(1)} collective-permute-done((f32[128,256]{1,0:T(8,128)S(1)}, f32[128,256]{1,0:T(8,128)S(1)}, u32[]{:S(2)}, u32[]{:S(2)}) %collective-permute-start.9) | collective-permute-done | bytes 131104 | tf_op jit(solution)/shard_map/ppermute | solution.py:249
  35.5 0.9 %collective-permute-start.12 = (bf16[128,256]{1,0:T(8,128)(2,1)S(1)}, bf16[128,256]{1,0:T(8,128)(2,1)S(1)}, u32[]{:S(2)}, u32[]{:S(2)}) collective-permute-start(bf16[128,256]{1,0:T(8,128)(2,1)S(1)} %round_sum.1.h), channel_id=1, source_target_pairs={{0,4},{4,0},{8,12},{12,8},{16,20},{20,16},{24,28},{28,24},{32,36},... | collective-permute-start | bytes 196616 | tf_op jit(solution)/shard_map/ppermute | solution.py:249
  36.4 0.7 %dots_own.1._.old = f32[4096,128]{1,0:T(8,128)S(1)} custom-call(bf16[128,256]{1,0:T(8,128)(2,1)S(1)} %round_sum.1.h, bf16[4096,2048]{1,0:T(8,128)(2,1)S(1)} %copy-done), custom_call_target="tpu_custom_call" | custom-call | flops 268435456 | bytes 1048576 | tf_op jit(solution)/shard_map/dots_own/pallas_call | solution.py:36
  37.1 0.2 collective-permute-done.12.o.h
  37.3 0.8 %collective-permute-start.15 = (bf16[128,512]{1,0:T(8,128)(2,1)S(1)}, bf16[128,512]{1,0:T(8,128)(2,1)S(1)}, u32[]{:S(2)}, u32[]{:S(2)}) collective-permute-start(bf16[128,512]{1,0:T(8,128)(2,1)S(1)} %join.1.j0), channel_id=1, source_target_pairs={{0,8},{4,12},{8,16},{12,20},{16,24},{20,28},{24,0},{28,4},{32,40},... | collective-permute-start | bytes 393224 | tf_op jit(solution)/shard_map/ppermute | solution.py:249
  38.1 1.9 %collective-permute-start.14 = (bf16[128,512]{1,0:T(8,128)(2,1)S(1)}, bf16[128,512]{1,0:T(8,128)(2,1)S(1)}, u32[]{:S(2)}, u32[]{:S(2)}) collective-permute-start(bf16[128,512]{1,0:T(8,128)(2,1)S(1)} %join.1.j0), channel_id=1, source_target_pairs={{0,24},{4,28},{8,0},{12,4},{16,8},{20,12},{24,16},{28,20},{32,56},... | collective-permute-start | bytes 393224 | tf_op jit(solution)/shard_map/ppermute | solution.py:249
  40.0 0.8 %collective-permute-start.13 = (bf16[128,512]{1,0:T(8,128)(2,1)S(1)}, bf16[128,512]{1,0:T(8,128)(2,1)S(1)}, u32[]{:S(2)}, u32[]{:S(2)}) collective-permute-start(bf16[128,512]{1,0:T(8,128)(2,1)S(1)} %join.1.j0), channel_id=1, source_target_pairs={{0,16},{4,20},{8,24},{12,28},{16,0},{20,4},{24,8},{28,12},{32,48},... | collective-permute-start | bytes 393224 | tf_op jit(solution)/shard_map/ppermute | solution.py:249
  40.8 0.8 %dots_other.1.f_2_ = f32[4096,128]{1,0:T(8,128)S(1)} custom-call(bf16[128,256]{1,0:T(8,128)(2,1)S(1)} %collective-permute-done.12.o.h, bf16[4096,2048]{1,0:T(8,128)(2,1)S(1)} %copy-done, f32[4096,128]{1,0:T(8,128)S(1)} %dots_own.1._.old), custom_call_target="tpu_custom_call", output_to_operand_aliasing={{}: (2, {})} | custom-call | flops 268435456 | bytes 1048576 | tf_op jit(solution)/shard_map/dots_other/pallas_call | solution.py:36
  41.6 1.7 %collective-permute-done.15.f_0_.ja = bf16[128,512]{1,0:T(8,128)(2,1)S(1)} collective-permute-done((bf16[128,512]{1,0:T(8,128)(2,1)S(1)}, bf16[128,512]{1,0:T(8,128)(2,1)S(1)}, u32[]{:S(2)}, u32[]{:S(2)}) %collective-permute-start.15) | collective-permute-done | bytes 131104 | tf_op jit(solution)/shard_map/ppermute | solution.py:249
  43.3 1.4 %dots_next1.1.f_2_ = f32[4096,128]{1,0:T(8,128)S(1)} custom-call(bf16[128,512]{1,0:T(8,128)(2,1)S(1)} %collective-permute-done.15.f_0_.ja, bf16[4096,2048]{1,0:T(8,128)(2,1)S(1)} %copy-done, f32[4096,128]{1,0:T(8,128)S(1)} %dots_other.1.f_2_), custom_call_target="tpu_custom_call", output_to_operand_aliasing={{}: (2, {})} | custom-call | flops 536870912 | bytes 1048576 | tf_op jit(solution)/shard_map/dots_next1/pallas_call | solution.py:36
  44.7 0.0 collective-permute-done.14.f_0_.jb
  44.7 1.4 %dots_next3.1.old = f32[4096,128]{1,0:T(8,128)S(1)} custom-call(bf16[128,512]{1,0:T(8,128)(2,1)S(1)} %collective-permute-done.14.f_0_.jb, bf16[4096,2048]{1,0:T(8,128)(2,1)S(1)} %copy-done, f32[4096,128]{1,0:T(8,128)S(1)} %dots_next1.1.f_2_), custom_call_target="tpu_custom_call", output_to_operand_aliasing={{}: (2, {})} | custom-call | flops 536870912 | bytes 1048576 | tf_op jit(solution)/shard_map/dots_next3/pallas_call | solution.py:36
  46.0 0.8 %collective-permute-done.13.k = bf16[128,512]{1,0:T(8,128)(2,1)S(1)} collective-permute-done((bf16[128,512]{1,0:T(8,128)(2,1)S(1)}, bf16[128,512]{1,0:T(8,128)(2,1)S(1)}, u32[]{:S(2)}, u32[]{:S(2)}) %collective-permute-start.13) | collective-permute-done | bytes 131104 | tf_op jit(solution)/shard_map/ppermute | solution.py:249
  46.9 0.8 %dots_first_half.1 = (f32[32,2048]{1,0:T(8,128)S(1)}, f32[32,128]{1,0:T(8,128)S(1)}, f32[32,128]{1,0:T(8,128)S(1)}, bf16[32,2432]{1,0:T(8,128)(2,1)S(1)}, bf16[3...) custom-call(bf16[128,512]{1,0:T(8,128)(2,1)S(1)} %collective-permute-done.13.k, bf16[128,512]{1,0:T(8,128)(2,1)S(1)} %join.1.j0, ...), custom_call_target="tpu_custom_call" | custom-call | flops 268435456 | bytes 1048576 | tf_op jit(solution)/shard_map/dots_first_half/pallas_call | solution.py:36
  47.7 1.7 %collective-permute-start.16 = (bf16[32,2432]{1,0:T(8,128)(2,1)S(1)}, bf16[32,2432]{1,0:T(8,128)(2,1)S(1)}, u32[]{:S(2)}, u32[]{:S(2)}) collective-permute-start(bf16[32,2432]{1,0:T(8,128)(2,1)S(1)} %get-tuple-element.52), channel_id=1, source_target_pairs={{0,1},{1,2},{2,3},{3,0},{4,5},{5,6},{6,7},{7,4},{8,9},{9,10},{10,1... | collective-permute-start | bytes 466952 | tf_op jit(solution)/shard_map/ppermute | solution.py:253
  49.4 3.3 %collective-permute-start.17 = (bf16[32,2432]{1,0:T(8,128)(2,1)S(1)}, bf16[32,2432]{1,0:T(8,128)(2,1)S(1)}, u32[]{:S(2)}, u32[]{:S(2)}) collective-permute-start(bf16[32,2432]{1,0:T(8,128)(2,1)S(1)} %get-tuple-element.53), channel_id=1, source_target_pairs={{0,2},{1,3},{2,0},{3,1},{4,6},{5,7},{6,4},{7,5},{8,10},{9,11},{10,... | collective-permute-start | bytes 466952 | tf_op jit(solution)/shard_map/ppermute | solution.py:253
  52.7 0.7 %collective-permute-start.18 = (bf16[32,2432]{1,0:T(8,128)(2,1)S(1)}, bf16[32,2432]{1,0:T(8,128)(2,1)S(1)}, u32[]{:S(2)}, u32[]{:S(2)}) collective-permute-start(bf16[32,2432]{1,0:T(8,128)(2,1)S(1)} %get-tuple-element.54), channel_id=1, source_target_pairs={{0,3},{1,0},{2,1},{3,2},{4,7},{5,4},{6,5},{7,6},{8,11},{9,8},{10,9... | collective-permute-start | bytes 466952 | tf_op jit(solution)/shard_map/ppermute | solution.py:253
  53.4 0.8 %dots_second_half.1 = (f32[32,2048]{1,0:T(8,128)S(1)}, bf16[32,2048]{1,0:T(8,128)(2,1)S(1)}, bf16[32,2048]{1,0:T(8,128)(2,1)S(1)}, bf16[32,2048]{1,0:T(8,128)(2,1)S(1)}) custom-call(bf16[128,512]{1,0:T(8,128)(2,1)S(1)} %collective-permute-done.13.k, bf16[4096,2048]{1,0:T(8,128)(2,1)S(1)} %copy-done, f32[4096,128]{1,0:T(8,128)S(1)} %dots_next3.1.old, ...), custom_call_target="tpu_custom_call" | custom-call | flops 268435456 | bytes 1048576 | tf_op jit(solution)/shard_map/dots_second_half/pallas_call | solution.py:36
  54.2 0.8 %collective-permute-start.19 = (bf16[32,2048]{1,0:T(8,128)(2,1)S(1)}, bf16[32,2048]{1,0:T(8,128)(2,1)S(1)}, u32[]{:S(2)}, u32[]{:S(2)}) collective-permute-start(bf16[32,2048]{1,0:T(8,128)(2,1)S(1)} %get-tuple-element.57), channel_id=1, source_target_pairs={{0,1},{1,2},{2,3},{3,0},{4,5},{5,6},{6,7},{7,4},{8,9},{9,10},{10,1... | collective-permute-start | bytes 393224 | tf_op jit(solution)/shard_map/ppermute | solution.py:253
  55.0 0.4 collective-permute-start.20
  55.5 0.0 collective-permute-done.16.z1
  55.5 2.0 %collective-permute-start.21 = (bf16[32,2048]{1,0:T(8,128)(2,1)S(1)}, bf16[32,2048]{1,0:T(8,128)(2,1)S(1)}, u32[]{:S(2)}, u32[]{:S(2)}) collective-permute-start(bf16[32,2048]{1,0:T(8,128)(2,1)S(1)} %get-tuple-element.59), channel_id=1, source_target_pairs={{0,3},{1,0},{2,1},{3,2},{4,7},{5,4},{6,5},{7,6},{8,11},{9,8},{10,9... | collective-permute-start | bytes 393224 | tf_op jit(solution)/shard_map/ppermute | solution.py:253
  57.5 1.1 %collective-permute-done.17.z2 = bf16[32,2432]{1,0:T(8,128)(2,1)S(1)} collective-permute-done((bf16[32,2432]{1,0:T(8,128)(2,1)S(1)}, bf16[32,2432]{1,0:T(8,128)(2,1)S(1)}, u32[]{:S(2)}, u32[]{:S(2)}) %collective-permute-start.17) | collective-permute-done | bytes 155680 | tf_op jit(solution)/shard_map/ppermute | solution.py:253
  58.6 0.1 collective-permute-done.18.z3
  58.8 0.9 %finish_first.1 = (f32[32,4096]{1,0:T(8,128)}, f32[32,128]{1,0:T(8,128)S(1)}, f32[32,128]{1,0:T(8,128)S(1)}) custom-call(f32[32,2048]{1,0:T(8,128)S(1)} %get-tuple-element.50.own, f32[32,128]{1,0:T(8,128)S(1)} %get-tuple-element.48._.gn, f32[32,128]{1,0:T(8,128)S(1)} %get-tuple-element.51.qn, bf16[32,2432]{1,0:T(8,128)(2,1)S(1)} %collective-permute-done.16.z1, ...), custom_call_target="tpu_custom_call" | custom-call | tf_op jit(solution)/shard_map/finish_first/pallas_call | solution.py:326
  59.6 1.3 %collective-permute-done.19.z1 = bf16[32,2048]{1,0:T(8,128)(2,1)S(1)} collective-permute-done((bf16[32,2048]{1,0:T(8,128)(2,1)S(1)}, bf16[32,2048]{1,0:T(8,128)(2,1)S(1)}, u32[]{:S(2)}, u32[]{:S(2)}) %collective-permute-start.19) | collective-permute-done | bytes 131104 | tf_op jit(solution)/shard_map/ppermute | solution.py:253
  61.0 3.2 %collective-permute-done.20.z2 = bf16[32,2048]{1,0:T(8,128)(2,1)S(1)} collective-permute-done((bf16[32,2048]{1,0:T(8,128)(2,1)S(1)}, bf16[32,2048]{1,0:T(8,128)(2,1)S(1)}, u32[]{:S(2)}, u32[]{:S(2)}) %collective-permute-start.20) | collective-permute-done | bytes 131104 | tf_op jit(solution)/shard_map/ppermute | solution.py:253
  64.2 0.0 collective-permute-done.21.z3
  64.2 0.8 %finish_second.1 = f32[32,4096]{1,0:T(8,128)} custom-call(f32[32,2048]{1,0:T(8,128)S(1)} %get-tuple-element.49.own, f32[32,128]{1,0:T(8,128)S(1)} %get-tuple-element.55.g, f32[32,128]{1,0:T(8,128)S(1)} %get-tuple-element.56.q, bf16[32,2048]{1,0:T(8,128)(2,1)S(1)} %collective-permute-done.19.z1, ...), custom_call_target="tpu_custom_call", output_to_operand_aliasing={{}: (6, {})} | custom-call | tf_op jit(solution)/shard_map/finish_second/pallas_call | solution.py:330
  (3 shorter events, 0.1 us)
Async XLA Ops:
  0.0 3.6 %collective-permute-start = (bf16[128,2048]{1,0:T(8,128)(2,1)}, bf16[128,2048]{1,0:T(8,128)(2,1)S(1)}, u32[]{:S(2)}, u32[]{:S(2)}) collective-permute-start(bf16[128,2048]{1,0:T(8,128)(2,1)} %bitcast.3), channel_id=1, source_target_pairs={{0,4},{4,0},{8,12},{12,8},{16,20},{20,16},{24,28},{28,24},{32,36},... | collective-permute-start | bytes 1572872 | tf_op jit(solution)/shard_map/ppermute | solution.py:249
  1.4 2.2 %collective-permute-start.1 = (bf16[64,2048]{1,0:T(8,128)(2,1)}, bf16[64,2048]{1,0:T(8,128)(2,1)S(1)}, u32[]{:S(2)}, u32[]{:S(2)}) collective-permute-start(bf16[64,2048]{1,0:T(8,128)(2,1)} %bitcast.5), channel_id=1, source_target_pairs={{0,4},{4,0},{8,12},{12,8},{16,20},{20,16},{24,28},{28,24},{32,36},... | collective-permute-start | bytes 786440 | tf_op jit(solution)/shard_map/ppermute | solution.py:249
  1.4 14.9 %copy-start = (bf16[4096,2048]{1,0:T(8,128)(2,1)S(1)}, bf16[4096,2048]{1,0:T(8,128)(2,1)}, u32[]{:S(2)}) copy-start(bf16[4096,2048]{1,0:T(8,128)(2,1)} %v.7) | copy-start | bytes 50331652
  3.9 5.0 %collective-permute-start.2 = (bf16[64,512]{1,0:T(8,128)(2,1)S(1)}, bf16[64,512]{1,0:T(8,128)(2,1)S(1)}, u32[]{:S(2)}, u32[]{:S(2)}) collective-permute-start(bf16[64,512]{1,0:T(8,128)(2,1)S(1)} %get-tuple-element.37), channel_id=1, source_target_pairs={{0,32},{4,36},{8,40},{12,44},{16,48},{20,52},{24,56},{28,60},{32,6... | collective-permute-start | bytes 196616 | tf_op jit(solution)/shard_map/ppermute | solution.py:249
  5.2 5.2 %collective-permute-start.3 = (bf16[64,512]{1,0:T(8,128)(2,1)S(1)}, bf16[64,512]{1,0:T(8,128)(2,1)S(1)}, u32[]{:S(2)}, u32[]{:S(2)}) collective-permute-start(bf16[64,512]{1,0:T(8,128)(2,1)S(1)} %get-tuple-element.38), channel_id=1, source_target_pairs={{0,64},{4,68},{8,72},{12,76},{16,80},{20,84},{24,88},{28,92},{32,9... | collective-permute-start | bytes 196616 | tf_op jit(solution)/shard_map/ppermute | solution.py:249
  7.7 3.4 %collective-permute-start.4 = (bf16[64,512]{1,0:T(8,128)(2,1)S(1)}, bf16[64,512]{1,0:T(8,128)(2,1)S(1)}, u32[]{:S(2)}, u32[]{:S(2)}) collective-permute-start(bf16[64,512]{1,0:T(8,128)(2,1)S(1)} %get-tuple-element.39), channel_id=1, source_target_pairs={{0,96},{4,100},{8,104},{12,108},{16,112},{20,116},{24,120},{28,124... | collective-permute-start | bytes 196616 | tf_op jit(solution)/shard_map/ppermute | solution.py:249
  11.2 6.8 %collective-permute-start.5 = (bf16[64,1024]{1,0:T(8,128)(2,1)S(1)}, bf16[64,1024]{1,0:T(8,128)(2,1)S(1)}, u32[]{:S(2)}, u32[]{:S(2)}) collective-permute-start(bf16[64,1024]{1,0:T(8,128)(2,1)S(1)} %get-tuple-element.44), channel_id=1, source_target_pairs={{0,8},{4,12},{8,16},{12,20},{16,24},{20,28},{24,0},{28,4},{32,40},... | collective-permute-start | bytes 393224 | tf_op jit(solution)/shard_map/ppermute | solution.py:249
  12.6 6.9 %collective-permute-start.6 = (bf16[64,1024]{1,0:T(8,128)(2,1)S(1)}, bf16[64,1024]{1,0:T(8,128)(2,1)S(1)}, u32[]{:S(2)}, u32[]{:S(2)}) collective-permute-start(bf16[64,1024]{1,0:T(8,128)(2,1)S(1)} %get-tuple-element.45), channel_id=1, source_target_pairs={{0,16},{4,20},{8,24},{12,28},{16,0},{20,4},{24,8},{28,12},{32,48},... | collective-permute-start | bytes 393224 | tf_op jit(solution)/shard_map/ppermute | solution.py:249
  15.2 5.1 %collective-permute-start.7 = (bf16[64,1024]{1,0:T(8,128)(2,1)S(1)}, bf16[64,1024]{1,0:T(8,128)(2,1)S(1)}, u32[]{:S(2)}, u32[]{:S(2)}) collective-permute-start(bf16[64,1024]{1,0:T(8,128)(2,1)S(1)} %get-tuple-element.46), channel_id=1, source_target_pairs={{0,24},{4,28},{8,0},{12,4},{16,8},{20,12},{24,16},{28,20},{32,56},... | collective-permute-start | bytes 393224 | tf_op jit(solution)/shard_map/ppermute | solution.py:249
  20.4 3.2 %collective-permute-start.8 = (bf16[64,512]{1,0:T(8,128)(2,1)S(1)}, bf16[64,512]{1,0:T(8,128)(2,1)S(1)}, u32[]{:S(2)}, u32[]{:S(2)}) collective-permute-start(bf16[64,512]{1,0:T(8,128)(2,1)S(1)} %pick.1.rc), channel_id=1, source_target_pairs={{0,4},{4,0},{8,12},{12,8},{16,20},{20,16},{24,28},{28,24},{32,36},... | collective-permute-start | bytes 196616 | tf_op jit(solution)/shard_map/ppermute | solution.py:249
  23.9 5.6 %collective-permute-start.11 = (f32[128,256]{1,0:T(8,128)S(1)}, f32[128,256]{1,0:T(8,128)S(1)}, u32[]{:S(2)}, u32[]{:S(2)}) collective-permute-start(f32[128,256]{1,0:T(8,128)S(1)} %product.1.refs_1_.s0), channel_id=1, source_target_pairs={{0,96},{4,100},{8,104},{12,108},{16,112},{20,116},{24,120},{28,124... | collective-permute-start | bytes 393224 | tf_op jit(solution)/shard_map/ppermute | solution.py:249
  26.3 6.0 %collective-permute-start.10 = (f32[128,256]{1,0:T(8,128)S(1)}, f32[128,256]{1,0:T(8,128)S(1)}, u32[]{:S(2)}, u32[]{:S(2)}) collective-permute-start(f32[128,256]{1,0:T(8,128)S(1)} %product.1.refs_1_.s0), channel_id=1, source_target_pairs={{0,64},{4,68},{8,72},{12,76},{16,80},{20,84},{24,88},{28,92},{32,9... | collective-permute-start | bytes 393224 | tf_op jit(solution)/shard_map/ppermute | solution.py:249
  26.3 9.1 %collective-permute-start.9 = (f32[128,256]{1,0:T(8,128)S(1)}, f32[128,256]{1,0:T(8,128)S(1)}, u32[]{:S(2)}, u32[]{:S(2)}) collective-permute-start(f32[128,256]{1,0:T(8,128)S(1)} %product.1.refs_1_.s0), channel_id=1, source_target_pairs={{0,32},{4,36},{8,40},{12,44},{16,48},{20,52},{24,56},{28,60},{32,6... | collective-permute-start | bytes 393224 | tf_op jit(solution)/shard_map/ppermute | solution.py:249
  35.5 1.8 %collective-permute-start.12 = (bf16[128,256]{1,0:T(8,128)(2,1)S(1)}, bf16[128,256]{1,0:T(8,128)(2,1)S(1)}, u32[]{:S(2)}, u32[]{:S(2)}) collective-permute-start(bf16[128,256]{1,0:T(8,128)(2,1)S(1)} %round_sum.1.h), channel_id=1, source_target_pairs={{0,4},{4,0},{8,12},{12,8},{16,20},{20,16},{24,28},{28,24},{32,36},... | collective-permute-start | bytes 196616 | tf_op jit(solution)/shard_map/ppermute | solution.py:249
  37.3 6.0 %collective-permute-start.15 = (bf16[128,512]{1,0:T(8,128)(2,1)S(1)}, bf16[128,512]{1,0:T(8,128)(2,1)S(1)}, u32[]{:S(2)}, u32[]{:S(2)}) collective-permute-start(bf16[128,512]{1,0:T(8,128)(2,1)S(1)} %join.1.j0), channel_id=1, source_target_pairs={{0,8},{4,12},{8,16},{12,20},{16,24},{20,28},{24,0},{28,4},{32,40},... | collective-permute-start | bytes 393224 | tf_op jit(solution)/shard_map/ppermute | solution.py:249
  38.1 6.6 %collective-permute-start.14 = (bf16[128,512]{1,0:T(8,128)(2,1)S(1)}, bf16[128,512]{1,0:T(8,128)(2,1)S(1)}, u32[]{:S(2)}, u32[]{:S(2)}) collective-permute-start(bf16[128,512]{1,0:T(8,128)(2,1)S(1)} %join.1.j0), channel_id=1, source_target_pairs={{0,24},{4,28},{8,0},{12,4},{16,8},{20,12},{24,16},{28,20},{32,56},... | collective-permute-start | bytes 393224 | tf_op jit(solution)/shard_map/ppermute | solution.py:249
  40.0 6.8 %collective-permute-start.13 = (bf16[128,512]{1,0:T(8,128)(2,1)S(1)}, bf16[128,512]{1,0:T(8,128)(2,1)S(1)}, u32[]{:S(2)}, u32[]{:S(2)}) collective-permute-start(bf16[128,512]{1,0:T(8,128)(2,1)S(1)} %join.1.j0), channel_id=1, source_target_pairs={{0,16},{4,20},{8,24},{12,28},{16,0},{20,4},{24,8},{28,12},{32,48},... | collective-permute-start | bytes 393224 | tf_op jit(solution)/shard_map/ppermute | solution.py:249
  47.7 7.8 %collective-permute-start.16 = (bf16[32,2432]{1,0:T(8,128)(2,1)S(1)}, bf16[32,2432]{1,0:T(8,128)(2,1)S(1)}, u32[]{:S(2)}, u32[]{:S(2)}) collective-permute-start(bf16[32,2432]{1,0:T(8,128)(2,1)S(1)} %get-tuple-element.52), channel_id=1, source_target_pairs={{0,1},{1,2},{2,3},{3,0},{4,5},{5,6},{6,7},{7,4},{8,9},{9,10},{10,1... | collective-permute-start | bytes 466952 | tf_op jit(solution)/shard_map/ppermute | solution.py:253
  49.4 9.2 %collective-permute-start.17 = (bf16[32,2432]{1,0:T(8,128)(2,1)S(1)}, bf16[32,2432]{1,0:T(8,128)(2,1)S(1)}, u32[]{:S(2)}, u32[]{:S(2)}) collective-permute-start(bf16[32,2432]{1,0:T(8,128)(2,1)S(1)} %get-tuple-element.53), channel_id=1, source_target_pairs={{0,2},{1,3},{2,0},{3,1},{4,6},{5,7},{6,4},{7,5},{8,10},{9,11},{10,... | collective-permute-start | bytes 466952 | tf_op jit(solution)/shard_map/ppermute | solution.py:253
  52.7 6.0 %collective-permute-start.18 = (bf16[32,2432]{1,0:T(8,128)(2,1)S(1)}, bf16[32,2432]{1,0:T(8,128)(2,1)S(1)}, u32[]{:S(2)}, u32[]{:S(2)}) collective-permute-start(bf16[32,2432]{1,0:T(8,128)(2,1)S(1)} %get-tuple-element.54), channel_id=1, source_target_pairs={{0,3},{1,0},{2,1},{3,2},{4,7},{5,4},{6,5},{7,6},{8,11},{9,8},{10,9... | collective-permute-start | bytes 466952 | tf_op jit(solution)/shard_map/ppermute | solution.py:253
  54.2 6.8 %collective-permute-start.19 = (bf16[32,2048]{1,0:T(8,128)(2,1)S(1)}, bf16[32,2048]{1,0:T(8,128)(2,1)S(1)}, u32[]{:S(2)}, u32[]{:S(2)}) collective-permute-start(bf16[32,2048]{1,0:T(8,128)(2,1)S(1)} %get-tuple-element.57), channel_id=1, source_target_pairs={{0,1},{1,2},{2,3},{3,0},{4,5},{5,6},{6,7},{7,4},{8,9},{9,10},{10,1... | collective-permute-start | bytes 393224 | tf_op jit(solution)/shard_map/ppermute | solution.py:253
  55.0 9.2 %collective-permute-start.20 = (bf16[32,2048]{1,0:T(8,128)(2,1)S(1)}, bf16[32,2048]{1,0:T(8,128)(2,1)S(1)}, u32[]{:S(2)}, u32[]{:S(2)}) collective-permute-start(bf16[32,2048]{1,0:T(8,128)(2,1)S(1)} %get-tuple-element.58), channel_id=1, source_target_pairs={{0,2},{1,3},{2,0},{3,1},{4,6},{5,7},{6,4},{7,5},{8,10},{9,11},{10,... | collective-permute-start | bytes 393224 | tf_op jit(solution)/shard_map/ppermute | solution.py:253
  55.5 8.8 %collective-permute-start.21 = (bf16[32,2048]{1,0:T(8,128)(2,1)S(1)}, bf16[32,2048]{1,0:T(8,128)(2,1)S(1)}, u32[]{:S(2)}, u32[]{:S(2)}) collective-permute-start(bf16[32,2048]{1,0:T(8,128)(2,1)S(1)} %get-tuple-element.59), channel_id=1, source_target_pairs={{0,3},{1,0},{2,1},{3,2},{4,7},{5,4},{6,5},{7,6},{8,11},{9,8},{10,9... | collective-permute-start | bytes 393224 | tf_op jit(solution)/shard_map/ppermute | solution.py:253

commit v4 on v3

v4 whole, which is shorter than its diff:
```python
import math

import jax
import jax.numpy as jnp
from jax import lax
from jax.experimental import pallas as pl
from jax.experimental.pallas import tpu as pltpu
from jax.sharding import PartitionSpec as P

BF16, F32 = jnp.bfloat16, jnp.float32
NT = (((1,), (1,)), ((), ()))
VMEM, HBM = pltpu.VMEM, pltpu.HBM
PART = 1024
PARTS = 4


def shape(dims, dtype=BF16):
    return jax.ShapeDtypeStruct(dims, dtype)


def place():
    e = lax.axis_index("ex")
    return e // 8, (e // 2) % 4, e % 2


def at(start, size):
    return pl.ds(pl.multiple_of(start, size), size)


def call(body, name, ins, outs, spaces=None, scratch=(), limit=24 << 20, flops=0, moved=1 << 20, alias=None):
    spaces = spaces or {}
    ins = [
        pltpu.with_memory_space_constraint(a, HBM) if spaces.get(i) in (HBM, pltpu.SMEM) else a
        for i, a in enumerate(ins)
    ]
    return pl.pallas_call(
        body,
        name=name,
        in_specs=[pl.BlockSpec(memory_space=spaces.get(i, VMEM)) for i in range(len(ins))],
        out_specs=[pl.BlockSpec(memory_space=VMEM)] * len(outs),
        out_shape=outs,
        scratch_shapes=scratch,
        input_output_aliases=alias or {},
        compiler_params=pltpu.CompilerParams(vmem_limit_bytes=limit),
        cost_estimate=pl.CostEstimate(flops=flops, bytes_accessed=moved, transcendentals=0),
    )(*ins)


def fetch(owners, q, p, _, w, qc, pv, sems):
    x, y, c = place()
    one = pltpu.make_async_copy(q.at[at(c * 64, 64), :], qc, sems.at[0])
    two = pltpu.make_async_copy(p, pv, sems.at[1])
    one.start()
    two.start()
    o = owners[c]
    xback = lax.rem(x - o // 8 + 4, 4)
    yback = lax.rem(y - (o // 2) % 4 + 4, 4)
    tests = [o % 2 == c, o % 2 != c] + [xback == d for d in range(4)] + [yback == d for d in range(4)]
    for i, test in enumerate(tests):
        w[i, :, :] = jnp.full((16, 128), jnp.where(test, 1.0, 0.0), F32).astype(BF16)
    one.wait()
    two.wait()


def weigh(w, first, refs, columns):
    total = None
    for d, ref in enumerate(refs):
        term = ref(columns) * w[first + d, 0:1, :]
        total = term if total is None else total + term
    return total


def slices(w, qc, qo, pv, po, a0, a1, a2, a3, b0, b1, b2, b3):
    x, y, c = place()
    for d, a in enumerate((a0, a1, a2, a3)):
        for k in range(4):
            columns = at(lax.rem(x + d, 4) * 512 + 128 * k, 128)
            a[:, 128 * k:128 * k + 128] = weigh(
                w, 0, (lambda s: qc[:, s], lambda s: qo[at(c * 64, 64), s]), columns
            )
    for d, b in enumerate((b0, b1, b2, b3)):
        columns = at(lax.rem(y + d, 4) * 512, 512)
        b[at(c * 64, 64), :] = pv[:, columns]
        b[at(64 - c * 64, 64), :] = po[:, columns]


def pack(w, a0, a1, a2, a3, b1, b2, b3, r, t1, t2, t3):
    for k in range(4):
        columns = slice(128 * k, 128 * k + 128)
        got = weigh(w, 2, [lambda s, a=a: a[:, s] for a in (a0, a1, a2, a3)], columns)
        for t in (r, t1, t2, t3):
            t[:, columns] = got
    for b, t in ((b1, t1), (b2, t2), (b3, t3)):
        t[:, 512:1024] = b[0:64, :]
        t[:, 1024:1536] = b[64:128, :]


def product(w, r, b0, u1, u2, u3, _, s, s1, s2, s3, raw, block):
    _, y, _ = place()
    for k in range(4):
        columns = slice(128 * k, 128 * k + 128)
        raw[:, columns] = weigh(w, 6, [lambda s, u=u: u[:, s] for u in (r, u1, u2, u3)], columns)
    block[at(y * 128, 128), :] = b0[...]
    for d, u in enumerate((u1, u2, u3)):
        first = lax.rem(y - (d + 1) + 4, 4) * 128
        block[at(first, 64), :] = u[:, 512:1024]
        block[at(first + 64, 64), :] = u[:, 1024:1536]
    total = jnp.dot(raw[...], block[...], preferred_element_type=F32)
    for ref in (s, s1, s2, s3):
        ref[...] = total


def round_sum(s0, s1, s2, s3, _, h):
    total = ((s0[...] + s2[...]) + (s1[...] + s3[...])).astype(BF16)
    h[...] = total * jnp.asarray(0.5, BF16)


def join(h, o, j1, j3, j2):
    _, _, c = place()
    layer = lax.axis_index("layer")
    for ref, block in ((h, c), (o, 1 - c)):
        for t in range(2):
            rows = at(lax.rem(2 * block + t - layer + 4, 4) * 32, 32)
            for j in (j1, j3, j2):
                j[rows, :] = ref[32 * t:32 * t + 32, :]


def norms(part, v, after, gn):
    for i in range(8):
        rows = slice(2048 * part + 256 * i, 2048 * part + 256 * i + 256)
        squares = None
        for k in range(16):
            t = v[rows, 128 * k:128 * k + 128].astype(F32)
            squares = t * t if squares is None else squares + t * t
        line = jnp.sum(squares.T, axis=0, keepdims=True) * 0.5
        for k in range(2):
            gn[2 * i + k:2 * i + k + 1, :] = line[:, 128 * k:128 * k + 128]


def term(d, j, v, rows):
    _, y, _ = place()
    columns = at(lax.rem(y - d + 4, 4) * 512, 512)
    return lax.dot_general(v[rows, columns], j[...], NT, preferred_element_type=F32)


def dots_first(j, v, acc):
    for i in range(PARTS):
        rows = slice(PART * i, PART * i + PART)
        acc[rows, :] = term(0, j, v, rows)


def dots_next(d, j, v, old, acc):
    for i in range(PARTS):
        rows = slice(PART * i, PART * i + PART)
        acc[rows, :] = old[rows, :] + term(d, j, v, rows)


def dots_last(d, j, j0, ja, jb, v, old, g0, g1, own, gn, qn, z1, z3, z2):
    zs = ((1, z1), (2, z2), (3, z3))
    for i in range(PARTS):
        rows = slice(PART * i, PART * i + PART)
        out = (old[rows, :] + term(d, j, v, rows)).T
        own[:, rows] = out[0:32, :]
        for e, z in zs:
            z[:, rows] = out[32 * e:32 * e + 32, :].astype(BF16)
    total = None
    for piece in (j, j0, ja, jb):
        for k in range(4):
            t = piece[:, 128 * k:128 * k + 128].astype(F32)
            total = t * t if total is None else total + t * t
    qsum = jnp.broadcast_to(jnp.sum(total, axis=1, keepdims=True), (128, 128))
    qn[...] = qsum[0:32, :]
    for i, g in enumerate((g0, g1)):
        gn[16 * i:16 * i + 16, :] = g[...]
    g = gn[...]
    hi = g.astype(BF16)
    lo = (g - hi.astype(F32)).astype(BF16)
    lane = lax.broadcasted_iota(jnp.int32, (32, 128), 1)
    for e, z in zs:
        part = qsum[32 * e:32 * e + 32, :]
        top = part.astype(BF16).astype(F32)
        z[:, 4096:4224] = hi
        z[:, 4224:4352] = lo
        z[:, 4352:4480] = jnp.where(lane < 64, top, part - top).astype(BF16)


def norm_parts(z):
    return (
        z[:, 4096:4224].astype(F32) + z[:, 4224:4352].astype(F32),
        z[:, 4352:4353].astype(F32) + z[:, 4416:4417].astype(F32),
    )


def finish_first(own, gn, qn, z1, z3, t, g, q):
    g1, q1 = norm_parts(z1)
    g3, q3 = norm_parts(z3)
    g[...] = gn[...] + (g1 + g3)
    q[...] = jnp.broadcast_to(qn[:, 0:1] + (q1 + q3), (32, 128))
    for i in range(32):
        columns = slice(128 * i, 128 * i + 128)
        t[:, columns] = own[:, columns] + (z1[:, columns].astype(F32) + z3[:, columns].astype(F32))


def finish_last(t, g, q, z2, out, part, sems):
    g2, q2 = norm_parts(z2)
    g = lax.rsqrt((g[...] + g2) * 2.0 + 1e-06)
    q = lax.rsqrt((q[:, 0:1] + q2) * 4.0 + 1e-06) * (2.0 * math.sqrt(8192.0))
    copies = []
    for n in range(4):
        for i in range(8 * n, 8 * n + 8):
            columns = slice(128 * i, 128 * i + 128)
            part[:, columns] = (t[:, columns] + z2[:, columns].astype(F32)) * g[i:i + 1, :] * q
        columns = pl.ds(1024 * n, 1024)
        copies.append(pltpu.make_async_copy(part.at[:, columns], out.at[:, columns], sems.at[n]))
        copies[-1].start()
    for copy in copies:
        copy.wait()


def moved(dx, dy, dc):
    pairs = []
    for x in range(4):
        for y in range(4):
            for c in range(2):
                to = ((x + dx) % 4 * 4 + (y + dy) % 4) * 2 + (c + dc) % 2
                pairs.append(((x * 4 + y) * 2 + c, to))
    return pairs


def send(a, dx=0, dy=0, dc=0):
    return lax.ppermute(a, "ex", moved(dx, dy, dc))


def send_layer(a, d):
    return lax.ppermute(a, "layer", [(i, (i + d) % 4) for i in range(4)])


def norms_part(part, store, after):
    return call(
        lambda *refs: norms(part, *refs), "norms%d" % part, (store, after), [shape((16, 128), F32)],
        spaces={1: pl.ANY}, flops=3 * 2048 * 2048, moved=8 << 20,
    )[0]


def shards(store, precond, query_slots, owners):

    q = query_slots.reshape(128, 2048)
    p = precond.reshape(64, 2048)
    qo = send(q, dc=1)
    po = send(p, dc=1)
    piece = shape((64, 512))
    block = shape((128, 512))
    w, qc, pv = call(
        fetch, "fetch", (owners, q, p, store), [shape((10, 16, 128)), shape((64, 2048)), shape((64, 2048))],
        spaces={0: pltpu.SMEM, 1: HBM, 2: HBM, 3: HBM}, scratch=[pltpu.SemaphoreType.DMA((2,))],
    )
    a0, a1, a2, a3, b0, b1, b2, b3 = call(slices, "slices", (w, qc, qo, pv, po), [piece] * 4 + [block] * 4)
    a1, a2, a3 = send(a1, dx=1), send(a2, dx=2), send(a3, dx=3)
    r, t1, t2, t3 = call(
        pack, "pack", (w, a0, a1, a2, a3, b1, b2, b3), [piece] + [shape((64, 1536))] * 3,
    )
    g0 = norms_part(0, store, r)
    t1, t2, t3 = send(t1, dy=1), send(t2, dy=2), send(t3, dy=3)
    s, s1, s2, s3 = call(
        product, "product", (w, r, b0, t1, t2, t3, g0), [shape((64, 512), F32)] * 4, spaces={6: pl.ANY},
        scratch=[VMEM((64, 512), BF16), VMEM((512, 512), BF16)], flops=2 * 64 * 512 * 512,
    )
    g1 = norms_part(1, store, s)
    s1, s2, s3 = send(s1, dx=1), send(s2, dx=2), send(s3, dx=3)
    (h,) = call(round_sum, "round_sum", (s, s1, s2, s3, g1), [piece], spaces={4: pl.ANY})
    o = send(h, dc=1)
    j1, j3, j2 = call(join, "join", (h, o), [shape((128, 512))] * 3)
    j = j1
    j1, j3, j2 = send(j1, dy=1), send(j3, dy=3), send(j2, dy=2)
    accs = [shape((4096, 128), F32)]
    work = 2 * 128 * 512 * 4096
    (acc,) = call(dots_first, "dots_first", (j, store), accs, flops=work)
    for d, got in ((1, j1), (3, j3)):
        (acc,) = call(
            lambda *f, d=d: dots_next(d, *f), "dots_next%d" % d, (got, store, acc), accs, flops=work, alias={2: 0},
        )
    norm = shape((32, 128), F32)
    own, gn, qn, z1, z3, z2 = call(
        lambda *f: dots_last(2, *f), "dots_last", (j2, j, j1, j3, store, acc, g0, g1),
        [shape((32, 4096), F32), norm, norm] + [shape((32, 4480))] * 3, flops=work,
    )
    z1, z3, z2 = send_layer(z1, 1), send_layer(z3, 3), send_layer(z2, 2)
    t, g, q = call(finish_first, "finish_first", (own, gn, qn, z1, z3), [shape((32, 4096), F32), norm, norm])
    out = pl.pallas_call(
        finish_last,
        name="finish_last",
        in_specs=[pl.BlockSpec(memory_space=VMEM)] * 4,
        out_specs=pl.BlockSpec(memory_space=pl.ANY),
        out_shape=shape((32, 4096), F32),
        scratch_shapes=[VMEM((32, 4096), F32), pltpu.SemaphoreType.DMA((4,))],
        compiler_params=pltpu.CompilerParams(vmem_limit_bytes=24 << 20),
    )(t, g, q, z2)
    return out.T


def solution(mesh):
    return jax.shard_map(
        shards,
        mesh=mesh,
        in_specs=(P("ex", "layer"), P("layer", "ex", None), P("ex", None, None, "layer"), P()),
        out_specs=P("ex", "layer"),
        check_vma=False,
    )
```

time: 66.3 us -> 64.4 us (0.971)
  starting transfers between devices: 30.4 us -> 28.7 us
  Pallas kernels: 13.7 us -> 12.7 us
  waiting for transfers between devices: 20.8 us -> 21.5 us
    ppermute x6 -> x3, waiting for transfers between devices: 5.81 us -> 11.1 us  [send_layer(): return lax.ppermute(a, 'layer', [(i, (i + d) % 4) for i in range(4)])]
    ppermute x16 -> x15, waiting for transfers between devices: 15 us -> 10.4 us  [send(): return lax.ppermute(a, 'ex', moved(dx, dy, dc))]
    ppermute x6 -> x3, starting transfers between devices: 9.02 us -> 5.11 us  [send_layer(): return lax.ppermute(a, 'layer', [(i, (i + d) % 4) for i in range(4)])]
    ppermute x16 -> x15, starting transfers between devices: 21.4 us -> 23.6 us  [send(): return lax.ppermute(a, 'ex', moved(dx, dy, dc))]
    pallas_call x2 -> x1, Pallas kernels: 1.67 us -> 0.99 us  [shards(): pl.pallas_call(finish_last, name='finish_last', in_specs=[pl.BlockSpec(me...]
    pallas_call x15 -> x13, Pallas kernels: 12 us -> 11.7 us  [call(): pl.pallas_call(body, name=name, in_specs=[pl.BlockSpec(memory_space=space...]
  transfers between devices with their start and end apart: 22 -> 18, of which waited for: 15 -> 10; matrix products, arithmetic and copies ran while one was open for 0% -> 0% of each run, Pallas kernels for 18% -> 15%
where the time goes in v4:
time: 64.4 us; the launch traced here: 63.2 us
  starting transfers between devices  28.7 us (45%)
  waiting for transfers between devices  21.5 us (33%)
  Pallas kernels  12.7 us (20%)
    ppermute x15, starting transfers between devices, send(): return lax.ppermute(a, 'ex', moved(dx, dy, dc))  23.6 us
    pallas_call x13, Pallas kernels, call(): pl.pallas_call(body, name=name, in_specs=[pl.BlockSpec(memory_space=space...  11.7 us
    ppermute x3, waiting for transfers between devices, send_layer(): return lax.ppermute(a, 'layer', [(i, (i + d) % 4) for i in range(4)])  11.1 us
    ppermute x15, waiting for transfers between devices, send(): return lax.ppermute(a, 'ex', moved(dx, dy, dc))  10.4 us
    ppermute x3, starting transfers between devices, send_layer(): return lax.ppermute(a, 'layer', [(i, (i + d) % 4) for i in range(4)])  5.11 us
  transfers between devices with their start and end apart: 18, of which 10 were waited for; matrix products, arithmetic and copies ran while one was open for 0% of the time, Pallas kernels for 15%

profile of v4, /device:TPU:1, one launch (start us, length us, event | category | flops | bytes accessed | tf_op | source)
XLA Modules:
  0.0 63.2 jit_solution(17610478286636143103)
XLA Ops:
  0.0 1.4 %collective-permute-start = (bf16[128,2048]{1,0:T(8,128)(2,1)}, bf16[128,2048]{1,0:T(8,128)(2,1)S(1)}, u32[]{:S(2)}, u32[]{:S(2)}) collective-permute-start(bf16[128,2048]{1,0:T(8,128)(2,1)} %bitcast.3), channel_id=1, source_target_pairs={{0,4},{4,0},{8,12},{12,8},{16,20},{20,16},{24,28},{28,24},{32,36},... | collective-permute-start | bytes 1572872 | tf_op jit(solution)/shard_map/ppermute | solution.py:231
  1.4 0.0 collective-permute-start.1
  1.4 0.0 copy-start
  1.4 2.2 %fetch.1 = (bf16[10,16,128]{2,1,0:T(8,128)(2,1)S(1)}, bf16[64,2048]{1,0:T(8,128)(2,1)S(1)}, bf16[64,2048]{1,0:T(8,128)(2,1)S(1)}) custom-call(s32[2]{0:T(128)} %owners.1, bf16[128,2048]{1,0:T(8,128)(2,1)} %bitcast.4, bf16[64,2048]{1,0:T(8,128)(2,1)} %bitcast.6, bf16[4096,2048]{1,0:T(8,128)(2,1)} %f_4_.1), custom_call_target="tpu_custom_call" | custom-call | bytes 1048576 | tf_op jit(solution)/shard_map/fetch/pallas_call | solution.py:36
  3.6 0.0 collective-permute-done.1.po
  3.6 0.0 collective-permute-done.qo
  3.6 0.2 slices.1
  3.9 1.4 %collective-permute-start.2 = (bf16[64,512]{1,0:T(8,128)(2,1)S(1)}, bf16[64,512]{1,0:T(8,128)(2,1)S(1)}, u32[]{:S(2)}, u32[]{:S(2)}) collective-permute-start(bf16[64,512]{1,0:T(8,128)(2,1)S(1)} %get-tuple-element.40), channel_id=1, source_target_pairs={{0,32},{4,36},{8,40},{12,44},{16,48},{20,52},{24,56},{28,60},{32,6... | collective-permute-start | bytes 196616 | tf_op jit(solution)/shard_map/ppermute | solution.py:231
  5.2 2.5 %collective-permute-start.3 = (bf16[64,512]{1,0:T(8,128)(2,1)S(1)}, bf16[64,512]{1,0:T(8,128)(2,1)S(1)}, u32[]{:S(2)}, u32[]{:S(2)}) collective-permute-start(bf16[64,512]{1,0:T(8,128)(2,1)S(1)} %get-tuple-element.41), channel_id=1, source_target_pairs={{0,64},{4,68},{8,72},{12,76},{16,80},{20,84},{24,88},{28,92},{32,9... | collective-permute-start | bytes 196616 | tf_op jit(solution)/shard_map/ppermute | solution.py:231
  7.7 1.2 %collective-permute-start.4 = (bf16[64,512]{1,0:T(8,128)(2,1)S(1)}, bf16[64,512]{1,0:T(8,128)(2,1)S(1)}, u32[]{:S(2)}, u32[]{:S(2)}) collective-permute-start(bf16[64,512]{1,0:T(8,128)(2,1)S(1)} %get-tuple-element.42), channel_id=1, source_target_pairs={{0,96},{4,100},{8,104},{12,108},{16,112},{20,116},{24,120},{28,124... | collective-permute-start | bytes 196616 | tf_op jit(solution)/shard_map/ppermute | solution.py:231
  8.8 0.0 collective-permute-done.2.a1
  8.8 1.6 %collective-permute-done.3.a2 = bf16[64,512]{1,0:T(8,128)(2,1)S(1)} collective-permute-done((bf16[64,512]{1,0:T(8,128)(2,1)S(1)}, bf16[64,512]{1,0:T(8,128)(2,1)S(1)}, u32[]{:S(2)}, u32[]{:S(2)}) %collective-permute-start.3) | collective-permute-done | bytes 65568 | tf_op jit(solution)/shard_map/ppermute | solution.py:231
  10.5 0.6 collective-permute-done.4.a3
  11.1 0.1 pack.1
  11.2 1.4 %collective-permute-start.5 = (bf16[64,1536]{1,0:T(8,128)(2,1)S(1)}, bf16[64,1536]{1,0:T(8,128)(2,1)S(1)}, u32[]{:S(2)}, u32[]{:S(2)}) collective-permute-start(bf16[64,1536]{1,0:T(8,128)(2,1)S(1)} %get-tuple-element.48), channel_id=1, source_target_pairs={{0,8},{4,12},{8,16},{12,20},{16,24},{20,28},{24,0},{28,4},{32,40},... | collective-permute-start | bytes 589832 | tf_op jit(solution)/shard_map/ppermute | solution.py:231
  12.6 2.6 %collective-permute-start.6 = (bf16[64,1536]{1,0:T(8,128)(2,1)S(1)}, bf16[64,1536]{1,0:T(8,128)(2,1)S(1)}, u32[]{:S(2)}, u32[]{:S(2)}) collective-permute-start(bf16[64,1536]{1,0:T(8,128)(2,1)S(1)} %get-tuple-element.49), channel_id=1, source_target_pairs={{0,16},{4,20},{8,24},{12,28},{16,0},{20,4},{24,8},{28,12},{32,48},... | collective-permute-start | bytes 589832 | tf_op jit(solution)/shard_map/ppermute | solution.py:231
  15.2 1.1 %collective-permute-start.7 = (bf16[64,1536]{1,0:T(8,128)(2,1)S(1)}, bf16[64,1536]{1,0:T(8,128)(2,1)S(1)}, u32[]{:S(2)}, u32[]{:S(2)}) collective-permute-start(bf16[64,1536]{1,0:T(8,128)(2,1)S(1)} %get-tuple-element.50), channel_id=1, source_target_pairs={{0,24},{4,28},{8,0},{12,4},{16,8},{20,12},{24,16},{28,20},{32,56},... | collective-permute-start | bytes 589832 | tf_op jit(solution)/shard_map/ppermute | solution.py:231
  16.3 0.0 copy-done
  16.3 1.7 %norms0.1._.f_6_ = f32[16,128]{1,0:T(8,128)S(1)} custom-call(bf16[4096,2048]{1,0:T(8,128)(2,1)S(1)} %copy-done, bf16[64,512]{1,0:T(8,128)(2,1)S(1)} %get-tuple-element.46.refs_1_.r), custom_call_target="tpu_custom_call" | custom-call | flops 12582912 | bytes 8388608 | tf_op jit(solution)/shard_map/norms0/pallas_call | solution.py:36
  18.0 0.0 collective-permute-done.5.u1
  18.0 4.2 %collective-permute-done.6.u2 = bf16[64,1536]{1,0:T(8,128)(2,1)S(1)} collective-permute-done((bf16[64,1536]{1,0:T(8,128)(2,1)S(1)}, bf16[64,1536]{1,0:T(8,128)(2,1)S(1)}, u32[]{:S(2)}, u32[]{:S(2)}) %collective-permute-start.6) | collective-permute-done | bytes 196640 | tf_op jit(solution)/shard_map/ppermute | solution.py:231
  22.2 0.0 collective-permute-done.7.u3
  22.2 0.3 product.1
  22.5 0.1 collective-permute-start.8
  22.6 3.0 %collective-permute-start.9 = (f32[64,512]{1,0:T(8,128)S(1)}, f32[64,512]{1,0:T(8,128)S(1)}, u32[]{:S(2)}, u32[]{:S(2)}) collective-permute-start(f32[64,512]{1,0:T(8,128)S(1)} %get-tuple-element.53), channel_id=1, source_target_pairs={{0,64},{4,68},{8,72},{12,76},{16,80},{20,84},{24,88},{28,92},{32,9... | collective-permute-start | bytes 393224 | tf_op jit(solution)/shard_map/ppermute | solution.py:231
  25.6 0.2 collective-permute-start.10
  25.9 1.7 %norms1.1._.f_7_ = f32[16,128]{1,0:T(8,128)S(1)} custom-call(bf16[4096,2048]{1,0:T(8,128)(2,1)S(1)} %copy-done, f32[64,512]{1,0:T(8,128)S(1)} %get-tuple-element.51.refs_1_.s0), custom_call_target="tpu_custom_call" | custom-call | flops 12582912 | bytes 8388608 | tf_op jit(solution)/shard_map/norms1/pallas_call | solution.py:36
  27.6 0.1 collective-permute-done.8.s1
  27.6 1.7 %collective-permute-done.9.s2 = f32[64,512]{1,0:T(8,128)S(1)} collective-permute-done((f32[64,512]{1,0:T(8,128)S(1)}, f32[64,512]{1,0:T(8,128)S(1)}, u32[]{:S(2)}, u32[]{:S(2)}) %collective-permute-start.9) | collective-permute-done | bytes 131104 | tf_op jit(solution)/shard_map/ppermute | solution.py:231
  29.4 0.2 collective-permute-done.10.s3
  29.6 4.9 %collective-permute-start.11 = (bf16[64,512]{1,0:T(8,128)(2,1)S(1)}, bf16[64,512]{1,0:T(8,128)(2,1)S(1)}, u32[]{:S(2)}, u32[]{:S(2)}) collective-permute-start(bf16[64,512]{1,0:T(8,128)(2,1)S(1)} %round_sum.1.h), channel_id=1, source_target_pairs={{0,4},{4,0},{8,12},{12,8},{16,20},{20,16},{24,28},{28,24},{32,36},... | collective-permute-start | bytes 196616 | tf_op jit(solution)/shard_map/ppermute | solution.py:231
  34.6 0.9 %collective-permute-done.11.o = bf16[64,512]{1,0:T(8,128)(2,1)S(1)} collective-permute-done((bf16[64,512]{1,0:T(8,128)(2,1)S(1)}, bf16[64,512]{1,0:T(8,128)(2,1)S(1)}, u32[]{:S(2)}, u32[]{:S(2)}) %collective-permute-start.11) | collective-permute-done | bytes 65568 | tf_op jit(solution)/shard_map/ppermute | solution.py:231
  35.5 1.5 %collective-permute-start.13 = (bf16[128,512]{1,0:T(8,128)(2,1)S(1)}, bf16[128,512]{1,0:T(8,128)(2,1)S(1)}, u32[]{:S(2)}, u32[]{:S(2)}) collective-permute-start(bf16[128,512]{1,0:T(8,128)(2,1)S(1)} %get-tuple-element.56.j.f_1_), channel_id=1, source_target_pairs={{0,8},{4,12},{8,16},{12,20},{16,24},{20,28},{24,0},{28,4},{32,40},... | collective-permute-start | bytes 393224 | tf_op jit(solution)/shard_map/ppermute | solution.py:231
  37.0 1.3 %collective-permute-start.14 = (bf16[128,512]{1,0:T(8,128)(2,1)S(1)}, bf16[128,512]{1,0:T(8,128)(2,1)S(1)}, u32[]{:S(2)}, u32[]{:S(2)}) collective-permute-start(bf16[128,512]{1,0:T(8,128)(2,1)S(1)} %get-tuple-element.57), channel_id=1, source_target_pairs={{0,24},{4,28},{8,0},{12,4},{16,8},{20,12},{24,16},{28,20},{32,56},... | collective-permute-start | bytes 393224 | tf_op jit(solution)/shard_map/ppermute | solution.py:231
  38.3 1.1 %collective-permute-start.12 = (bf16[128,512]{1,0:T(8,128)(2,1)S(1)}, bf16[128,512]{1,0:T(8,128)(2,1)S(1)}, u32[]{:S(2)}, u32[]{:S(2)}) collective-permute-start(bf16[128,512]{1,0:T(8,128)(2,1)S(1)} %get-tuple-element.55), channel_id=1, source_target_pairs={{0,16},{4,20},{8,24},{12,28},{16,0},{20,4},{24,8},{28,12},{32,48},... | collective-permute-start | bytes 393224 | tf_op jit(solution)/shard_map/ppermute | solution.py:231
  39.4 1.2 %dots_first.1.f_2_ = f32[4096,128]{1,0:T(8,128)S(1)} custom-call(bf16[128,512]{1,0:T(8,128)(2,1)S(1)} %get-tuple-element.56.j.f_1_, bf16[4096,2048]{1,0:T(8,128)(2,1)S(1)} %copy-done), custom_call_target="tpu_custom_call" | custom-call | flops 536870912 | bytes 1048576 | tf_op jit(solution)/shard_map/dots_first/pallas_call | solution.py:36
  40.6 0.9 %collective-permute-done.13.f_0_.f_2_ = bf16[128,512]{1,0:T(8,128)(2,1)S(1)} collective-permute-done((bf16[128,512]{1,0:T(8,128)(2,1)S(1)}, bf16[128,512]{1,0:T(8,128)(2,1)S(1)}, u32[]{:S(2)}, u32[]{:S(2)}) %collective-permute-start.13) | collective-permute-done | bytes 131104 | tf_op jit(solution)/shard_map/ppermute | solution.py:231
  41.5 1.4 %dots_next1.1.f_2_ = f32[4096,128]{1,0:T(8,128)S(1)} custom-call(bf16[128,512]{1,0:T(8,128)(2,1)S(1)} %collective-permute-done.13.f_0_.f_2_, bf16[4096,2048]{1,0:T(8,128)(2,1)S(1)} %copy-done, f32[4096,128]{1,0:T(8,128)S(1)} %dots_first.1.f_2_), custom_call_target="tpu_custom_call", output_to_operand_aliasing={{}: (2, {})} | custom-call | flops 536870912 | bytes 1048576 | tf_op jit(solution)/shard_map/dots_next1/pallas_call | solution.py:36
  42.9 0.0 collective-permute-done.14.f_0_.f_3_
  42.9 1.4 %dots_next3.1.f_5_ = f32[4096,128]{1,0:T(8,128)S(1)} custom-call(bf16[128,512]{1,0:T(8,128)(2,1)S(1)} %collective-permute-done.14.f_0_.f_3_, bf16[4096,2048]{1,0:T(8,128)(2,1)S(1)} %copy-done, f32[4096,128]{1,0:T(8,128)S(1)} %dots_next1.1.f_2_), custom_call_target="tpu_custom_call", output_to_operand_aliasing={{}: (2, {})} | custom-call | flops 536870912 | bytes 1048576 | tf_op jit(solution)/shard_map/dots_next3/pallas_call | solution.py:36
  44.3 0.0 collective-permute-done.12.f_0_
  44.3 1.4 %dots_last.1 = (f32[32,4096]{1,0:T(8,128)S(1)}, f32[32,128]{1,0:T(8,128)S(1)}, f32[32,128]{1,0:T(8,128)S(1)}, bf16[32,4480]{1,0:T(8,128)(2,1)S(1)}, bf16[32,4480...) custom-call(bf16[128,512]{1,0:T(8,128)(2,1)S(1)} %collective-permute-done.12.f_0_, ...), custom_call_target="tpu_custom_call" | custom-call | flops 536870912 | bytes 1048576 | tf_op jit(solution)/shard_map/dots_last/pallas_call | solution.py:36
  45.7 1.7 %collective-permute-start.15 = (bf16[32,4480]{1,0:T(8,128)(2,1)S(1)}, bf16[32,4480]{1,0:T(8,128)(2,1)S(1)}, u32[]{:S(2)}, u32[]{:S(2)}) collective-permute-start(bf16[32,4480]{1,0:T(8,128)(2,1)S(1)} %get-tuple-element.61), channel_id=1, source_target_pairs={{0,1},{1,2},{2,3},{3,0},{4,5},{5,6},{6,7},{7,4},{8,9},{9,10},{10,1... | collective-permute-start | bytes 860168 | tf_op jit(solution)/shard_map/ppermute | solution.py:235
  47.4 2.2 %collective-permute-start.16 = (bf16[32,4480]{1,0:T(8,128)(2,1)S(1)}, bf16[32,4480]{1,0:T(8,128)(2,1)S(1)}, u32[]{:S(2)}, u32[]{:S(2)}) collective-permute-start(bf16[32,4480]{1,0:T(8,128)(2,1)S(1)} %get-tuple-element.62), channel_id=1, source_target_pairs={{0,3},{1,0},{2,1},{3,2},{4,7},{5,4},{6,5},{7,6},{8,11},{9,8},{10,9... | collective-permute-start | bytes 860168 | tf_op jit(solution)/shard_map/ppermute | solution.py:235
  49.6 1.2 %collective-permute-start.17 = (bf16[32,4480]{1,0:T(8,128)(2,1)S(1)}, bf16[32,4480]{1,0:T(8,128)(2,1)S(1)}, u32[]{:S(2)}, u32[]{:S(2)}) collective-permute-start(bf16[32,4480]{1,0:T(8,128)(2,1)S(1)} %get-tuple-element.66), channel_id=1, source_target_pairs={{0,2},{1,3},{2,0},{3,1},{4,6},{5,7},{6,4},{7,5},{8,10},{9,11},{10,... | collective-permute-start | bytes 860168 | tf_op jit(solution)/shard_map/ppermute | solution.py:235
  50.8 4.2 %collective-permute-done.15.z1 = bf16[32,4480]{1,0:T(8,128)(2,1)S(1)} collective-permute-done((bf16[32,4480]{1,0:T(8,128)(2,1)S(1)}, bf16[32,4480]{1,0:T(8,128)(2,1)S(1)}, u32[]{:S(2)}, u32[]{:S(2)}) %collective-permute-start.15) | collective-permute-done | bytes 286752 | tf_op jit(solution)/shard_map/ppermute | solution.py:235
  55.0 0.0 collective-permute-done.16.z3
  55.0 0.1 finish_first.1
  55.2 6.9 %collective-permute-done.17.z2 = bf16[32,4480]{1,0:T(8,128)(2,1)S(1)} collective-permute-done((bf16[32,4480]{1,0:T(8,128)(2,1)S(1)}, bf16[32,4480]{1,0:T(8,128)(2,1)S(1)}, u32[]{:S(2)}, u32[]{:S(2)}) %collective-permute-start.17) | collective-permute-done | bytes 286752 | tf_op jit(solution)/shard_map/ppermute | solution.py:235
  62.1 1.0 %finish_last.1 = f32[32,4096]{1,0:T(8,128)} custom-call(f32[32,4096]{1,0:T(8,128)S(1)} %get-tuple-element.63.t, f32[32,128]{1,0:T(8,128)S(1)} %get-tuple-element.64.g, f32[32,128]{1,0:T(8,128)S(1)} %get-tuple-element.65.q, bf16[32,4480]{1,0:T(8,128)(2,1)S(1)} %collective-permute-done.17.z2), custom_call_target="tpu_custom_call" | custom-call | tf_op jit(solution)/shard_map/finish_last/pallas_call | solution.py:289
  (2 shorter events, 0.1 us)
Async XLA Ops:
  0.0 3.6 %collective-permute-start = (bf16[128,2048]{1,0:T(8,128)(2,1)}, bf16[128,2048]{1,0:T(8,128)(2,1)S(1)}, u32[]{:S(2)}, u32[]{:S(2)}) collective-permute-start(bf16[128,2048]{1,0:T(8,128)(2,1)} %bitcast.3), channel_id=1, source_target_pairs={{0,4},{4,0},{8,12},{12,8},{16,20},{20,16},{24,28},{28,24},{32,36},... | collective-permute-start | bytes 1572872 | tf_op jit(solution)/shard_map/ppermute | solution.py:231
  1.4 2.2 %collective-permute-start.1 = (bf16[64,2048]{1,0:T(8,128)(2,1)}, bf16[64,2048]{1,0:T(8,128)(2,1)S(1)}, u32[]{:S(2)}, u32[]{:S(2)}) collective-permute-start(bf16[64,2048]{1,0:T(8,128)(2,1)} %bitcast.5), channel_id=1, source_target_pairs={{0,4},{4,0},{8,12},{12,8},{16,20},{20,16},{24,28},{28,24},{32,36},... | collective-permute-start | bytes 786440 | tf_op jit(solution)/shard_map/ppermute | solution.py:231
  1.4 14.9 %copy-start = (bf16[4096,2048]{1,0:T(8,128)(2,1)S(1)}, bf16[4096,2048]{1,0:T(8,128)(2,1)}, u32[]{:S(2)}) copy-start(bf16[4096,2048]{1,0:T(8,128)(2,1)} %f_4_.1) | copy-start | bytes 50331652
  3.9 5.0 %collective-permute-start.2 = (bf16[64,512]{1,0:T(8,128)(2,1)S(1)}, bf16[64,512]{1,0:T(8,128)(2,1)S(1)}, u32[]{:S(2)}, u32[]{:S(2)}) collective-permute-start(bf16[64,512]{1,0:T(8,128)(2,1)S(1)} %get-tuple-element.40), channel_id=1, source_target_pairs={{0,32},{4,36},{8,40},{12,44},{16,48},{20,52},{24,56},{28,60},{32,6... | collective-permute-start | bytes 196616 | tf_op jit(solution)/shard_map/ppermute | solution.py:231
  5.2 5.2 %collective-permute-start.3 = (bf16[64,512]{1,0:T(8,128)(2,1)S(1)}, bf16[64,512]{1,0:T(8,128)(2,1)S(1)}, u32[]{:S(2)}, u32[]{:S(2)}) collective-permute-start(bf16[64,512]{1,0:T(8,128)(2,1)S(1)} %get-tuple-element.41), channel_id=1, source_target_pairs={{0,64},{4,68},{8,72},{12,76},{16,80},{20,84},{24,88},{28,92},{32,9... | collective-permute-start | bytes 196616 | tf_op jit(solution)/shard_map/ppermute | solution.py:231
  7.7 3.4 %collective-permute-start.4 = (bf16[64,512]{1,0:T(8,128)(2,1)S(1)}, bf16[64,512]{1,0:T(8,128)(2,1)S(1)}, u32[]{:S(2)}, u32[]{:S(2)}) collective-permute-start(bf16[64,512]{1,0:T(8,128)(2,1)S(1)} %get-tuple-element.42), channel_id=1, source_target_pairs={{0,96},{4,100},{8,104},{12,108},{16,112},{20,116},{24,120},{28,124... | collective-permute-start | bytes 196616 | tf_op jit(solution)/shard_map/ppermute | solution.py:231
  11.2 6.8 %collective-permute-start.5 = (bf16[64,1536]{1,0:T(8,128)(2,1)S(1)}, bf16[64,1536]{1,0:T(8,128)(2,1)S(1)}, u32[]{:S(2)}, u32[]{:S(2)}) collective-permute-start(bf16[64,1536]{1,0:T(8,128)(2,1)S(1)} %get-tuple-element.48), channel_id=1, source_target_pairs={{0,8},{4,12},{8,16},{12,20},{16,24},{20,28},{24,0},{28,4},{32,40},... | collective-permute-start | bytes 589832 | tf_op jit(solution)/shard_map/ppermute | solution.py:231
  12.6 9.6 %collective-permute-start.6 = (bf16[64,1536]{1,0:T(8,128)(2,1)S(1)}, bf16[64,1536]{1,0:T(8,128)(2,1)S(1)}, u32[]{:S(2)}, u32[]{:S(2)}) collective-permute-start(bf16[64,1536]{1,0:T(8,128)(2,1)S(1)} %get-tuple-element.49), channel_id=1, source_target_pairs={{0,16},{4,20},{8,24},{12,28},{16,0},{20,4},{24,8},{28,12},{32,48},... | collective-permute-start | bytes 589832 | tf_op jit(solution)/shard_map/ppermute | solution.py:231
  15.2 7.0 %collective-permute-start.7 = (bf16[64,1536]{1,0:T(8,128)(2,1)S(1)}, bf16[64,1536]{1,0:T(8,128)(2,1)S(1)}, u32[]{:S(2)}, u32[]{:S(2)}) collective-permute-start(bf16[64,1536]{1,0:T(8,128)(2,1)S(1)} %get-tuple-element.50), channel_id=1, source_target_pairs={{0,24},{4,28},{8,0},{12,4},{16,8},{20,12},{24,16},{28,20},{32,56},... | collective-permute-start | bytes 589832 | tf_op jit(solution)/shard_map/ppermute | solution.py:231
  22.5 5.1 %collective-permute-start.8 = (f32[64,512]{1,0:T(8,128)S(1)}, f32[64,512]{1,0:T(8,128)S(1)}, u32[]{:S(2)}, u32[]{:S(2)}) collective-permute-start(f32[64,512]{1,0:T(8,128)S(1)} %get-tuple-element.52), channel_id=1, source_target_pairs={{0,32},{4,36},{8,40},{12,44},{16,48},{20,52},{24,56},{28,60},{32,6... | collective-permute-start | bytes 393224 | tf_op jit(solution)/shard_map/ppermute | solution.py:231
  22.6 6.8 %collective-permute-start.9 = (f32[64,512]{1,0:T(8,128)S(1)}, f32[64,512]{1,0:T(8,128)S(1)}, u32[]{:S(2)}, u32[]{:S(2)}) collective-permute-start(f32[64,512]{1,0:T(8,128)S(1)} %get-tuple-element.53), channel_id=1, source_target_pairs={{0,64},{4,68},{8,72},{12,76},{16,80},{20,84},{24,88},{28,92},{32,9... | collective-permute-start | bytes 393224 | tf_op jit(solution)/shard_map/ppermute | solution.py:231
  25.6 4.0 %collective-permute-start.10 = (f32[64,512]{1,0:T(8,128)S(1)}, f32[64,512]{1,0:T(8,128)S(1)}, u32[]{:S(2)}, u32[]{:S(2)}) collective-permute-start(f32[64,512]{1,0:T(8,128)S(1)} %get-tuple-element.54), channel_id=1, source_target_pairs={{0,96},{4,100},{8,104},{12,108},{16,112},{20,116},{24,120},{28,124... | collective-permute-start | bytes 393224 | tf_op jit(solution)/shard_map/ppermute | solution.py:231
  29.6 5.8 %collective-permute-start.11 = (bf16[64,512]{1,0:T(8,128)(2,1)S(1)}, bf16[64,512]{1,0:T(8,128)(2,1)S(1)}, u32[]{:S(2)}, u32[]{:S(2)}) collective-permute-start(bf16[64,512]{1,0:T(8,128)(2,1)S(1)} %round_sum.1.h), channel_id=1, source_target_pairs={{0,4},{4,0},{8,12},{12,8},{16,20},{20,16},{24,28},{28,24},{32,36},... | collective-permute-start | bytes 196616 | tf_op jit(solution)/shard_map/ppermute | solution.py:231
  35.5 6.0 %collective-permute-start.13 = (bf16[128,512]{1,0:T(8,128)(2,1)S(1)}, bf16[128,512]{1,0:T(8,128)(2,1)S(1)}, u32[]{:S(2)}, u32[]{:S(2)}) collective-permute-start(bf16[128,512]{1,0:T(8,128)(2,1)S(1)} %get-tuple-element.56.j.f_1_), channel_id=1, source_target_pairs={{0,8},{4,12},{8,16},{12,20},{16,24},{20,28},{24,0},{28,4},{32,40},... | collective-permute-start | bytes 393224 | tf_op jit(solution)/shard_map/ppermute | solution.py:231
  37.0 5.9 %collective-permute-start.14 = (bf16[128,512]{1,0:T(8,128)(2,1)S(1)}, bf16[128,512]{1,0:T(8,128)(2,1)S(1)}, u32[]{:S(2)}, u32[]{:S(2)}) collective-permute-start(bf16[128,512]{1,0:T(8,128)(2,1)S(1)} %get-tuple-element.57), channel_id=1, source_target_pairs={{0,24},{4,28},{8,0},{12,4},{16,8},{20,12},{24,16},{28,20},{32,56},... | collective-permute-start | bytes 393224 | tf_op jit(solution)/shard_map/ppermute | solution.py:231
  38.3 6.0 %collective-permute-start.12 = (bf16[128,512]{1,0:T(8,128)(2,1)S(1)}, bf16[128,512]{1,0:T(8,128)(2,1)S(1)}, u32[]{:S(2)}, u32[]{:S(2)}) collective-permute-start(bf16[128,512]{1,0:T(8,128)(2,1)S(1)} %get-tuple-element.55), channel_id=1, source_target_pairs={{0,16},{4,20},{8,24},{12,28},{16,0},{20,4},{24,8},{28,12},{32,48},... | collective-permute-start | bytes 393224 | tf_op jit(solution)/shard_map/ppermute | solution.py:231
  45.7 9.3 %collective-permute-start.15 = (bf16[32,4480]{1,0:T(8,128)(2,1)S(1)}, bf16[32,4480]{1,0:T(8,128)(2,1)S(1)}, u32[]{:S(2)}, u32[]{:S(2)}) collective-permute-start(bf16[32,4480]{1,0:T(8,128)(2,1)S(1)} %get-tuple-element.61), channel_id=1, source_target_pairs={{0,1},{1,2},{2,3},{3,0},{4,5},{5,6},{6,7},{7,4},{8,9},{9,10},{10,1... | collective-permute-start | bytes 860168 | tf_op jit(solution)/shard_map/ppermute | solution.py:235
  47.4 7.7 %collective-permute-start.16 = (bf16[32,4480]{1,0:T(8,128)(2,1)S(1)}, bf16[32,4480]{1,0:T(8,128)(2,1)S(1)}, u32[]{:S(2)}, u32[]{:S(2)}) collective-permute-start(bf16[32,4480]{1,0:T(8,128)(2,1)S(1)} %get-tuple-element.62), channel_id=1, source_target_pairs={{0,3},{1,0},{2,1},{3,2},{4,7},{5,4},{6,5},{7,6},{8,11},{9,8},{10,9... | collective-permute-start | bytes 860168 | tf_op jit(solution)/shard_map/ppermute | solution.py:235
  49.6 12.5 %collective-permute-start.17 = (bf16[32,4480]{1,0:T(8,128)(2,1)S(1)}, bf16[32,4480]{1,0:T(8,128)(2,1)S(1)}, u32[]{:S(2)}, u32[]{:S(2)}) collective-permute-start(bf16[32,4480]{1,0:T(8,128)(2,1)S(1)} %get-tuple-element.66), channel_id=1, source_target_pairs={{0,2},{1,3},{2,0},{3,1},{4,6},{5,7},{6,4},{7,5},{8,10},{9,11},{10,... | collective-permute-start | bytes 860168 | tf_op jit(solution)/shard_map/ppermute | solution.py:235

commit v5 on v4

--- a/solution.py
+++ b/solution.py
@@ -30,7 +30,7 @@
 def call(body, name, ins, outs, spaces=None, scratch=(), limit=24 << 20, flops=0, moved=1 << 20, alias=None):
     spaces = spaces or {}
     ins = [
-        pltpu.with_memory_space_constraint(a, HBM) if spaces.get(i) in (HBM, pltpu.SMEM) else a
+        pltpu.with_memory_space_constraint(a, HBM) if spaces.get(i) is HBM else a
         for i, a in enumerate(ins)
     ]
     return pl.pallas_call(
@@ -46,20 +46,24 @@
     )(*ins)
 
 
-def fetch(owners, q, p, _, w, qc, pv, sems):
+def fetch(owners, q, p, w, qc, pv, o_ref, sems):
     x, y, c = place()
-    one = pltpu.make_async_copy(q.at[at(c * 64, 64), :], qc, sems.at[0])
-    two = pltpu.make_async_copy(p, pv, sems.at[1])
-    one.start()
-    two.start()
-    o = owners[c]
+    copies = [
+        pltpu.make_async_copy(owners, o_ref, sems.at[0]),
+        pltpu.make_async_copy(q.at[at(c * 64, 64), :], qc, sems.at[1]),
+        pltpu.make_async_copy(p, pv, sems.at[2]),
+    ]
+    for copy in copies:
+        copy.start()
+    copies[0].wait()
+    o = o_ref[c]
     xback = lax.rem(x - o // 8 + 4, 4)
     yback = lax.rem(y - (o // 2) % 4 + 4, 4)
     tests = [o % 2 == c, o % 2 != c] + [xback == d for d in range(4)] + [yback == d for d in range(4)]
     for i, test in enumerate(tests):
         w[i, :, :] = jnp.full((16, 128), jnp.where(test, 1.0, 0.0), F32).astype(BF16)
-    one.wait()
-    two.wait()
+    copies[1].wait()
+    copies[2].wait()
 
 
 def weigh(w, first, refs, columns):
@@ -70,49 +74,60 @@
     return total
 
 
-def slices(w, qc, qo, pv, po, a0, a1, a2, a3, b0, b1, b2, b3):
-    x, y, c = place()
+def slices(w, qc, qo, _, a0, a1, a2, a3):
+    x, _, c = place()
     for d, a in enumerate((a0, a1, a2, a3)):
         for k in range(4):
             columns = at(lax.rem(x + d, 4) * 512 + 128 * k, 128)
             a[:, 128 * k:128 * k + 128] = weigh(
                 w, 0, (lambda s: qc[:, s], lambda s: qo[at(c * 64, 64), s]), columns
             )
+
+
+def cut(pv, _, b0, b1, b2, b3):
+    _, y, _ = place()
     for d, b in enumerate((b0, b1, b2, b3)):
-        columns = at(lax.rem(y + d, 4) * 512, 512)
-        b[at(c * 64, 64), :] = pv[:, columns]
-        b[at(64 - c * 64, 64), :] = po[:, columns]
-
-
-def pack(w, a0, a1, a2, a3, b1, b2, b3, r, t1, t2, t3):
+        b[...] = pv[:, at(lax.rem(y + d, 4) * 512, 512)]
+
+
+def choose(w, a0, a1, a2, a3, r1, r2, r3):
     for k in range(4):
         columns = slice(128 * k, 128 * k + 128)
         got = weigh(w, 2, [lambda s, a=a: a[:, s] for a in (a0, a1, a2, a3)], columns)
-        for t in (r, t1, t2, t3):
-            t[:, columns] = got
-    for b, t in ((b1, t1), (b2, t2), (b3, t3)):
-        t[:, 512:1024] = b[0:64, :]
-        t[:, 1024:1536] = b[64:128, :]
-
-
-def product(w, r, b0, u1, u2, u3, _, s, s1, s2, s3, raw, block):
-    _, y, _ = place()
+        for r in (r1, r2, r3):
+            r[:, columns] = got
+
+
+def pick(w, r, u1, u2, u3, raw):
     for k in range(4):
         columns = slice(128 * k, 128 * k + 128)
         raw[:, columns] = weigh(w, 6, [lambda s, u=u: u[:, s] for u in (r, u1, u2, u3)], columns)
-    block[at(y * 128, 128), :] = b0[...]
-    for d, u in enumerate((u1, u2, u3)):
-        first = lax.rem(y - (d + 1) + 4, 4) * 128
-        block[at(first, 64), :] = u[:, 512:1024]
-        block[at(first + 64, 64), :] = u[:, 1024:1536]
+
+
+def product(raw, po, b0, b1, b2, b3, o1, o2, o3, s, s1, s2, s3, block):
+    _, y, c = place()
+    for d, (b, o) in enumerate(((b0, None), (b1, o1), (b2, o2), (b3, o3))):
+        first = lax.rem(y - d + 4, 4) * 128
+        block[at(first + c * 64, 64), :] = b[...]
+        block[at(first + 64 - c * 64, 64), :] = po[:, at(y * 512, 512)] if o is None else o[...]
     total = jnp.dot(raw[...], block[...], preferred_element_type=F32)
     for ref in (s, s1, s2, s3):
         ref[...] = total
 
 
-def round_sum(s0, s1, s2, s3, _, h):
+def round_sum(s0, s1, s2, s3, _, __, h):
     total = ((s0[...] + s2[...]) + (s1[...] + s3[...])).astype(BF16)
     h[...] = total * jnp.asarray(0.5, BF16)
+
+
+WAYS = ((1, 3, 2), (2, 1, 3))
+
+
+def slot(ahead, c):
+    found = 0
+    for k in range(3):
+        found = jnp.where(ahead == jnp.where(c == 0, WAYS[0][k], WAYS[1][k]), k + 1, found)
+    return found
 
 
 def join(h, o, j1, j3, j2):
@@ -120,7 +135,7 @@
     layer = lax.axis_index("layer")
     for ref, block in ((h, c), (o, 1 - c)):
         for t in range(2):
-            rows = at(lax.rem(2 * block + t - layer + 4, 4) * 32, 32)
+            rows = at(slot(lax.rem(2 * block + t - layer + 4, 4), c) * 32, 32)
             for j in (j1, j3, j2):
                 j[rows, :] = ref[32 * t:32 * t + 32, :]
 
@@ -155,7 +170,7 @@
         acc[rows, :] = old[rows, :] + term(d, j, v, rows)
 
 
-def dots_last(d, j, j0, ja, jb, v, old, g0, g1, own, gn, qn, z1, z3, z2):
+def dots_last(d, j, j0, ja, jb, v, old, g0, g1, own, gn, qn, z1, z2, z3):
     zs = ((1, z1), (2, z2), (3, z3))
     for i in range(PARTS):
         rows = slice(PART * i, PART * i + PART)
@@ -172,23 +187,16 @@
     qn[...] = qsum[0:32, :]
     for i, g in enumerate((g0, g1)):
         gn[16 * i:16 * i + 16, :] = g[...]
-    g = gn[...]
-    hi = g.astype(BF16)
-    lo = (g - hi.astype(F32)).astype(BF16)
     lane = lax.broadcasted_iota(jnp.int32, (32, 128), 1)
     for e, z in zs:
         part = qsum[32 * e:32 * e + 32, :]
         top = part.astype(BF16).astype(F32)
-        z[:, 4096:4224] = hi
-        z[:, 4224:4352] = lo
-        z[:, 4352:4480] = jnp.where(lane < 64, top, part - top).astype(BF16)
+        z[:, 4096:4224] = gn[...].astype(BF16)
+        z[:, 4224:4352] = jnp.where(lane < 64, top, part - top).astype(BF16)
 
 
 def norm_parts(z):
-    return (
-        z[:, 4096:4224].astype(F32) + z[:, 4224:4352].astype(F32),
-        z[:, 4352:4353].astype(F32) + z[:, 4416:4417].astype(F32),
-    )
+    return z[:, 4096:4224].astype(F32), z[:, 4224:4225].astype(F32) + z[:, 4288:4289].astype(F32)
 
 
 def finish_first(own, gn, qn, z1, z3, t, g, q):
@@ -231,8 +239,12 @@
     return lax.ppermute(a, "ex", moved(dx, dy, dc))
 
 
-def send_layer(a, d):
-    return lax.ppermute(a, "layer", [(i, (i + d) % 4) for i in range(4)])
+def send_layer(a, k):
+    pairs = []
+    for e in range(32):
+        for layer in range(4):
+            pairs.append((4 * e + layer, 4 * e + (layer + WAYS[e % 2][k]) % 4))
+    return lax.ppermute(a, ("ex", "layer"), pairs)
 
 
 def norms_part(part, store, after):
@@ -243,31 +255,32 @@
 
 
 def shards(store, precond, query_slots, owners):
-
     q = query_slots.reshape(128, 2048)
     p = precond.reshape(64, 2048)
     qo = send(q, dc=1)
     po = send(p, dc=1)
     piece = shape((64, 512))
-    block = shape((128, 512))
     w, qc, pv = call(
-        fetch, "fetch", (owners, q, p, store), [shape((10, 16, 128)), shape((64, 2048)), shape((64, 2048))],
-        spaces={0: pltpu.SMEM, 1: HBM, 2: HBM, 3: HBM}, scratch=[pltpu.SemaphoreType.DMA((2,))],
+        fetch, "fetch", (owners, q, p), [shape((10, 16, 128)), shape((64, 2048)), shape((64, 2048))],
+        spaces={0: HBM, 1: HBM, 2: HBM}, scratch=[pltpu.SMEM((2,), jnp.int32), pltpu.SemaphoreType.DMA((3,))],
     )
-    a0, a1, a2, a3, b0, b1, b2, b3 = call(slices, "slices", (w, qc, qo, pv, po), [piece] * 4 + [block] * 4)
+    a0, a1, a2, a3 = call(slices, "slices", (w, qc, qo, store), [piece] * 4, spaces={3: HBM})
     a1, a2, a3 = send(a1, dx=1), send(a2, dx=2), send(a3, dx=3)
-    r, t1, t2, t3 = call(
-        pack, "pack", (w, a0, a1, a2, a3, b1, b2, b3), [piece] + [shape((64, 1536))] * 3,
+    b0, b1, b2, b3 = call(cut, "cut", (pv, a0), [piece] * 4, spaces={1: pl.ANY})
+    b1, b2, b3 = send(b1, dy=1), send(b2, dy=2), send(b3, dy=3)
+    r1, r2, r3 = call(choose, "choose", (w, a0, a1, a2, a3), [piece] * 3)
+    r = r1
+    r1, r2, r3 = send(r1, dy=1), send(r2, dy=2), send(r3, dy=3)
+    o1, o2, o3 = send(b1, dc=1), send(b2, dc=1), send(b3, dc=1)
+    (raw,) = call(pick, "pick", (w, r, r1, r2, r3), [piece])
+    s, s1, s2, s3 = call(
+        product, "product", (raw, po, b0, b1, b2, b3, o1, o2, o3), [shape((64, 512), F32)] * 4,
+        scratch=[VMEM((512, 512), BF16)], flops=2 * 64 * 512 * 512,
     )
-    g0 = norms_part(0, store, r)
-    t1, t2, t3 = send(t1, dy=1), send(t2, dy=2), send(t3, dy=3)
-    s, s1, s2, s3 = call(
-        product, "product", (w, r, b0, t1, t2, t3, g0), [shape((64, 512), F32)] * 4, spaces={6: pl.ANY},
-        scratch=[VMEM((64, 512), BF16), VMEM((512, 512), BF16)], flops=2 * 64 * 512 * 512,
-    )
+    g0 = norms_part(0, store, s)
     g1 = norms_part(1, store, s)
     s1, s2, s3 = send(s1, dx=1), send(s2, dx=2), send(s3, dx=3)
-    (h,) = call(round_sum, "round_sum", (s, s1, s2, s3, g1), [piece], spaces={4: pl.ANY})
+    (h,) = call(round_sum, "round_sum", (s, s1, s2, s3, g0, g1), [piece], spaces={4: pl.ANY, 5: pl.ANY})
     o = send(h, dc=1)
     j1, j3, j2 = call(join, "join", (h, o), [shape((128, 512))] * 3)
     j = j1
@@ -280,12 +293,12 @@
             lambda *f, d=d: dots_next(d, *f), "dots_next%d" % d, (got, store, acc), accs, flops=work, alias={2: 0},
         )
     norm = shape((32, 128), F32)
-    own, gn, qn, z1, z3, z2 = call(
+    own, gn, qn, z1, z2, z3 = call(
         lambda *f: dots_last(2, *f), "dots_last", (j2, j, j1, j3, store, acc, g0, g1),
-        [shape((32, 4096), F32), norm, norm] + [shape((32, 4480))] * 3, flops=work,
+        [shape((32, 4096), F32), norm, norm] + [shape((32, 4352))] * 3, flops=work,
     )
-    z1, z3, z2 = send_layer(z1, 1), send_layer(z3, 3), send_layer(z2, 2)
-    t, g, q = call(finish_first, "finish_first", (own, gn, qn, z1, z3), [shape((32, 4096), F32), norm, norm])
+    z1, z2, z3 = send_layer(z1, 0), send_layer(z2, 1), send_layer(z3, 2)
+    t, g, q = call(finish_first, "finish_first", (own, gn, qn, z1, z2), [shape((32, 4096), F32), norm, norm])
     out = pl.pallas_call(
         finish_last,
         name="finish_last",
@@ -294,7 +307,7 @@
         out_shape=shape((32, 4096), F32),
         scratch_shapes=[VMEM((32, 4096), F32), pltpu.SemaphoreType.DMA((4,))],
         compiler_params=pltpu.CompilerParams(vmem_limit_bytes=24 << 20),
-    )(t, g, q, z2)
+    )(t, g, q, z3)
     return out.T
 
 

time: 64.4 us -> 63.9 us (level); the launches traced: 63.2 us -> 63.8 us
  starting transfers between devices: 28.7 us -> 35.6 us
  waiting for transfers between devices: 21.5 us -> 16.3 us
  Pallas kernels: 12.7 us -> 11.6 us
    ppermute x15 -> x21, starting transfers between devices: 23.6 us -> 29.3 us  [send(): return lax.ppermute(a, 'ex', moved(dx, dy, dc))]
    ppermute x15 -> x21, waiting for transfers between devices: 10.4 us -> 5.91 us  [send(): return lax.ppermute(a, 'ex', moved(dx, dy, dc))]
    ppermute x3, starting transfers between devices: 5.11 us -> 6.32 us  [send_layer(): return lax.ppermute(a, ('ex', 'layer'), pairs)]
    pallas_call x13 -> x15, Pallas kernels: 11.7 us -> 10.6 us  [call(): pl.pallas_call(body, name=name, in_specs=[pl.BlockSpec(memory_space=space...]
    ppermute x3, waiting for transfers between devices: 11.1 us -> 10.4 us  [send_layer(): return lax.ppermute(a, ('ex', 'layer'), pairs)]
  transfers between devices with their start and end apart: 18 -> 24, of which waited for: 10 -> 12; matrix products, arithmetic and copies ran while one was open for 0% -> 0% of each run, Pallas kernels for 15% -> 14%
where the time goes in v5:
time: 63.9 us; the launch traced here: 63.8 us
  starting transfers between devices  35.6 us (56%)
  waiting for transfers between devices  16.3 us (26%)
  Pallas kernels  11.6 us (18%)
    ppermute x21, starting transfers between devices, send(): return lax.ppermute(a, 'ex', moved(dx, dy, dc))  29.3 us
    pallas_call x15, Pallas kernels, call(): pl.pallas_call(body, name=name, in_specs=[pl.BlockSpec(memory_space=space...  10.6 us
    ppermute x3, waiting for transfers between devices, send_layer(): return lax.ppermute(a, ('ex', 'layer'), pairs)  10.4 us
    ppermute x3, starting transfers between devices, send_layer(): return lax.ppermute(a, ('ex', 'layer'), pairs)  6.32 us
    ppermute x21, waiting for transfers between devices, send(): return lax.ppermute(a, 'ex', moved(dx, dy, dc))  5.91 us
  transfers between devices with their start and end apart: 24, of which 12 were waited for; matrix products, arithmetic and copies ran while one was open for 0% of the time, Pallas kernels for 14%

profile of v5, /device:TPU:1, one launch (start us, length us, event | category | flops | bytes accessed | tf_op | source)
XLA Modules:
  0.0 63.8 jit_solution(9584411329870956490)
XLA Ops:
  0.0 1.4 %collective-permute-start = (bf16[128,2048]{1,0:T(8,128)(2,1)}, bf16[128,2048]{1,0:T(8,128)(2,1)S(1)}, u32[]{:S(2)}, u32[]{:S(2)}) collective-permute-start(bf16[128,2048]{1,0:T(8,128)(2,1)} %bitcast.3), channel_id=1, source_target_pairs={{0,4},{4,0},{8,12},{12,8},{16,20},{20,16},{24,28},{28,24},{32,36},... | collective-permute-start | bytes 1572872 | tf_op jit(solution)/shard_map/ppermute | solution.py:239
  1.4 0.0 collective-permute-start.7
  1.4 1.1 %fetch.1 = (bf16[10,16,128]{2,1,0:T(8,128)(2,1)S(1)}, bf16[64,2048]{1,0:T(8,128)(2,1)S(1)}, bf16[64,2048]{1,0:T(8,128)(2,1)S(1)}) custom-call(s32[2]{0:T(128)} %owners.1, bf16[128,2048]{1,0:T(8,128)(2,1)} %bitcast.4, bf16[64,2048]{1,0:T(8,128)(2,1)} %bitcast.6), custom_call_target="tpu_custom_call" | custom-call | bytes 1048576 | tf_op jit(solution)/shard_map/fetch/pallas_call | solution.py:36
  2.5 0.7 %collective-permute-done.qo = bf16[128,2048]{1,0:T(8,128)(2,1)S(1)} collective-permute-done((bf16[128,2048]{1,0:T(8,128)(2,1)}, bf16[128,2048]{1,0:T(8,128)(2,1)S(1)}, u32[]{:S(2)}, u32[]{:S(2)}) %collective-permute-start) | collective-permute-done | bytes 524320 | tf_op jit(solution)/shard_map/ppermute | solution.py:239
  3.2 0.0 copy-start
  3.2 0.1 slices.1
  3.3 1.4 %collective-permute-start.1 = (bf16[64,512]{1,0:T(8,128)(2,1)S(1)}, bf16[64,512]{1,0:T(8,128)(2,1)S(1)}, u32[]{:S(2)}, u32[]{:S(2)}) collective-permute-start(bf16[64,512]{1,0:T(8,128)(2,1)S(1)} %get-tuple-element.38), channel_id=1, source_target_pairs={{0,32},{4,36},{8,40},{12,44},{16,48},{20,52},{24,56},{28,60},{32,6... | collective-permute-start | bytes 196616 | tf_op jit(solution)/shard_map/ppermute | solution.py:239
  4.7 2.5 %collective-permute-start.2 = (bf16[64,512]{1,0:T(8,128)(2,1)S(1)}, bf16[64,512]{1,0:T(8,128)(2,1)S(1)}, u32[]{:S(2)}, u32[]{:S(2)}) collective-permute-start(bf16[64,512]{1,0:T(8,128)(2,1)S(1)} %get-tuple-element.39), channel_id=1, source_target_pairs={{0,64},{4,68},{8,72},{12,76},{16,80},{20,84},{24,88},{28,92},{32,9... | collective-permute-start | bytes 196616 | tf_op jit(solution)/shard_map/ppermute | solution.py:239
  7.1 1.2 %collective-permute-start.3 = (bf16[64,512]{1,0:T(8,128)(2,1)S(1)}, bf16[64,512]{1,0:T(8,128)(2,1)S(1)}, u32[]{:S(2)}, u32[]{:S(2)}) collective-permute-start(bf16[64,512]{1,0:T(8,128)(2,1)S(1)} %get-tuple-element.40), channel_id=1, source_target_pairs={{0,96},{4,100},{8,104},{12,108},{16,112},{20,116},{24,120},{28,124... | collective-permute-start | bytes 196616 | tf_op jit(solution)/shard_map/ppermute | solution.py:239
  8.3 1.4 %collective-permute-start.8 = (bf16[64,512]{1,0:T(8,128)(2,1)S(1)}, bf16[64,512]{1,0:T(8,128)(2,1)S(1)}, u32[]{:S(2)}, u32[]{:S(2)}) collective-permute-start(bf16[64,512]{1,0:T(8,128)(2,1)S(1)} %get-tuple-element.46), channel_id=1, source_target_pairs={{0,8},{4,12},{8,16},{12,20},{16,24},{20,28},{24,0},{28,4},{32,40},... | collective-permute-start | bytes 196616 | tf_op jit(solution)/shard_map/ppermute | solution.py:239
  9.7 0.0 collective-permute-done.1.a1
  9.7 2.6 %collective-permute-start.9 = (bf16[64,512]{1,0:T(8,128)(2,1)S(1)}, bf16[64,512]{1,0:T(8,128)(2,1)S(1)}, u32[]{:S(2)}, u32[]{:S(2)}) collective-permute-start(bf16[64,512]{1,0:T(8,128)(2,1)S(1)} %get-tuple-element.47), channel_id=1, source_target_pairs={{0,16},{4,20},{8,24},{12,28},{16,0},{20,4},{24,8},{28,12},{32,48},... | collective-permute-start | bytes 196616 | tf_op jit(solution)/shard_map/ppermute | solution.py:239
  12.3 0.0 collective-permute-done.2.a2
  12.3 1.1 %collective-permute-start.10 = (bf16[64,512]{1,0:T(8,128)(2,1)S(1)}, bf16[64,512]{1,0:T(8,128)(2,1)S(1)}, u32[]{:S(2)}, u32[]{:S(2)}) collective-permute-start(bf16[64,512]{1,0:T(8,128)(2,1)S(1)} %get-tuple-element.48), channel_id=1, source_target_pairs={{0,24},{4,28},{8,0},{12,4},{16,8},{20,12},{24,16},{28,20},{32,56},... | collective-permute-start | bytes 196616 | tf_op jit(solution)/shard_map/ppermute | solution.py:239
  13.4 0.0 collective-permute-done.3.a3
  13.4 0.1 choose.1
  13.4 0.3 collective-permute-start.5
  13.7 0.0 collective-permute-done.8.b1
  13.7 2.6 %collective-permute-start.6 = (bf16[64,512]{1,0:T(8,128)(2,1)S(1)}, bf16[64,512]{1,0:T(8,128)(2,1)S(1)}, u32[]{:S(2)}, u32[]{:S(2)}) collective-permute-start(bf16[64,512]{1,0:T(8,128)(2,1)S(1)} %get-tuple-element.43), channel_id=1, source_target_pairs={{0,24},{4,28},{8,0},{12,4},{16,8},{20,12},{24,16},{28,20},{32,56},... | collective-permute-start | bytes 196616 | tf_op jit(solution)/shard_map/ppermute | solution.py:239
  16.3 0.0 collective-permute-done.9.b2
  16.3 0.0 collective-permute-start.4
  16.3 0.0 collective-permute-done.10.b3
  16.3 2.7 %collective-permute-start.11 = (bf16[64,512]{1,0:T(8,128)(2,1)S(1)}, bf16[64,512]{1,0:T(8,128)(2,1)S(1)}, u32[]{:S(2)}, u32[]{:S(2)}) collective-permute-start(bf16[64,512]{1,0:T(8,128)(2,1)S(1)} %collective-permute-done.8.b1), channel_id=1, source_target_pairs={{0,4},{4,0},{8,12},{12,8},{16,20},{20,16},{24,28},{28,24},{32,36},... | collective-permute-start | bytes 196616 | tf_op jit(solution)/shard_map/ppermute | solution.py:239
  19.0 0.0 collective-permute-done.5.u2
  19.0 2.4 %collective-permute-start.12 = (bf16[64,512]{1,0:T(8,128)(2,1)S(1)}, bf16[64,512]{1,0:T(8,128)(2,1)S(1)}, u32[]{:S(2)}, u32[]{:S(2)}) collective-permute-start(bf16[64,512]{1,0:T(8,128)(2,1)S(1)} %collective-permute-done.9.b2), channel_id=1, source_target_pairs={{0,4},{4,0},{8,12},{12,8},{16,20},{20,16},{24,28},{28,24},{32,36},... | collective-permute-start | bytes 196616 | tf_op jit(solution)/shard_map/ppermute | solution.py:239
  21.4 0.0 collective-permute-done.6.u3
  21.4 0.0 collective-permute-start.13
  21.4 0.0 collective-permute-done.4.u1
  21.5 0.0 collective-permute-done.7.po
  21.5 0.0 collective-permute-done.11.o1
  21.5 0.8 %collective-permute-done.12.o2 = bf16[64,512]{1,0:T(8,128)(2,1)S(1)} collective-permute-done((bf16[64,512]{1,0:T(8,128)(2,1)S(1)}, bf16[64,512]{1,0:T(8,128)(2,1)S(1)}, u32[]{:S(2)}, u32[]{:S(2)}) %collective-permute-start.12) | collective-permute-done | bytes 65568 | tf_op jit(solution)/shard_map/ppermute | solution.py:239
  22.3 0.4 collective-permute-done.13.o3
  22.7 0.3 product.1
  23.0 0.4 collective-permute-start.14
  23.4 1.4 %collective-permute-start.15 = (f32[64,512]{1,0:T(8,128)S(1)}, f32[64,512]{1,0:T(8,128)S(1)}, u32[]{:S(2)}, u32[]{:S(2)}) collective-permute-start(f32[64,512]{1,0:T(8,128)S(1)} %get-tuple-element.51), channel_id=1, source_target_pairs={{0,64},{4,68},{8,72},{12,76},{16,80},{20,84},{24,88},{28,92},{32,9... | collective-permute-start | bytes 393224 | tf_op jit(solution)/shard_map/ppermute | solution.py:239
  24.7 1.4 %collective-permute-start.16 = (f32[64,512]{1,0:T(8,128)S(1)}, f32[64,512]{1,0:T(8,128)S(1)}, u32[]{:S(2)}, u32[]{:S(2)}) collective-permute-start(f32[64,512]{1,0:T(8,128)S(1)} %get-tuple-element.52), channel_id=1, source_target_pairs={{0,96},{4,100},{8,104},{12,108},{16,112},{20,116},{24,120},{28,124... | collective-permute-start | bytes 393224 | tf_op jit(solution)/shard_map/ppermute | solution.py:239
  26.2 0.0 copy-done
  26.2 1.7 %norms1.1.__.f_7_ = f32[16,128]{1,0:T(8,128)S(1)} custom-call(bf16[4096,2048]{1,0:T(8,128)(2,1)S(1)} %copy-done, f32[64,512]{1,0:T(8,128)S(1)} %get-tuple-element.49.refs_1_.s0), custom_call_target="tpu_custom_call" | custom-call | flops 12582912 | bytes 8388608 | tf_op jit(solution)/shard_map/norms1/pallas_call | solution.py:36
  27.9 1.7 %norms0.1._.f_6_ = f32[16,128]{1,0:T(8,128)S(1)} custom-call(bf16[4096,2048]{1,0:T(8,128)(2,1)S(1)} %copy-done, f32[64,512]{1,0:T(8,128)S(1)} %get-tuple-element.49.refs_1_.s0), custom_call_target="tpu_custom_call" | custom-call | flops 12582912 | bytes 8388608 | tf_op jit(solution)/shard_map/norms0/pallas_call | solution.py:36
  29.6 0.1 collective-permute-done.14.s1
  29.7 0.1 collective-permute-done.15.s2
  29.7 0.8 %collective-permute-done.16.s3 = f32[64,512]{1,0:T(8,128)S(1)} collective-permute-done((f32[64,512]{1,0:T(8,128)S(1)}, f32[64,512]{1,0:T(8,128)S(1)}, u32[]{:S(2)}, u32[]{:S(2)}) %collective-permute-start.16) | collective-permute-done | bytes 131104 | tf_op jit(solution)/shard_map/ppermute | solution.py:239
  30.6 3.1 %collective-permute-start.17 = (bf16[64,512]{1,0:T(8,128)(2,1)S(1)}, bf16[64,512]{1,0:T(8,128)(2,1)S(1)}, u32[]{:S(2)}, u32[]{:S(2)}) collective-permute-start(bf16[64,512]{1,0:T(8,128)(2,1)S(1)} %round_sum.1.h), channel_id=1, source_target_pairs={{0,4},{4,0},{8,12},{12,8},{16,20},{20,16},{24,28},{28,24},{32,36},... | collective-permute-start | bytes 196616 | tf_op jit(solution)/shard_map/ppermute | solution.py:239
  33.7 0.9 %collective-permute-done.17.o = bf16[64,512]{1,0:T(8,128)(2,1)S(1)} collective-permute-done((bf16[64,512]{1,0:T(8,128)(2,1)S(1)}, bf16[64,512]{1,0:T(8,128)(2,1)S(1)}, u32[]{:S(2)}, u32[]{:S(2)}) %collective-permute-start.17) | collective-permute-done | bytes 65568 | tf_op jit(solution)/shard_map/ppermute | solution.py:239
  34.7 0.4 collective-permute-start.19
  35.0 2.4 %collective-permute-start.20 = (bf16[128,512]{1,0:T(8,128)(2,1)S(1)}, bf16[128,512]{1,0:T(8,128)(2,1)S(1)}, u32[]{:S(2)}, u32[]{:S(2)}) collective-permute-start(bf16[128,512]{1,0:T(8,128)(2,1)S(1)} %get-tuple-element.55), channel_id=1, source_target_pairs={{0,24},{4,28},{8,0},{12,4},{16,8},{20,12},{24,16},{28,20},{32,56},... | collective-permute-start | bytes 393224 | tf_op jit(solution)/shard_map/ppermute | solution.py:239
  37.4 0.8 %collective-permute-start.18 = (bf16[128,512]{1,0:T(8,128)(2,1)S(1)}, bf16[128,512]{1,0:T(8,128)(2,1)S(1)}, u32[]{:S(2)}, u32[]{:S(2)}) collective-permute-start(bf16[128,512]{1,0:T(8,128)(2,1)S(1)} %get-tuple-element.53), channel_id=1, source_target_pairs={{0,16},{4,20},{8,24},{12,28},{16,0},{20,4},{24,8},{28,12},{32,48},... | collective-permute-start | bytes 393224 | tf_op jit(solution)/shard_map/ppermute | solution.py:239
  38.2 1.2 %dots_first.1.f_2_ = f32[4096,128]{1,0:T(8,128)S(1)} custom-call(bf16[128,512]{1,0:T(8,128)(2,1)S(1)} %get-tuple-element.54.j.f_1_, bf16[4096,2048]{1,0:T(8,128)(2,1)S(1)} %copy-done), custom_call_target="tpu_custom_call" | custom-call | flops 536870912 | bytes 1048576 | tf_op jit(solution)/shard_map/dots_first/pallas_call | solution.py:36
  39.5 1.2 %collective-permute-done.19.f_0_.f_2_ = bf16[128,512]{1,0:T(8,128)(2,1)S(1)} collective-permute-done((bf16[128,512]{1,0:T(8,128)(2,1)S(1)}, bf16[128,512]{1,0:T(8,128)(2,1)S(1)}, u32[]{:S(2)}, u32[]{:S(2)}) %collective-permute-start.19) | collective-permute-done | bytes 131104 | tf_op jit(solution)/shard_map/ppermute | solution.py:239
  40.7 1.4 %dots_next1.1.f_2_ = f32[4096,128]{1,0:T(8,128)S(1)} custom-call(bf16[128,512]{1,0:T(8,128)(2,1)S(1)} %collective-permute-done.19.f_0_.f_2_, bf16[4096,2048]{1,0:T(8,128)(2,1)S(1)} %copy-done, f32[4096,128]{1,0:T(8,128)S(1)} %dots_first.1.f_2_), custom_call_target="tpu_custom_call", output_to_operand_aliasing={{}: (2, {})} | custom-call | flops 536870912 | bytes 1048576 | tf_op jit(solution)/shard_map/dots_next1/pallas_call | solution.py:36
  42.0 0.0 collective-permute-done.20.f_0_.f_3_
  42.0 1.4 %dots_next3.1.f_5_ = f32[4096,128]{1,0:T(8,128)S(1)} custom-call(bf16[128,512]{1,0:T(8,128)(2,1)S(1)} %collective-permute-done.20.f_0_.f_3_, bf16[4096,2048]{1,0:T(8,128)(2,1)S(1)} %copy-done, f32[4096,128]{1,0:T(8,128)S(1)} %dots_next1.1.f_2_), custom_call_target="tpu_custom_call", output_to_operand_aliasing={{}: (2, {})} | custom-call | flops 536870912 | bytes 1048576 | tf_op jit(solution)/shard_map/dots_next3/pallas_call | solution.py:36
  43.4 0.9 %collective-permute-done.18.f_0_ = bf16[128,512]{1,0:T(8,128)(2,1)S(1)} collective-permute-done((bf16[128,512]{1,0:T(8,128)(2,1)S(1)}, bf16[128,512]{1,0:T(8,128)(2,1)S(1)}, u32[]{:S(2)}, u32[]{:S(2)}) %collective-permute-start.18) | collective-permute-done | bytes 131104 | tf_op jit(solution)/shard_map/ppermute | solution.py:239
  44.3 1.4 %dots_last.1 = (f32[32,4096]{1,0:T(8,128)S(1)}, f32[32,128]{1,0:T(8,128)S(1)}, f32[32,128]{1,0:T(8,128)S(1)}, bf16[32,4352]{1,0:T(8,128)(2,1)S(1)}, bf16[32,4352...) custom-call(bf16[128,512]{1,0:T(8,128)(2,1)S(1)} %collective-permute-done.18.f_0_, ...), custom_call_target="tpu_custom_call" | custom-call | flops 536870912 | bytes 1048576 | tf_op jit(solution)/shard_map/dots_last/pallas_call | solution.py:36
  45.7 3.6 %collective-permute-start.21 = (bf16[32,4352]{1,0:T(8,128)(2,1)S(1)}, bf16[32,4352]{1,0:T(8,128)(2,1)S(1)}, u32[]{:S(2)}, u32[]{:S(2)}) collective-permute-start(bf16[32,4352]{1,0:T(8,128)(2,1)S(1)} %get-tuple-element.59), channel_id=1, source_target_pairs={{0,1},{1,2},{2,3},{3,0},{4,6},{5,7},{6,4},{7,5},{8,9},{9,10},{10,1... | collective-permute-start | bytes 835592 | tf_op jit(solution)/shard_map/ppermute | solution.py:247
  49.4 0.7 %collective-permute-start.22 = (bf16[32,4352]{1,0:T(8,128)(2,1)S(1)}, bf16[32,4352]{1,0:T(8,128)(2,1)S(1)}, u32[]{:S(2)}, u32[]{:S(2)}) collective-permute-start(bf16[32,4352]{1,0:T(8,128)(2,1)S(1)} %get-tuple-element.60), channel_id=1, source_target_pairs={{0,3},{1,0},{2,1},{3,2},{4,5},{5,6},{6,7},{7,4},{8,11},{9,8},{10,9... | collective-permute-start | bytes 835592 | tf_op jit(solution)/shard_map/ppermute | solution.py:247
  50.1 1.9 %collective-permute-start.23 = (bf16[32,4352]{1,0:T(8,128)(2,1)S(1)}, bf16[32,4352]{1,0:T(8,128)(2,1)S(1)}, u32[]{:S(2)}, u32[]{:S(2)}) collective-permute-start(bf16[32,4352]{1,0:T(8,128)(2,1)S(1)} %get-tuple-element.64), channel_id=1, source_target_pairs={{0,2},{1,3},{2,0},{3,1},{4,7},{5,4},{6,5},{7,6},{8,10},{9,11},{10,... | collective-permute-start | bytes 835592 | tf_op jit(solution)/shard_map/ppermute | solution.py:247
  52.0 3.7 %collective-permute-done.21.z1 = bf16[32,4352]{1,0:T(8,128)(2,1)S(1)} collective-permute-done((bf16[32,4352]{1,0:T(8,128)(2,1)S(1)}, bf16[32,4352]{1,0:T(8,128)(2,1)S(1)}, u32[]{:S(2)}, u32[]{:S(2)}) %collective-permute-start.21) | collective-permute-done | bytes 278560 | tf_op jit(solution)/shard_map/ppermute | solution.py:247
  55.7 5.7 %collective-permute-done.22.z3 = bf16[32,4352]{1,0:T(8,128)(2,1)S(1)} collective-permute-done((bf16[32,4352]{1,0:T(8,128)(2,1)S(1)}, bf16[32,4352]{1,0:T(8,128)(2,1)S(1)}, u32[]{:S(2)}, u32[]{:S(2)}) %collective-permute-start.22) | collective-permute-done | bytes 278560 | tf_op jit(solution)/shard_map/ppermute | solution.py:247
  61.4 0.3 finish_first.1
  61.7 0.9 %collective-permute-done.23.z2 = bf16[32,4352]{1,0:T(8,128)(2,1)S(1)} collective-permute-done((bf16[32,4352]{1,0:T(8,128)(2,1)S(1)}, bf16[32,4352]{1,0:T(8,128)(2,1)S(1)}, u32[]{:S(2)}, u32[]{:S(2)}) %collective-permute-start.23) | collective-permute-done | bytes 278560 | tf_op jit(solution)/shard_map/ppermute | solution.py:247
  62.6 1.0 %finish_last.1 = f32[32,4096]{1,0:T(8,128)} custom-call(f32[32,4096]{1,0:T(8,128)S(1)} %get-tuple-element.61.t, f32[32,128]{1,0:T(8,128)S(1)} %get-tuple-element.62.g, f32[32,128]{1,0:T(8,128)S(1)} %get-tuple-element.63.q, bf16[32,4352]{1,0:T(8,128)(2,1)S(1)} %collective-permute-done.23.z2), custom_call_target="tpu_custom_call" | custom-call | tf_op jit(solution)/shard_map/finish_last/pallas_call | solution.py:302
  (4 shorter events, 0.1 us)
Async XLA Ops:
  0.0 3.2 %collective-permute-start = (bf16[128,2048]{1,0:T(8,128)(2,1)}, bf16[128,2048]{1,0:T(8,128)(2,1)S(1)}, u32[]{:S(2)}, u32[]{:S(2)}) collective-permute-start(bf16[128,2048]{1,0:T(8,128)(2,1)} %bitcast.3), channel_id=1, source_target_pairs={{0,4},{4,0},{8,12},{12,8},{16,20},{20,16},{24,28},{28,24},{32,36},... | collective-permute-start | bytes 1572872 | tf_op jit(solution)/shard_map/ppermute | solution.py:239
  1.4 20.1 %collective-permute-start.7 = (bf16[64,2048]{1,0:T(8,128)(2,1)}, bf16[64,2048]{1,0:T(8,128)(2,1)S(1)}, u32[]{:S(2)}, u32[]{:S(2)}) collective-permute-start(bf16[64,2048]{1,0:T(8,128)(2,1)} %bitcast.5), channel_id=1, source_target_pairs={{0,4},{4,0},{8,12},{12,8},{16,20},{20,16},{24,28},{28,24},{32,36},... | collective-permute-start | bytes 786440 | tf_op jit(solution)/shard_map/ppermute | solution.py:239
  3.2 23.0 %copy-start = (bf16[4096,2048]{1,0:T(8,128)(2,1)S(1)}, bf16[4096,2048]{1,0:T(8,128)(2,1)}, u32[]{:S(2)}) copy-start(bf16[4096,2048]{1,0:T(8,128)(2,1)} %f_4_.1) | copy-start | bytes 50331652
  3.3 6.4 %collective-permute-start.1 = (bf16[64,512]{1,0:T(8,128)(2,1)S(1)}, bf16[64,512]{1,0:T(8,128)(2,1)S(1)}, u32[]{:S(2)}, u32[]{:S(2)}) collective-permute-start(bf16[64,512]{1,0:T(8,128)(2,1)S(1)} %get-tuple-element.38), channel_id=1, source_target_pairs={{0,32},{4,36},{8,40},{12,44},{16,48},{20,52},{24,56},{28,60},{32,6... | collective-permute-start | bytes 196616 | tf_op jit(solution)/shard_map/ppermute | solution.py:239
  4.7 7.6 %collective-permute-start.2 = (bf16[64,512]{1,0:T(8,128)(2,1)S(1)}, bf16[64,512]{1,0:T(8,128)(2,1)S(1)}, u32[]{:S(2)}, u32[]{:S(2)}) collective-permute-start(bf16[64,512]{1,0:T(8,128)(2,1)S(1)} %get-tuple-element.39), channel_id=1, source_target_pairs={{0,64},{4,68},{8,72},{12,76},{16,80},{20,84},{24,88},{28,92},{32,9... | collective-permute-start | bytes 196616 | tf_op jit(solution)/shard_map/ppermute | solution.py:239
  7.1 6.2 %collective-permute-start.3 = (bf16[64,512]{1,0:T(8,128)(2,1)S(1)}, bf16[64,512]{1,0:T(8,128)(2,1)S(1)}, u32[]{:S(2)}, u32[]{:S(2)}) collective-permute-start(bf16[64,512]{1,0:T(8,128)(2,1)S(1)} %get-tuple-element.40), channel_id=1, source_target_pairs={{0,96},{4,100},{8,104},{12,108},{16,112},{20,116},{24,120},{28,124... | collective-permute-start | bytes 196616 | tf_op jit(solution)/shard_map/ppermute | solution.py:239
  8.3 5.4 %collective-permute-start.8 = (bf16[64,512]{1,0:T(8,128)(2,1)S(1)}, bf16[64,512]{1,0:T(8,128)(2,1)S(1)}, u32[]{:S(2)}, u32[]{:S(2)}) collective-permute-start(bf16[64,512]{1,0:T(8,128)(2,1)S(1)} %get-tuple-element.46), channel_id=1, source_target_pairs={{0,8},{4,12},{8,16},{12,20},{16,24},{20,28},{24,0},{28,4},{32,40},... | collective-permute-start | bytes 196616 | tf_op jit(solution)/shard_map/ppermute | solution.py:239
  9.7 6.6 %collective-permute-start.9 = (bf16[64,512]{1,0:T(8,128)(2,1)S(1)}, bf16[64,512]{1,0:T(8,128)(2,1)S(1)}, u32[]{:S(2)}, u32[]{:S(2)}) collective-permute-start(bf16[64,512]{1,0:T(8,128)(2,1)S(1)} %get-tuple-element.47), channel_id=1, source_target_pairs={{0,16},{4,20},{8,24},{12,28},{16,0},{20,4},{24,8},{28,12},{32,48},... | collective-permute-start | bytes 196616 | tf_op jit(solution)/shard_map/ppermute | solution.py:239
  12.3 4.0 %collective-permute-start.10 = (bf16[64,512]{1,0:T(8,128)(2,1)S(1)}, bf16[64,512]{1,0:T(8,128)(2,1)S(1)}, u32[]{:S(2)}, u32[]{:S(2)}) collective-permute-start(bf16[64,512]{1,0:T(8,128)(2,1)S(1)} %get-tuple-element.48), channel_id=1, source_target_pairs={{0,24},{4,28},{8,0},{12,4},{16,8},{20,12},{24,16},{28,20},{32,56},... | collective-permute-start | bytes 196616 | tf_op jit(solution)/shard_map/ppermute | solution.py:239
  13.4 5.6 %collective-permute-start.5 = (bf16[64,512]{1,0:T(8,128)(2,1)S(1)}, bf16[64,512]{1,0:T(8,128)(2,1)S(1)}, u32[]{:S(2)}, u32[]{:S(2)}) collective-permute-start(bf16[64,512]{1,0:T(8,128)(2,1)S(1)} %get-tuple-element.42), channel_id=1, source_target_pairs={{0,16},{4,20},{8,24},{12,28},{16,0},{20,4},{24,8},{28,12},{32,48},... | collective-permute-start | bytes 196616 | tf_op jit(solution)/shard_map/ppermute | solution.py:239
  13.7 7.7 %collective-permute-start.6 = (bf16[64,512]{1,0:T(8,128)(2,1)S(1)}, bf16[64,512]{1,0:T(8,128)(2,1)S(1)}, u32[]{:S(2)}, u32[]{:S(2)}) collective-permute-start(bf16[64,512]{1,0:T(8,128)(2,1)S(1)} %get-tuple-element.43), channel_id=1, source_target_pairs={{0,24},{4,28},{8,0},{12,4},{16,8},{20,12},{24,16},{28,20},{32,56},... | collective-permute-start | bytes 196616 | tf_op jit(solution)/shard_map/ppermute | solution.py:239
  16.3 5.1 %collective-permute-start.4 = (bf16[64,512]{1,0:T(8,128)(2,1)S(1)}, bf16[64,512]{1,0:T(8,128)(2,1)S(1)}, u32[]{:S(2)}, u32[]{:S(2)}) collective-permute-start(bf16[64,512]{1,0:T(8,128)(2,1)S(1)} %get-tuple-element.41.r), channel_id=1, source_target_pairs={{0,8},{4,12},{8,16},{12,20},{16,24},{20,28},{24,0},{28,4},{32,40},... | collective-permute-start | bytes 196616 | tf_op jit(solution)/shard_map/ppermute | solution.py:239
  16.3 5.2 %collective-permute-start.11 = (bf16[64,512]{1,0:T(8,128)(2,1)S(1)}, bf16[64,512]{1,0:T(8,128)(2,1)S(1)}, u32[]{:S(2)}, u32[]{:S(2)}) collective-permute-start(bf16[64,512]{1,0:T(8,128)(2,1)S(1)} %collective-permute-done.8.b1), channel_id=1, source_target_pairs={{0,4},{4,0},{8,12},{12,8},{16,20},{20,16},{24,28},{28,24},{32,36},... | collective-permute-start | bytes 196616 | tf_op jit(solution)/shard_map/ppermute | solution.py:239
  19.0 3.3 %collective-permute-start.12 = (bf16[64,512]{1,0:T(8,128)(2,1)S(1)}, bf16[64,512]{1,0:T(8,128)(2,1)S(1)}, u32[]{:S(2)}, u32[]{:S(2)}) collective-permute-start(bf16[64,512]{1,0:T(8,128)(2,1)S(1)} %collective-permute-done.9.b2), channel_id=1, source_target_pairs={{0,4},{4,0},{8,12},{12,8},{16,20},{20,16},{24,28},{28,24},{32,36},... | collective-permute-start | bytes 196616 | tf_op jit(solution)/shard_map/ppermute | solution.py:239
  21.4 1.3 %collective-permute-start.13 = (bf16[64,512]{1,0:T(8,128)(2,1)S(1)}, bf16[64,512]{1,0:T(8,128)(2,1)S(1)}, u32[]{:S(2)}, u32[]{:S(2)}) collective-permute-start(bf16[64,512]{1,0:T(8,128)(2,1)S(1)} %collective-permute-done.10.b3), channel_id=1, source_target_pairs={{0,4},{4,0},{8,12},{12,8},{16,20},{20,16},{24,28},{28,24},{32,36},... | collective-permute-start | bytes 196616 | tf_op jit(solution)/shard_map/ppermute | solution.py:239
  23.0 6.7 %collective-permute-start.14 = (f32[64,512]{1,0:T(8,128)S(1)}, f32[64,512]{1,0:T(8,128)S(1)}, u32[]{:S(2)}, u32[]{:S(2)}) collective-permute-start(f32[64,512]{1,0:T(8,128)S(1)} %get-tuple-element.50), channel_id=1, source_target_pairs={{0,32},{4,36},{8,40},{12,44},{16,48},{20,52},{24,56},{28,60},{32,6... | collective-permute-start | bytes 393224 | tf_op jit(solution)/shard_map/ppermute | solution.py:239
  23.4 6.4 %collective-permute-start.15 = (f32[64,512]{1,0:T(8,128)S(1)}, f32[64,512]{1,0:T(8,128)S(1)}, u32[]{:S(2)}, u32[]{:S(2)}) collective-permute-start(f32[64,512]{1,0:T(8,128)S(1)} %get-tuple-element.51), channel_id=1, source_target_pairs={{0,64},{4,68},{8,72},{12,76},{16,80},{20,84},{24,88},{28,92},{32,9... | collective-permute-start | bytes 393224 | tf_op jit(solution)/shard_map/ppermute | solution.py:239
  24.7 5.8 %collective-permute-start.16 = (f32[64,512]{1,0:T(8,128)S(1)}, f32[64,512]{1,0:T(8,128)S(1)}, u32[]{:S(2)}, u32[]{:S(2)}) collective-permute-start(f32[64,512]{1,0:T(8,128)S(1)} %get-tuple-element.52), channel_id=1, source_target_pairs={{0,96},{4,100},{8,104},{12,108},{16,112},{20,116},{24,120},{28,124... | collective-permute-start | bytes 393224 | tf_op jit(solution)/shard_map/ppermute | solution.py:239
  30.6 4.0 %collective-permute-start.17 = (bf16[64,512]{1,0:T(8,128)(2,1)S(1)}, bf16[64,512]{1,0:T(8,128)(2,1)S(1)}, u32[]{:S(2)}, u32[]{:S(2)}) collective-permute-start(bf16[64,512]{1,0:T(8,128)(2,1)S(1)} %round_sum.1.h), channel_id=1, source_target_pairs={{0,4},{4,0},{8,12},{12,8},{16,20},{20,16},{24,28},{28,24},{32,36},... | collective-permute-start | bytes 196616 | tf_op jit(solution)/shard_map/ppermute | solution.py:239
  34.7 6.0 %collective-permute-start.19 = (bf16[128,512]{1,0:T(8,128)(2,1)S(1)}, bf16[128,512]{1,0:T(8,128)(2,1)S(1)}, u32[]{:S(2)}, u32[]{:S(2)}) collective-permute-start(bf16[128,512]{1,0:T(8,128)(2,1)S(1)} %get-tuple-element.54.j.f_1_), channel_id=1, source_target_pairs={{0,8},{4,12},{8,16},{12,20},{16,24},{20,28},{24,0},{28,4},{32,40},... | collective-permute-start | bytes 393224 | tf_op jit(solution)/shard_map/ppermute | solution.py:239
  35.0 7.0 %collective-permute-start.20 = (bf16[128,512]{1,0:T(8,128)(2,1)S(1)}, bf16[128,512]{1,0:T(8,128)(2,1)S(1)}, u32[]{:S(2)}, u32[]{:S(2)}) collective-permute-start(bf16[128,512]{1,0:T(8,128)(2,1)S(1)} %get-tuple-element.55), channel_id=1, source_target_pairs={{0,24},{4,28},{8,0},{12,4},{16,8},{20,12},{24,16},{28,20},{32,56},... | collective-permute-start | bytes 393224 | tf_op jit(solution)/shard_map/ppermute | solution.py:239
  37.4 6.9 %collective-permute-start.18 = (bf16[128,512]{1,0:T(8,128)(2,1)S(1)}, bf16[128,512]{1,0:T(8,128)(2,1)S(1)}, u32[]{:S(2)}, u32[]{:S(2)}) collective-permute-start(bf16[128,512]{1,0:T(8,128)(2,1)S(1)} %get-tuple-element.53), channel_id=1, source_target_pairs={{0,16},{4,20},{8,24},{12,28},{16,0},{20,4},{24,8},{28,12},{32,48},... | collective-permute-start | bytes 393224 | tf_op jit(solution)/shard_map/ppermute | solution.py:239
  45.7 10.0 %collective-permute-start.21 = (bf16[32,4352]{1,0:T(8,128)(2,1)S(1)}, bf16[32,4352]{1,0:T(8,128)(2,1)S(1)}, u32[]{:S(2)}, u32[]{:S(2)}) collective-permute-start(bf16[32,4352]{1,0:T(8,128)(2,1)S(1)} %get-tuple-element.59), channel_id=1, source_target_pairs={{0,1},{1,2},{2,3},{3,0},{4,6},{5,7},{6,4},{7,5},{8,9},{9,10},{10,1... | collective-permute-start | bytes 835592 | tf_op jit(solution)/shard_map/ppermute | solution.py:247
  49.4 12.1 %collective-permute-start.22 = (bf16[32,4352]{1,0:T(8,128)(2,1)S(1)}, bf16[32,4352]{1,0:T(8,128)(2,1)S(1)}, u32[]{:S(2)}, u32[]{:S(2)}) collective-permute-start(bf16[32,4352]{1,0:T(8,128)(2,1)S(1)} %get-tuple-element.60), channel_id=1, source_target_pairs={{0,3},{1,0},{2,1},{3,2},{4,5},{5,6},{6,7},{7,4},{8,11},{9,8},{10,9... | collective-permute-start | bytes 835592 | tf_op jit(solution)/shard_map/ppermute | solution.py:247
  50.1 12.6 %collective-permute-start.23 = (bf16[32,4352]{1,0:T(8,128)(2,1)S(1)}, bf16[32,4352]{1,0:T(8,128)(2,1)S(1)}, u32[]{:S(2)}, u32[]{:S(2)}) collective-permute-start(bf16[32,4352]{1,0:T(8,128)(2,1)S(1)} %get-tuple-element.64), channel_id=1, source_target_pairs={{0,2},{1,3},{2,0},{3,1},{4,7},{5,4},{6,5},{7,6},{8,10},{9,11},{10,... | collective-permute-start | bytes 835592 | tf_op jit(solution)/shard_map/ppermute | solution.py:247

commit v6 on v5

--- a/solution.py
+++ b/solution.py
@@ -61,7 +61,7 @@
     yback = lax.rem(y - (o // 2) % 4 + 4, 4)
     tests = [o % 2 == c, o % 2 != c] + [xback == d for d in range(4)] + [yback == d for d in range(4)]
     for i, test in enumerate(tests):
-        w[i, :, :] = jnp.full((16, 128), jnp.where(test, 1.0, 0.0), F32).astype(BF16)
+        w[i, :, :] = jnp.full((64, 128), jnp.where(test, 1.0, 0.0), F32).astype(BF16)
     copies[1].wait()
     copies[2].wait()
 
@@ -69,7 +69,7 @@
 def weigh(w, first, refs, columns):
     total = None
     for d, ref in enumerate(refs):
-        term = ref(columns) * w[first + d, 0:1, :]
+        term = ref(columns) * w[first + d, :, :]
         total = term if total is None else total + term
     return total
 
@@ -261,7 +261,7 @@
     po = send(p, dc=1)
     piece = shape((64, 512))
     w, qc, pv = call(
-        fetch, "fetch", (owners, q, p), [shape((10, 16, 128)), shape((64, 2048)), shape((64, 2048))],
+        fetch, "fetch", (owners, q, p), [shape((10, 64, 128)), shape((64, 2048)), shape((64, 2048))],
         spaces={0: HBM, 1: HBM, 2: HBM}, scratch=[pltpu.SMEM((2,), jnp.int32), pltpu.SemaphoreType.DMA((3,))],
     )
     a0, a1, a2, a3 = call(slices, "slices", (w, qc, qo, store), [piece] * 4, spaces={3: HBM})

time: 63.9 us -> 63.9 us (level)
  no operation moved by 1% of the time
where the time goes in v6:
time: 63.9 us; the launch traced here: 63.8 us
  starting transfers between devices  35.6 us (56%)
  waiting for transfers between devices  16.3 us (26%)
  Pallas kernels  11.6 us (18%)
    ppermute x21, starting transfers between devices, send(): return lax.ppermute(a, 'ex', moved(dx, dy, dc))  29.3 us
    pallas_call x15, Pallas kernels, call(): pl.pallas_call(body, name=name, in_specs=[pl.BlockSpec(memory_space=space...  10.6 us
    ppermute x3, waiting for transfers between devices, send_layer(): return lax.ppermute(a, ('ex', 'layer'), pairs)  10.4 us
    ppermute x3, starting transfers between devices, send_layer(): return lax.ppermute(a, ('ex', 'layer'), pairs)  6.32 us
    ppermute x21, waiting for transfers between devices, send(): return lax.ppermute(a, 'ex', moved(dx, dy, dc))  5.91 us
  transfers between devices with their start and end apart: 24, of which 12 were waited for; matrix products, arithmetic and copies ran while one was open for 0% of the time, Pallas kernels for 14%

profile of v6, /device:TPU:1, one launch (start us, length us, event | category | flops | bytes accessed | tf_op | source)
XLA Modules:
  0.0 63.8 jit_solution(14475293896258497445)
XLA Ops:
  0.0 1.4 %collective-permute-start = (bf16[128,2048]{1,0:T(8,128)(2,1)}, bf16[128,2048]{1,0:T(8,128)(2,1)S(1)}, u32[]{:S(2)}, u32[]{:S(2)}) collective-permute-start(bf16[128,2048]{1,0:T(8,128)(2,1)} %bitcast.3), channel_id=1, source_target_pairs={{0,4},{4,0},{8,12},{12,8},{16,20},{20,16},{24,28},{28,24},{32,36},... | collective-permute-start | bytes 1572872 | tf_op jit(solution)/shard_map/ppermute | solution.py:239
  1.4 0.0 collective-permute-start.7
  1.4 1.1 %fetch.1 = (bf16[10,64,128]{2,1,0:T(8,128)(2,1)S(1)}, bf16[64,2048]{1,0:T(8,128)(2,1)S(1)}, bf16[64,2048]{1,0:T(8,128)(2,1)S(1)}) custom-call(s32[2]{0:T(128)} %owners.1, bf16[128,2048]{1,0:T(8,128)(2,1)} %bitcast.4, bf16[64,2048]{1,0:T(8,128)(2,1)} %bitcast.6), custom_call_target="tpu_custom_call" | custom-call | bytes 1048576 | tf_op jit(solution)/shard_map/fetch/pallas_call | solution.py:36
  2.5 0.7 %collective-permute-done.qo = bf16[128,2048]{1,0:T(8,128)(2,1)S(1)} collective-permute-done((bf16[128,2048]{1,0:T(8,128)(2,1)}, bf16[128,2048]{1,0:T(8,128)(2,1)S(1)}, u32[]{:S(2)}, u32[]{:S(2)}) %collective-permute-start) | collective-permute-done | bytes 524320 | tf_op jit(solution)/shard_map/ppermute | solution.py:239
  3.2 0.0 copy-start
  3.2 0.1 slices.1
  3.3 1.4 %collective-permute-start.1 = (bf16[64,512]{1,0:T(8,128)(2,1)S(1)}, bf16[64,512]{1,0:T(8,128)(2,1)S(1)}, u32[]{:S(2)}, u32[]{:S(2)}) collective-permute-start(bf16[64,512]{1,0:T(8,128)(2,1)S(1)} %get-tuple-element.38), channel_id=1, source_target_pairs={{0,32},{4,36},{8,40},{12,44},{16,48},{20,52},{24,56},{28,60},{32,6... | collective-permute-start | bytes 196616 | tf_op jit(solution)/shard_map/ppermute | solution.py:239
  4.7 2.5 %collective-permute-start.2 = (bf16[64,512]{1,0:T(8,128)(2,1)S(1)}, bf16[64,512]{1,0:T(8,128)(2,1)S(1)}, u32[]{:S(2)}, u32[]{:S(2)}) collective-permute-start(bf16[64,512]{1,0:T(8,128)(2,1)S(1)} %get-tuple-element.39), channel_id=1, source_target_pairs={{0,64},{4,68},{8,72},{12,76},{16,80},{20,84},{24,88},{28,92},{32,9... | collective-permute-start | bytes 196616 | tf_op jit(solution)/shard_map/ppermute | solution.py:239
  7.1 1.2 %collective-permute-start.3 = (bf16[64,512]{1,0:T(8,128)(2,1)S(1)}, bf16[64,512]{1,0:T(8,128)(2,1)S(1)}, u32[]{:S(2)}, u32[]{:S(2)}) collective-permute-start(bf16[64,512]{1,0:T(8,128)(2,1)S(1)} %get-tuple-element.40), channel_id=1, source_target_pairs={{0,96},{4,100},{8,104},{12,108},{16,112},{20,116},{24,120},{28,124... | collective-permute-start | bytes 196616 | tf_op jit(solution)/shard_map/ppermute | solution.py:239
  8.3 1.4 %collective-permute-start.8 = (bf16[64,512]{1,0:T(8,128)(2,1)S(1)}, bf16[64,512]{1,0:T(8,128)(2,1)S(1)}, u32[]{:S(2)}, u32[]{:S(2)}) collective-permute-start(bf16[64,512]{1,0:T(8,128)(2,1)S(1)} %get-tuple-element.46), channel_id=1, source_target_pairs={{0,8},{4,12},{8,16},{12,20},{16,24},{20,28},{24,0},{28,4},{32,40},... | collective-permute-start | bytes 196616 | tf_op jit(solution)/shard_map/ppermute | solution.py:239
  9.7 0.0 collective-permute-done.1.a1
  9.7 2.6 %collective-permute-start.9 = (bf16[64,512]{1,0:T(8,128)(2,1)S(1)}, bf16[64,512]{1,0:T(8,128)(2,1)S(1)}, u32[]{:S(2)}, u32[]{:S(2)}) collective-permute-start(bf16[64,512]{1,0:T(8,128)(2,1)S(1)} %get-tuple-element.47), channel_id=1, source_target_pairs={{0,16},{4,20},{8,24},{12,28},{16,0},{20,4},{24,8},{28,12},{32,48},... | collective-permute-start | bytes 196616 | tf_op jit(solution)/shard_map/ppermute | solution.py:239
  12.3 0.0 collective-permute-done.2.a2
  12.3 1.1 %collective-permute-start.10 = (bf16[64,512]{1,0:T(8,128)(2,1)S(1)}, bf16[64,512]{1,0:T(8,128)(2,1)S(1)}, u32[]{:S(2)}, u32[]{:S(2)}) collective-permute-start(bf16[64,512]{1,0:T(8,128)(2,1)S(1)} %get-tuple-element.48), channel_id=1, source_target_pairs={{0,24},{4,28},{8,0},{12,4},{16,8},{20,12},{24,16},{28,20},{32,56},... | collective-permute-start | bytes 196616 | tf_op jit(solution)/shard_map/ppermute | solution.py:239
  13.4 0.0 collective-permute-done.3.a3
  13.4 0.3 collective-permute-start.5
  13.7 0.0 collective-permute-done.8.b1
  13.7 2.6 %collective-permute-start.6 = (bf16[64,512]{1,0:T(8,128)(2,1)S(1)}, bf16[64,512]{1,0:T(8,128)(2,1)S(1)}, u32[]{:S(2)}, u32[]{:S(2)}) collective-permute-start(bf16[64,512]{1,0:T(8,128)(2,1)S(1)} %get-tuple-element.43), channel_id=1, source_target_pairs={{0,24},{4,28},{8,0},{12,4},{16,8},{20,12},{24,16},{28,20},{32,56},... | collective-permute-start | bytes 196616 | tf_op jit(solution)/shard_map/ppermute | solution.py:239
  16.3 0.0 collective-permute-done.9.b2
  16.3 0.0 collective-permute-start.4
  16.3 0.0 collective-permute-done.10.b3
  16.3 2.7 %collective-permute-start.11 = (bf16[64,512]{1,0:T(8,128)(2,1)S(1)}, bf16[64,512]{1,0:T(8,128)(2,1)S(1)}, u32[]{:S(2)}, u32[]{:S(2)}) collective-permute-start(bf16[64,512]{1,0:T(8,128)(2,1)S(1)} %collective-permute-done.8.b1), channel_id=1, source_target_pairs={{0,4},{4,0},{8,12},{12,8},{16,20},{20,16},{24,28},{28,24},{32,36},... | collective-permute-start | bytes 196616 | tf_op jit(solution)/shard_map/ppermute | solution.py:239
  19.0 0.0 collective-permute-done.5.u2
  19.0 2.4 %collective-permute-start.12 = (bf16[64,512]{1,0:T(8,128)(2,1)S(1)}, bf16[64,512]{1,0:T(8,128)(2,1)S(1)}, u32[]{:S(2)}, u32[]{:S(2)}) collective-permute-start(bf16[64,512]{1,0:T(8,128)(2,1)S(1)} %collective-permute-done.9.b2), channel_id=1, source_target_pairs={{0,4},{4,0},{8,12},{12,8},{16,20},{20,16},{24,28},{28,24},{32,36},... | collective-permute-start | bytes 196616 | tf_op jit(solution)/shard_map/ppermute | solution.py:239
  21.4 0.0 collective-permute-done.6.u3
  21.4 0.0 collective-permute-start.13
  21.4 0.0 collective-permute-done.4.u1
  21.5 0.0 collective-permute-done.7.po
  21.5 0.0 collective-permute-done.11.o1
  21.5 0.8 %collective-permute-done.12.o2 = bf16[64,512]{1,0:T(8,128)(2,1)S(1)} collective-permute-done((bf16[64,512]{1,0:T(8,128)(2,1)S(1)}, bf16[64,512]{1,0:T(8,128)(2,1)S(1)}, u32[]{:S(2)}, u32[]{:S(2)}) %collective-permute-start.12) | collective-permute-done | bytes 65568 | tf_op jit(solution)/shard_map/ppermute | solution.py:239
  22.3 0.4 collective-permute-done.13.o3
  22.7 0.3 product.1
  23.0 0.4 collective-permute-start.14
  23.4 1.4 %collective-permute-start.15 = (f32[64,512]{1,0:T(8,128)S(1)}, f32[64,512]{1,0:T(8,128)S(1)}, u32[]{:S(2)}, u32[]{:S(2)}) collective-permute-start(f32[64,512]{1,0:T(8,128)S(1)} %get-tuple-element.51), channel_id=1, source_target_pairs={{0,64},{4,68},{8,72},{12,76},{16,80},{20,84},{24,88},{28,92},{32,9... | collective-permute-start | bytes 393224 | tf_op jit(solution)/shard_map/ppermute | solution.py:239
  24.7 1.4 %collective-permute-start.16 = (f32[64,512]{1,0:T(8,128)S(1)}, f32[64,512]{1,0:T(8,128)S(1)}, u32[]{:S(2)}, u32[]{:S(2)}) collective-permute-start(f32[64,512]{1,0:T(8,128)S(1)} %get-tuple-element.52), channel_id=1, source_target_pairs={{0,96},{4,100},{8,104},{12,108},{16,112},{20,116},{24,120},{28,124... | collective-permute-start | bytes 393224 | tf_op jit(solution)/shard_map/ppermute | solution.py:239
  26.2 0.0 copy-done
  26.2 1.7 %norms1.1.__.f_7_ = f32[16,128]{1,0:T(8,128)S(1)} custom-call(bf16[4096,2048]{1,0:T(8,128)(2,1)S(1)} %copy-done, f32[64,512]{1,0:T(8,128)S(1)} %get-tuple-element.49.refs_1_.s0), custom_call_target="tpu_custom_call" | custom-call | flops 12582912 | bytes 8388608 | tf_op jit(solution)/shard_map/norms1/pallas_call | solution.py:36
  27.9 1.7 %norms0.1._.f_6_ = f32[16,128]{1,0:T(8,128)S(1)} custom-call(bf16[4096,2048]{1,0:T(8,128)(2,1)S(1)} %copy-done, f32[64,512]{1,0:T(8,128)S(1)} %get-tuple-element.49.refs_1_.s0), custom_call_target="tpu_custom_call" | custom-call | flops 12582912 | bytes 8388608 | tf_op jit(solution)/shard_map/norms0/pallas_call | solution.py:36
  29.6 0.1 collective-permute-done.14.s1
  29.7 0.1 collective-permute-done.15.s2
  29.7 0.8 %collective-permute-done.16.s3 = f32[64,512]{1,0:T(8,128)S(1)} collective-permute-done((f32[64,512]{1,0:T(8,128)S(1)}, f32[64,512]{1,0:T(8,128)S(1)}, u32[]{:S(2)}, u32[]{:S(2)}) %collective-permute-start.16) | collective-permute-done | bytes 131104 | tf_op jit(solution)/shard_map/ppermute | solution.py:239
  30.6 3.1 %collective-permute-start.17 = (bf16[64,512]{1,0:T(8,128)(2,1)S(1)}, bf16[64,512]{1,0:T(8,128)(2,1)S(1)}, u32[]{:S(2)}, u32[]{:S(2)}) collective-permute-start(bf16[64,512]{1,0:T(8,128)(2,1)S(1)} %round_sum.1.h), channel_id=1, source_target_pairs={{0,4},{4,0},{8,12},{12,8},{16,20},{20,16},{24,28},{28,24},{32,36},... | collective-permute-start | bytes 196616 | tf_op jit(solution)/shard_map/ppermute | solution.py:239
  33.7 0.9 %collective-permute-done.17.o = bf16[64,512]{1,0:T(8,128)(2,1)S(1)} collective-permute-done((bf16[64,512]{1,0:T(8,128)(2,1)S(1)}, bf16[64,512]{1,0:T(8,128)(2,1)S(1)}, u32[]{:S(2)}, u32[]{:S(2)}) %collective-permute-start.17) | collective-permute-done | bytes 65568 | tf_op jit(solution)/shard_map/ppermute | solution.py:239
  34.7 0.4 collective-permute-start.19
  35.0 2.4 %collective-permute-start.20 = (bf16[128,512]{1,0:T(8,128)(2,1)S(1)}, bf16[128,512]{1,0:T(8,128)(2,1)S(1)}, u32[]{:S(2)}, u32[]{:S(2)}) collective-permute-start(bf16[128,512]{1,0:T(8,128)(2,1)S(1)} %get-tuple-element.55), channel_id=1, source_target_pairs={{0,24},{4,28},{8,0},{12,4},{16,8},{20,12},{24,16},{28,20},{32,56},... | collective-permute-start | bytes 393224 | tf_op jit(solution)/shard_map/ppermute | solution.py:239
  37.4 0.8 %collective-permute-start.18 = (bf16[128,512]{1,0:T(8,128)(2,1)S(1)}, bf16[128,512]{1,0:T(8,128)(2,1)S(1)}, u32[]{:S(2)}, u32[]{:S(2)}) collective-permute-start(bf16[128,512]{1,0:T(8,128)(2,1)S(1)} %get-tuple-element.53), channel_id=1, source_target_pairs={{0,16},{4,20},{8,24},{12,28},{16,0},{20,4},{24,8},{28,12},{32,48},... | collective-permute-start | bytes 393224 | tf_op jit(solution)/shard_map/ppermute | solution.py:239
  38.2 1.2 %dots_first.1.f_2_ = f32[4096,128]{1,0:T(8,128)S(1)} custom-call(bf16[128,512]{1,0:T(8,128)(2,1)S(1)} %get-tuple-element.54.j.f_1_, bf16[4096,2048]{1,0:T(8,128)(2,1)S(1)} %copy-done), custom_call_target="tpu_custom_call" | custom-call | flops 536870912 | bytes 1048576 | tf_op jit(solution)/shard_map/dots_first/pallas_call | solution.py:36
  39.5 1.2 %collective-permute-done.19.f_0_.f_2_ = bf16[128,512]{1,0:T(8,128)(2,1)S(1)} collective-permute-done((bf16[128,512]{1,0:T(8,128)(2,1)S(1)}, bf16[128,512]{1,0:T(8,128)(2,1)S(1)}, u32[]{:S(2)}, u32[]{:S(2)}) %collective-permute-start.19) | collective-permute-done | bytes 131104 | tf_op jit(solution)/shard_map/ppermute | solution.py:239
  40.7 1.4 %dots_next1.1.f_2_ = f32[4096,128]{1,0:T(8,128)S(1)} custom-call(bf16[128,512]{1,0:T(8,128)(2,1)S(1)} %collective-permute-done.19.f_0_.f_2_, bf16[4096,2048]{1,0:T(8,128)(2,1)S(1)} %copy-done, f32[4096,128]{1,0:T(8,128)S(1)} %dots_first.1.f_2_), custom_call_target="tpu_custom_call", output_to_operand_aliasing={{}: (2, {})} | custom-call | flops 536870912 | bytes 1048576 | tf_op jit(solution)/shard_map/dots_next1/pallas_call | solution.py:36
  42.0 0.0 collective-permute-done.20.f_0_.f_3_
  42.0 1.4 %dots_next3.1.f_5_ = f32[4096,128]{1,0:T(8,128)S(1)} custom-call(bf16[128,512]{1,0:T(8,128)(2,1)S(1)} %collective-permute-done.20.f_0_.f_3_, bf16[4096,2048]{1,0:T(8,128)(2,1)S(1)} %copy-done, f32[4096,128]{1,0:T(8,128)S(1)} %dots_next1.1.f_2_), custom_call_target="tpu_custom_call", output_to_operand_aliasing={{}: (2, {})} | custom-call | flops 536870912 | bytes 1048576 | tf_op jit(solution)/shard_map/dots_next3/pallas_call | solution.py:36
  43.4 0.9 %collective-permute-done.18.f_0_ = bf16[128,512]{1,0:T(8,128)(2,1)S(1)} collective-permute-done((bf16[128,512]{1,0:T(8,128)(2,1)S(1)}, bf16[128,512]{1,0:T(8,128)(2,1)S(1)}, u32[]{:S(2)}, u32[]{:S(2)}) %collective-permute-start.18) | collective-permute-done | bytes 131104 | tf_op jit(solution)/shard_map/ppermute | solution.py:239
  44.3 1.4 %dots_last.1 = (f32[32,4096]{1,0:T(8,128)S(1)}, f32[32,128]{1,0:T(8,128)S(1)}, f32[32,128]{1,0:T(8,128)S(1)}, bf16[32,4352]{1,0:T(8,128)(2,1)S(1)}, bf16[32,4352...) custom-call(bf16[128,512]{1,0:T(8,128)(2,1)S(1)} %collective-permute-done.18.f_0_, ...), custom_call_target="tpu_custom_call" | custom-call | flops 536870912 | bytes 1048576 | tf_op jit(solution)/shard_map/dots_last/pallas_call | solution.py:36
  45.7 3.6 %collective-permute-start.21 = (bf16[32,4352]{1,0:T(8,128)(2,1)S(1)}, bf16[32,4352]{1,0:T(8,128)(2,1)S(1)}, u32[]{:S(2)}, u32[]{:S(2)}) collective-permute-start(bf16[32,4352]{1,0:T(8,128)(2,1)S(1)} %get-tuple-element.59), channel_id=1, source_target_pairs={{0,1},{1,2},{2,3},{3,0},{4,6},{5,7},{6,4},{7,5},{8,9},{9,10},{10,1... | collective-permute-start | bytes 835592 | tf_op jit(solution)/shard_map/ppermute | solution.py:247
  49.3 0.7 %collective-permute-start.22 = (bf16[32,4352]{1,0:T(8,128)(2,1)S(1)}, bf16[32,4352]{1,0:T(8,128)(2,1)S(1)}, u32[]{:S(2)}, u32[]{:S(2)}) collective-permute-start(bf16[32,4352]{1,0:T(8,128)(2,1)S(1)} %get-tuple-element.60), channel_id=1, source_target_pairs={{0,3},{1,0},{2,1},{3,2},{4,5},{5,6},{6,7},{7,4},{8,11},{9,8},{10,9... | collective-permute-start | bytes 835592 | tf_op jit(solution)/shard_map/ppermute | solution.py:247
  50.1 1.9 %collective-permute-start.23 = (bf16[32,4352]{1,0:T(8,128)(2,1)S(1)}, bf16[32,4352]{1,0:T(8,128)(2,1)S(1)}, u32[]{:S(2)}, u32[]{:S(2)}) collective-permute-start(bf16[32,4352]{1,0:T(8,128)(2,1)S(1)} %get-tuple-element.64), channel_id=1, source_target_pairs={{0,2},{1,3},{2,0},{3,1},{4,7},{5,4},{6,5},{7,6},{8,10},{9,11},{10,... | collective-permute-start | bytes 835592 | tf_op jit(solution)/shard_map/ppermute | solution.py:247
  52.0 3.7 %collective-permute-done.21.z1 = bf16[32,4352]{1,0:T(8,128)(2,1)S(1)} collective-permute-done((bf16[32,4352]{1,0:T(8,128)(2,1)S(1)}, bf16[32,4352]{1,0:T(8,128)(2,1)S(1)}, u32[]{:S(2)}, u32[]{:S(2)}) %collective-permute-start.21) | collective-permute-done | bytes 278560 | tf_op jit(solution)/shard_map/ppermute | solution.py:247
  55.7 5.7 %collective-permute-done.22.z3 = bf16[32,4352]{1,0:T(8,128)(2,1)S(1)} collective-permute-done((bf16[32,4352]{1,0:T(8,128)(2,1)S(1)}, bf16[32,4352]{1,0:T(8,128)(2,1)S(1)}, u32[]{:S(2)}, u32[]{:S(2)}) %collective-permute-start.22) | collective-permute-done | bytes 278560 | tf_op jit(solution)/shard_map/ppermute | solution.py:247
  61.4 0.3 finish_first.1
  61.7 0.9 %collective-permute-done.23.z2 = bf16[32,4352]{1,0:T(8,128)(2,1)S(1)} collective-permute-done((bf16[32,4352]{1,0:T(8,128)(2,1)S(1)}, bf16[32,4352]{1,0:T(8,128)(2,1)S(1)}, u32[]{:S(2)}, u32[]{:S(2)}) %collective-permute-start.23) | collective-permute-done | bytes 278560 | tf_op jit(solution)/shard_map/ppermute | solution.py:247
  62.6 1.0 %finish_last.1 = f32[32,4096]{1,0:T(8,128)} custom-call(f32[32,4096]{1,0:T(8,128)S(1)} %get-tuple-element.61.t, f32[32,128]{1,0:T(8,128)S(1)} %get-tuple-element.62.g, f32[32,128]{1,0:T(8,128)S(1)} %get-tuple-element.63.q, bf16[32,4352]{1,0:T(8,128)(2,1)S(1)} %collective-permute-done.23.z2), custom_call_target="tpu_custom_call" | custom-call | tf_op jit(solution)/shard_map/finish_last/pallas_call | solution.py:302
  (5 shorter events, 0.2 us)
Async XLA Ops:
  0.0 3.2 %collective-permute-start = (bf16[128,2048]{1,0:T(8,128)(2,1)}, bf16[128,2048]{1,0:T(8,128)(2,1)S(1)}, u32[]{:S(2)}, u32[]{:S(2)}) collective-permute-start(bf16[128,2048]{1,0:T(8,128)(2,1)} %bitcast.3), channel_id=1, source_target_pairs={{0,4},{4,0},{8,12},{12,8},{16,20},{20,16},{24,28},{28,24},{32,36},... | collective-permute-start | bytes 1572872 | tf_op jit(solution)/shard_map/ppermute | solution.py:239
  1.4 20.1 %collective-permute-start.7 = (bf16[64,2048]{1,0:T(8,128)(2,1)}, bf16[64,2048]{1,0:T(8,128)(2,1)S(1)}, u32[]{:S(2)}, u32[]{:S(2)}) collective-permute-start(bf16[64,2048]{1,0:T(8,128)(2,1)} %bitcast.5), channel_id=1, source_target_pairs={{0,4},{4,0},{8,12},{12,8},{16,20},{20,16},{24,28},{28,24},{32,36},... | collective-permute-start | bytes 786440 | tf_op jit(solution)/shard_map/ppermute | solution.py:239
  3.2 23.0 %copy-start = (bf16[4096,2048]{1,0:T(8,128)(2,1)S(1)}, bf16[4096,2048]{1,0:T(8,128)(2,1)}, u32[]{:S(2)}) copy-start(bf16[4096,2048]{1,0:T(8,128)(2,1)} %f_4_.1) | copy-start | bytes 50331652
  3.3 6.4 %collective-permute-start.1 = (bf16[64,512]{1,0:T(8,128)(2,1)S(1)}, bf16[64,512]{1,0:T(8,128)(2,1)S(1)}, u32[]{:S(2)}, u32[]{:S(2)}) collective-permute-start(bf16[64,512]{1,0:T(8,128)(2,1)S(1)} %get-tuple-element.38), channel_id=1, source_target_pairs={{0,32},{4,36},{8,40},{12,44},{16,48},{20,52},{24,56},{28,60},{32,6... | collective-permute-start | bytes 196616 | tf_op jit(solution)/shard_map/ppermute | solution.py:239
  4.7 7.6 %collective-permute-start.2 = (bf16[64,512]{1,0:T(8,128)(2,1)S(1)}, bf16[64,512]{1,0:T(8,128)(2,1)S(1)}, u32[]{:S(2)}, u32[]{:S(2)}) collective-permute-start(bf16[64,512]{1,0:T(8,128)(2,1)S(1)} %get-tuple-element.39), channel_id=1, source_target_pairs={{0,64},{4,68},{8,72},{12,76},{16,80},{20,84},{24,88},{28,92},{32,9... | collective-permute-start | bytes 196616 | tf_op jit(solution)/shard_map/ppermute | solution.py:239
  7.1 6.2 %collective-permute-start.3 = (bf16[64,512]{1,0:T(8,128)(2,1)S(1)}, bf16[64,512]{1,0:T(8,128)(2,1)S(1)}, u32[]{:S(2)}, u32[]{:S(2)}) collective-permute-start(bf16[64,512]{1,0:T(8,128)(2,1)S(1)} %get-tuple-element.40), channel_id=1, source_target_pairs={{0,96},{4,100},{8,104},{12,108},{16,112},{20,116},{24,120},{28,124... | collective-permute-start | bytes 196616 | tf_op jit(solution)/shard_map/ppermute | solution.py:239
  8.3 5.4 %collective-permute-start.8 = (bf16[64,512]{1,0:T(8,128)(2,1)S(1)}, bf16[64,512]{1,0:T(8,128)(2,1)S(1)}, u32[]{:S(2)}, u32[]{:S(2)}) collective-permute-start(bf16[64,512]{1,0:T(8,128)(2,1)S(1)} %get-tuple-element.46), channel_id=1, source_target_pairs={{0,8},{4,12},{8,16},{12,20},{16,24},{20,28},{24,0},{28,4},{32,40},... | collective-permute-start | bytes 196616 | tf_op jit(solution)/shard_map/ppermute | solution.py:239
  9.7 6.6 %collective-permute-start.9 = (bf16[64,512]{1,0:T(8,128)(2,1)S(1)}, bf16[64,512]{1,0:T(8,128)(2,1)S(1)}, u32[]{:S(2)}, u32[]{:S(2)}) collective-permute-start(bf16[64,512]{1,0:T(8,128)(2,1)S(1)} %get-tuple-element.47), channel_id=1, source_target_pairs={{0,16},{4,20},{8,24},{12,28},{16,0},{20,4},{24,8},{28,12},{32,48},... | collective-permute-start | bytes 196616 | tf_op jit(solution)/shard_map/ppermute | solution.py:239
  12.3 4.0 %collective-permute-start.10 = (bf16[64,512]{1,0:T(8,128)(2,1)S(1)}, bf16[64,512]{1,0:T(8,128)(2,1)S(1)}, u32[]{:S(2)}, u32[]{:S(2)}) collective-permute-start(bf16[64,512]{1,0:T(8,128)(2,1)S(1)} %get-tuple-element.48), channel_id=1, source_target_pairs={{0,24},{4,28},{8,0},{12,4},{16,8},{20,12},{24,16},{28,20},{32,56},... | collective-permute-start | bytes 196616 | tf_op jit(solution)/shard_map/ppermute | solution.py:239
  13.4 5.6 %collective-permute-start.5 = (bf16[64,512]{1,0:T(8,128)(2,1)S(1)}, bf16[64,512]{1,0:T(8,128)(2,1)S(1)}, u32[]{:S(2)}, u32[]{:S(2)}) collective-permute-start(bf16[64,512]{1,0:T(8,128)(2,1)S(1)} %get-tuple-element.42), channel_id=1, source_target_pairs={{0,16},{4,20},{8,24},{12,28},{16,0},{20,4},{24,8},{28,12},{32,48},... | collective-permute-start | bytes 196616 | tf_op jit(solution)/shard_map/ppermute | solution.py:239
  13.7 7.7 %collective-permute-start.6 = (bf16[64,512]{1,0:T(8,128)(2,1)S(1)}, bf16[64,512]{1,0:T(8,128)(2,1)S(1)}, u32[]{:S(2)}, u32[]{:S(2)}) collective-permute-start(bf16[64,512]{1,0:T(8,128)(2,1)S(1)} %get-tuple-element.43), channel_id=1, source_target_pairs={{0,24},{4,28},{8,0},{12,4},{16,8},{20,12},{24,16},{28,20},{32,56},... | collective-permute-start | bytes 196616 | tf_op jit(solution)/shard_map/ppermute | solution.py:239
  16.3 5.1 %collective-permute-start.4 = (bf16[64,512]{1,0:T(8,128)(2,1)S(1)}, bf16[64,512]{1,0:T(8,128)(2,1)S(1)}, u32[]{:S(2)}, u32[]{:S(2)}) collective-permute-start(bf16[64,512]{1,0:T(8,128)(2,1)S(1)} %get-tuple-element.41.r), channel_id=1, source_target_pairs={{0,8},{4,12},{8,16},{12,20},{16,24},{20,28},{24,0},{28,4},{32,40},... | collective-permute-start | bytes 196616 | tf_op jit(solution)/shard_map/ppermute | solution.py:239
  16.3 5.2 %collective-permute-start.11 = (bf16[64,512]{1,0:T(8,128)(2,1)S(1)}, bf16[64,512]{1,0:T(8,128)(2,1)S(1)}, u32[]{:S(2)}, u32[]{:S(2)}) collective-permute-start(bf16[64,512]{1,0:T(8,128)(2,1)S(1)} %collective-permute-done.8.b1), channel_id=1, source_target_pairs={{0,4},{4,0},{8,12},{12,8},{16,20},{20,16},{24,28},{28,24},{32,36},... | collective-permute-start | bytes 196616 | tf_op jit(solution)/shard_map/ppermute | solution.py:239
  19.0 3.3 %collective-permute-start.12 = (bf16[64,512]{1,0:T(8,128)(2,1)S(1)}, bf16[64,512]{1,0:T(8,128)(2,1)S(1)}, u32[]{:S(2)}, u32[]{:S(2)}) collective-permute-start(bf16[64,512]{1,0:T(8,128)(2,1)S(1)} %collective-permute-done.9.b2), channel_id=1, source_target_pairs={{0,4},{4,0},{8,12},{12,8},{16,20},{20,16},{24,28},{28,24},{32,36},... | collective-permute-start | bytes 196616 | tf_op jit(solution)/shard_map/ppermute | solution.py:239
  21.4 1.3 %collective-permute-start.13 = (bf16[64,512]{1,0:T(8,128)(2,1)S(1)}, bf16[64,512]{1,0:T(8,128)(2,1)S(1)}, u32[]{:S(2)}, u32[]{:S(2)}) collective-permute-start(bf16[64,512]{1,0:T(8,128)(2,1)S(1)} %collective-permute-done.10.b3), channel_id=1, source_target_pairs={{0,4},{4,0},{8,12},{12,8},{16,20},{20,16},{24,28},{28,24},{32,36},... | collective-permute-start | bytes 196616 | tf_op jit(solution)/shard_map/ppermute | solution.py:239
  23.0 6.7 %collective-permute-start.14 = (f32[64,512]{1,0:T(8,128)S(1)}, f32[64,512]{1,0:T(8,128)S(1)}, u32[]{:S(2)}, u32[]{:S(2)}) collective-permute-start(f32[64,512]{1,0:T(8,128)S(1)} %get-tuple-element.50), channel_id=1, source_target_pairs={{0,32},{4,36},{8,40},{12,44},{16,48},{20,52},{24,56},{28,60},{32,6... | collective-permute-start | bytes 393224 | tf_op jit(solution)/shard_map/ppermute | solution.py:239
  23.4 6.4 %collective-permute-start.15 = (f32[64,512]{1,0:T(8,128)S(1)}, f32[64,512]{1,0:T(8,128)S(1)}, u32[]{:S(2)}, u32[]{:S(2)}) collective-permute-start(f32[64,512]{1,0:T(8,128)S(1)} %get-tuple-element.51), channel_id=1, source_target_pairs={{0,64},{4,68},{8,72},{12,76},{16,80},{20,84},{24,88},{28,92},{32,9... | collective-permute-start | bytes 393224 | tf_op jit(solution)/shard_map/ppermute | solution.py:239
  24.7 5.8 %collective-permute-start.16 = (f32[64,512]{1,0:T(8,128)S(1)}, f32[64,512]{1,0:T(8,128)S(1)}, u32[]{:S(2)}, u32[]{:S(2)}) collective-permute-start(f32[64,512]{1,0:T(8,128)S(1)} %get-tuple-element.52), channel_id=1, source_target_pairs={{0,96},{4,100},{8,104},{12,108},{16,112},{20,116},{24,120},{28,124... | collective-permute-start | bytes 393224 | tf_op jit(solution)/shard_map/ppermute | solution.py:239
  30.6 4.0 %collective-permute-start.17 = (bf16[64,512]{1,0:T(8,128)(2,1)S(1)}, bf16[64,512]{1,0:T(8,128)(2,1)S(1)}, u32[]{:S(2)}, u32[]{:S(2)}) collective-permute-start(bf16[64,512]{1,0:T(8,128)(2,1)S(1)} %round_sum.1.h), channel_id=1, source_target_pairs={{0,4},{4,0},{8,12},{12,8},{16,20},{20,16},{24,28},{28,24},{32,36},... | collective-permute-start | bytes 196616 | tf_op jit(solution)/shard_map/ppermute | solution.py:239
  34.7 6.0 %collective-permute-start.19 = (bf16[128,512]{1,0:T(8,128)(2,1)S(1)}, bf16[128,512]{1,0:T(8,128)(2,1)S(1)}, u32[]{:S(2)}, u32[]{:S(2)}) collective-permute-start(bf16[128,512]{1,0:T(8,128)(2,1)S(1)} %get-tuple-element.54.j.f_1_), channel_id=1, source_target_pairs={{0,8},{4,12},{8,16},{12,20},{16,24},{20,28},{24,0},{28,4},{32,40},... | collective-permute-start | bytes 393224 | tf_op jit(solution)/shard_map/ppermute | solution.py:239
  35.0 7.0 %collective-permute-start.20 = (bf16[128,512]{1,0:T(8,128)(2,1)S(1)}, bf16[128,512]{1,0:T(8,128)(2,1)S(1)}, u32[]{:S(2)}, u32[]{:S(2)}) collective-permute-start(bf16[128,512]{1,0:T(8,128)(2,1)S(1)} %get-tuple-element.55), channel_id=1, source_target_pairs={{0,24},{4,28},{8,0},{12,4},{16,8},{20,12},{24,16},{28,20},{32,56},... | collective-permute-start | bytes 393224 | tf_op jit(solution)/shard_map/ppermute | solution.py:239
  37.4 6.9 %collective-permute-start.18 = (bf16[128,512]{1,0:T(8,128)(2,1)S(1)}, bf16[128,512]{1,0:T(8,128)(2,1)S(1)}, u32[]{:S(2)}, u32[]{:S(2)}) collective-permute-start(bf16[128,512]{1,0:T(8,128)(2,1)S(1)} %get-tuple-element.53), channel_id=1, source_target_pairs={{0,16},{4,20},{8,24},{12,28},{16,0},{20,4},{24,8},{28,12},{32,48},... | collective-permute-start | bytes 393224 | tf_op jit(solution)/shard_map/ppermute | solution.py:239
  45.7 10.0 %collective-permute-start.21 = (bf16[32,4352]{1,0:T(8,128)(2,1)S(1)}, bf16[32,4352]{1,0:T(8,128)(2,1)S(1)}, u32[]{:S(2)}, u32[]{:S(2)}) collective-permute-start(bf16[32,4352]{1,0:T(8,128)(2,1)S(1)} %get-tuple-element.59), channel_id=1, source_target_pairs={{0,1},{1,2},{2,3},{3,0},{4,6},{5,7},{6,4},{7,5},{8,9},{9,10},{10,1... | collective-permute-start | bytes 835592 | tf_op jit(solution)/shard_map/ppermute | solution.py:247
  49.3 12.1 %collective-permute-start.22 = (bf16[32,4352]{1,0:T(8,128)(2,1)S(1)}, bf16[32,4352]{1,0:T(8,128)(2,1)S(1)}, u32[]{:S(2)}, u32[]{:S(2)}) collective-permute-start(bf16[32,4352]{1,0:T(8,128)(2,1)S(1)} %get-tuple-element.60), channel_id=1, source_target_pairs={{0,3},{1,0},{2,1},{3,2},{4,5},{5,6},{6,7},{7,4},{8,11},{9,8},{10,9... | collective-permute-start | bytes 835592 | tf_op jit(solution)/shard_map/ppermute | solution.py:247
  50.1 12.6 %collective-permute-start.23 = (bf16[32,4352]{1,0:T(8,128)(2,1)S(1)}, bf16[32,4352]{1,0:T(8,128)(2,1)S(1)}, u32[]{:S(2)}, u32[]{:S(2)}) collective-permute-start(bf16[32,4352]{1,0:T(8,128)(2,1)S(1)} %get-tuple-element.64), channel_id=1, source_target_pairs={{0,2},{1,3},{2,0},{3,1},{4,7},{5,4},{6,5},{7,6},{8,10},{9,11},{10,... | collective-permute-start | bytes 835592 | tf_op jit(solution)/shard_map/ppermute | solution.py:247

commit v7 on v6

--- a/solution.py
+++ b/solution.py
@@ -170,7 +170,21 @@
         acc[rows, :] = old[rows, :] + term(d, j, v, rows)
 
 
-def dots_last(d, j, j0, ja, jb, v, old, g0, g1, own, gn, qn, z1, z2, z3):
+def squares(pieces):
+    total = None
+    for piece in pieces:
+        for k in range(4):
+            t = piece[:, 128 * k:128 * k + 128].astype(F32)
+            total = t * t if total is None else total + t * t
+    return total
+
+
+def dots_third(d, j, j0, ja, v, old, acc, sq):
+    dots_next(d, j, v, old, acc)
+    sq[...] = squares((j, j0, ja))
+
+
+def dots_last(d, j, sq, v, old, g0, g1, own, gn, qn, z1, z2, z3):
     zs = ((1, z1), (2, z2), (3, z3))
     for i in range(PARTS):
         rows = slice(PART * i, PART * i + PART)
@@ -178,11 +192,7 @@
         own[:, rows] = out[0:32, :]
         for e, z in zs:
             z[:, rows] = out[32 * e:32 * e + 32, :].astype(BF16)
-    total = None
-    for piece in (j, j0, ja, jb):
-        for k in range(4):
-            t = piece[:, 128 * k:128 * k + 128].astype(F32)
-            total = t * t if total is None else total + t * t
+    total = sq[...] + squares((j,))
     qsum = jnp.broadcast_to(jnp.sum(total, axis=1, keepdims=True), (128, 128))
     qn[...] = qsum[0:32, :]
     for i, g in enumerate((g0, g1)):
@@ -288,13 +298,16 @@
     accs = [shape((4096, 128), F32)]
     work = 2 * 128 * 512 * 4096
     (acc,) = call(dots_first, "dots_first", (j, store), accs, flops=work)
-    for d, got in ((1, j1), (3, j3)):
-        (acc,) = call(
-            lambda *f, d=d: dots_next(d, *f), "dots_next%d" % d, (got, store, acc), accs, flops=work, alias={2: 0},
-        )
+    (acc,) = call(
+        lambda *f: dots_next(1, *f), "dots_next1", (j1, store, acc), accs, flops=work, alias={2: 0},
+    )
+    acc, sq = call(
+        lambda *f: dots_third(3, *f), "dots_next3", (j3, j, j1, store, acc), accs + [shape((128, 128), F32)],
+        flops=work, alias={4: 0},
+    )
     norm = shape((32, 128), F32)
     own, gn, qn, z1, z2, z3 = call(
-        lambda *f: dots_last(2, *f), "dots_last", (j2, j, j1, j3, store, acc, g0, g1),
+        lambda *f: dots_last(2, *f), "dots_last", (j2, sq, store, acc, g0, g1),
         [shape((32, 4096), F32), norm, norm] + [shape((32, 4352))] * 3, flops=work,
     )
     z1, z2, z3 = send_layer(z1, 0), send_layer(z2, 1), send_layer(z3, 2)

time: 63.9 us -> 63.9 us (level)
  no operation moved by 1% of the time
where the time goes in v7:
time: 63.9 us; the launch traced here: 63.8 us
  starting transfers between devices  35.6 us (56%)
  waiting for transfers between devices  16.2 us (25%)
  Pallas kernels  11.6 us (18%)
    ppermute x21, starting transfers between devices, send(): return lax.ppermute(a, 'ex', moved(dx, dy, dc))  29.3 us
    pallas_call x15, Pallas kernels, call(): pl.pallas_call(body, name=name, in_specs=[pl.BlockSpec(memory_space=space...  10.6 us
    ppermute x3, waiting for transfers between devices, send_layer(): return lax.ppermute(a, ('ex', 'layer'), pairs)  10.4 us
    ppermute x3, starting transfers between devices, send_layer(): return lax.ppermute(a, ('ex', 'layer'), pairs)  6.32 us
    ppermute x21, waiting for transfers between devices, send(): return lax.ppermute(a, 'ex', moved(dx, dy, dc))  5.88 us
  transfers between devices with their start and end apart: 24, of which 12 were waited for; matrix products, arithmetic and copies ran while one was open for 0% of the time, Pallas kernels for 14%

profile of v7, /device:TPU:1, one launch (start us, length us, event | category | flops | bytes accessed | tf_op | source)
XLA Modules:
  0.0 63.8 jit_solution(15274005475344538774)
XLA Ops:
  0.0 1.4 %collective-permute-start = (bf16[128,2048]{1,0:T(8,128)(2,1)}, bf16[128,2048]{1,0:T(8,128)(2,1)S(1)}, u32[]{:S(2)}, u32[]{:S(2)}) collective-permute-start(bf16[128,2048]{1,0:T(8,128)(2,1)} %bitcast.3), channel_id=1, source_target_pairs={{0,4},{4,0},{8,12},{12,8},{16,20},{20,16},{24,28},{28,24},{32,36},... | collective-permute-start | bytes 1572872 | tf_op jit(solution)/shard_map/ppermute | solution.py:249
  1.4 0.0 collective-permute-start.7
  1.4 1.1 %fetch.1 = (bf16[10,64,128]{2,1,0:T(8,128)(2,1)S(1)}, bf16[64,2048]{1,0:T(8,128)(2,1)S(1)}, bf16[64,2048]{1,0:T(8,128)(2,1)S(1)}) custom-call(s32[2]{0:T(128)} %owners.1, bf16[128,2048]{1,0:T(8,128)(2,1)} %bitcast.4, bf16[64,2048]{1,0:T(8,128)(2,1)} %bitcast.6), custom_call_target="tpu_custom_call" | custom-call | bytes 1048576 | tf_op jit(solution)/shard_map/fetch/pallas_call | solution.py:36
  2.5 0.7 %collective-permute-done.qo = bf16[128,2048]{1,0:T(8,128)(2,1)S(1)} collective-permute-done((bf16[128,2048]{1,0:T(8,128)(2,1)}, bf16[128,2048]{1,0:T(8,128)(2,1)S(1)}, u32[]{:S(2)}, u32[]{:S(2)}) %collective-permute-start) | collective-permute-done | bytes 524320 | tf_op jit(solution)/shard_map/ppermute | solution.py:249
  3.2 0.0 copy-start
  3.2 0.1 slices.1
  3.3 1.4 %collective-permute-start.1 = (bf16[64,512]{1,0:T(8,128)(2,1)S(1)}, bf16[64,512]{1,0:T(8,128)(2,1)S(1)}, u32[]{:S(2)}, u32[]{:S(2)}) collective-permute-start(bf16[64,512]{1,0:T(8,128)(2,1)S(1)} %get-tuple-element.40), channel_id=1, source_target_pairs={{0,32},{4,36},{8,40},{12,44},{16,48},{20,52},{24,56},{28,60},{32,6... | collective-permute-start | bytes 196616 | tf_op jit(solution)/shard_map/ppermute | solution.py:249
  4.7 2.5 %collective-permute-start.2 = (bf16[64,512]{1,0:T(8,128)(2,1)S(1)}, bf16[64,512]{1,0:T(8,128)(2,1)S(1)}, u32[]{:S(2)}, u32[]{:S(2)}) collective-permute-start(bf16[64,512]{1,0:T(8,128)(2,1)S(1)} %get-tuple-element.41), channel_id=1, source_target_pairs={{0,64},{4,68},{8,72},{12,76},{16,80},{20,84},{24,88},{28,92},{32,9... | collective-permute-start | bytes 196616 | tf_op jit(solution)/shard_map/ppermute | solution.py:249
  7.1 1.2 %collective-permute-start.3 = (bf16[64,512]{1,0:T(8,128)(2,1)S(1)}, bf16[64,512]{1,0:T(8,128)(2,1)S(1)}, u32[]{:S(2)}, u32[]{:S(2)}) collective-permute-start(bf16[64,512]{1,0:T(8,128)(2,1)S(1)} %get-tuple-element.42), channel_id=1, source_target_pairs={{0,96},{4,100},{8,104},{12,108},{16,112},{20,116},{24,120},{28,124... | collective-permute-start | bytes 196616 | tf_op jit(solution)/shard_map/ppermute | solution.py:249
  8.3 1.4 %collective-permute-start.8 = (bf16[64,512]{1,0:T(8,128)(2,1)S(1)}, bf16[64,512]{1,0:T(8,128)(2,1)S(1)}, u32[]{:S(2)}, u32[]{:S(2)}) collective-permute-start(bf16[64,512]{1,0:T(8,128)(2,1)S(1)} %get-tuple-element.48), channel_id=1, source_target_pairs={{0,8},{4,12},{8,16},{12,20},{16,24},{20,28},{24,0},{28,4},{32,40},... | collective-permute-start | bytes 196616 | tf_op jit(solution)/shard_map/ppermute | solution.py:249
  9.7 0.0 collective-permute-done.1.a1
  9.7 2.6 %collective-permute-start.9 = (bf16[64,512]{1,0:T(8,128)(2,1)S(1)}, bf16[64,512]{1,0:T(8,128)(2,1)S(1)}, u32[]{:S(2)}, u32[]{:S(2)}) collective-permute-start(bf16[64,512]{1,0:T(8,128)(2,1)S(1)} %get-tuple-element.49), channel_id=1, source_target_pairs={{0,16},{4,20},{8,24},{12,28},{16,0},{20,4},{24,8},{28,12},{32,48},... | collective-permute-start | bytes 196616 | tf_op jit(solution)/shard_map/ppermute | solution.py:249
  12.3 0.0 collective-permute-done.2.a2
  12.3 1.1 %collective-permute-start.10 = (bf16[64,512]{1,0:T(8,128)(2,1)S(1)}, bf16[64,512]{1,0:T(8,128)(2,1)S(1)}, u32[]{:S(2)}, u32[]{:S(2)}) collective-permute-start(bf16[64,512]{1,0:T(8,128)(2,1)S(1)} %get-tuple-element.50), channel_id=1, source_target_pairs={{0,24},{4,28},{8,0},{12,4},{16,8},{20,12},{24,16},{28,20},{32,56},... | collective-permute-start | bytes 196616 | tf_op jit(solution)/shard_map/ppermute | solution.py:249
  13.4 0.0 collective-permute-done.3.a3
  13.4 0.3 collective-permute-start.5
  13.7 0.0 collective-permute-done.8.b1
  13.7 2.6 %collective-permute-start.6 = (bf16[64,512]{1,0:T(8,128)(2,1)S(1)}, bf16[64,512]{1,0:T(8,128)(2,1)S(1)}, u32[]{:S(2)}, u32[]{:S(2)}) collective-permute-start(bf16[64,512]{1,0:T(8,128)(2,1)S(1)} %get-tuple-element.45), channel_id=1, source_target_pairs={{0,24},{4,28},{8,0},{12,4},{16,8},{20,12},{24,16},{28,20},{32,56},... | collective-permute-start | bytes 196616 | tf_op jit(solution)/shard_map/ppermute | solution.py:249
  16.3 0.0 collective-permute-done.9.b2
  16.3 0.0 collective-permute-start.4
  16.3 0.0 collective-permute-done.10.b3
  16.3 2.7 %collective-permute-start.11 = (bf16[64,512]{1,0:T(8,128)(2,1)S(1)}, bf16[64,512]{1,0:T(8,128)(2,1)S(1)}, u32[]{:S(2)}, u32[]{:S(2)}) collective-permute-start(bf16[64,512]{1,0:T(8,128)(2,1)S(1)} %collective-permute-done.8.b1), channel_id=1, source_target_pairs={{0,4},{4,0},{8,12},{12,8},{16,20},{20,16},{24,28},{28,24},{32,36},... | collective-permute-start | bytes 196616 | tf_op jit(solution)/shard_map/ppermute | solution.py:249
  19.0 0.0 collective-permute-done.5.u2
  19.0 2.4 %collective-permute-start.12 = (bf16[64,512]{1,0:T(8,128)(2,1)S(1)}, bf16[64,512]{1,0:T(8,128)(2,1)S(1)}, u32[]{:S(2)}, u32[]{:S(2)}) collective-permute-start(bf16[64,512]{1,0:T(8,128)(2,1)S(1)} %collective-permute-done.9.b2), channel_id=1, source_target_pairs={{0,4},{4,0},{8,12},{12,8},{16,20},{20,16},{24,28},{28,24},{32,36},... | collective-permute-start | bytes 196616 | tf_op jit(solution)/shard_map/ppermute | solution.py:249
  21.4 0.0 collective-permute-done.6.u3
  21.4 0.0 collective-permute-start.13
  21.4 0.0 collective-permute-done.4.u1
  21.5 0.0 collective-permute-done.7.po
  21.5 0.0 collective-permute-done.11.o1
  21.5 0.8 %collective-permute-done.12.o2 = bf16[64,512]{1,0:T(8,128)(2,1)S(1)} collective-permute-done((bf16[64,512]{1,0:T(8,128)(2,1)S(1)}, bf16[64,512]{1,0:T(8,128)(2,1)S(1)}, u32[]{:S(2)}, u32[]{:S(2)}) %collective-permute-start.12) | collective-permute-done | bytes 65568 | tf_op jit(solution)/shard_map/ppermute | solution.py:249
  22.3 0.4 collective-permute-done.13.o3
  22.7 0.3 product.1
  23.0 0.4 collective-permute-start.14
  23.4 1.4 %collective-permute-start.15 = (f32[64,512]{1,0:T(8,128)S(1)}, f32[64,512]{1,0:T(8,128)S(1)}, u32[]{:S(2)}, u32[]{:S(2)}) collective-permute-start(f32[64,512]{1,0:T(8,128)S(1)} %get-tuple-element.53), channel_id=1, source_target_pairs={{0,64},{4,68},{8,72},{12,76},{16,80},{20,84},{24,88},{28,92},{32,9... | collective-permute-start | bytes 393224 | tf_op jit(solution)/shard_map/ppermute | solution.py:249
  24.7 1.4 %collective-permute-start.16 = (f32[64,512]{1,0:T(8,128)S(1)}, f32[64,512]{1,0:T(8,128)S(1)}, u32[]{:S(2)}, u32[]{:S(2)}) collective-permute-start(f32[64,512]{1,0:T(8,128)S(1)} %get-tuple-element.54), channel_id=1, source_target_pairs={{0,96},{4,100},{8,104},{12,108},{16,112},{20,116},{24,120},{28,124... | collective-permute-start | bytes 393224 | tf_op jit(solution)/shard_map/ppermute | solution.py:249
  26.2 0.0 copy-done
  26.2 1.7 %norms1.1.__.f_5_ = f32[16,128]{1,0:T(8,128)S(1)} custom-call(bf16[4096,2048]{1,0:T(8,128)(2,1)S(1)} %copy-done, f32[64,512]{1,0:T(8,128)S(1)} %get-tuple-element.51.refs_1_.s0), custom_call_target="tpu_custom_call" | custom-call | flops 12582912 | bytes 8388608 | tf_op jit(solution)/shard_map/norms1/pallas_call | solution.py:36
  27.9 1.7 %norms0.1._.f_4_ = f32[16,128]{1,0:T(8,128)S(1)} custom-call(bf16[4096,2048]{1,0:T(8,128)(2,1)S(1)} %copy-done, f32[64,512]{1,0:T(8,128)S(1)} %get-tuple-element.51.refs_1_.s0), custom_call_target="tpu_custom_call" | custom-call | flops 12582912 | bytes 8388608 | tf_op jit(solution)/shard_map/norms0/pallas_call | solution.py:36
  29.6 0.1 collective-permute-done.14.s1
  29.7 0.1 collective-permute-done.15.s2
  29.7 0.8 %collective-permute-done.16.s3 = f32[64,512]{1,0:T(8,128)S(1)} collective-permute-done((f32[64,512]{1,0:T(8,128)S(1)}, f32[64,512]{1,0:T(8,128)S(1)}, u32[]{:S(2)}, u32[]{:S(2)}) %collective-permute-start.16) | collective-permute-done | bytes 131104 | tf_op jit(solution)/shard_map/ppermute | solution.py:249
  30.6 3.1 %collective-permute-start.17 = (bf16[64,512]{1,0:T(8,128)(2,1)S(1)}, bf16[64,512]{1,0:T(8,128)(2,1)S(1)}, u32[]{:S(2)}, u32[]{:S(2)}) collective-permute-start(bf16[64,512]{1,0:T(8,128)(2,1)S(1)} %round_sum.1.h), channel_id=1, source_target_pairs={{0,4},{4,0},{8,12},{12,8},{16,20},{20,16},{24,28},{28,24},{32,36},... | collective-permute-start | bytes 196616 | tf_op jit(solution)/shard_map/ppermute | solution.py:249
  33.7 0.9 %collective-permute-done.17.o = bf16[64,512]{1,0:T(8,128)(2,1)S(1)} collective-permute-done((bf16[64,512]{1,0:T(8,128)(2,1)S(1)}, bf16[64,512]{1,0:T(8,128)(2,1)S(1)}, u32[]{:S(2)}, u32[]{:S(2)}) %collective-permute-start.17) | collective-permute-done | bytes 65568 | tf_op jit(solution)/shard_map/ppermute | solution.py:249
  34.7 0.4 collective-permute-start.20
  35.0 2.4 %collective-permute-start.19 = (bf16[128,512]{1,0:T(8,128)(2,1)S(1)}, bf16[128,512]{1,0:T(8,128)(2,1)S(1)}, u32[]{:S(2)}, u32[]{:S(2)}) collective-permute-start(bf16[128,512]{1,0:T(8,128)(2,1)S(1)} %get-tuple-element.56), channel_id=1, source_target_pairs={{0,24},{4,28},{8,0},{12,4},{16,8},{20,12},{24,16},{28,20},{32,56},... | collective-permute-start | bytes 393224 | tf_op jit(solution)/shard_map/ppermute | solution.py:249
  37.4 0.8 %collective-permute-start.18 = (bf16[128,512]{1,0:T(8,128)(2,1)S(1)}, bf16[128,512]{1,0:T(8,128)(2,1)S(1)}, u32[]{:S(2)}, u32[]{:S(2)}) collective-permute-start(bf16[128,512]{1,0:T(8,128)(2,1)S(1)} %get-tuple-element.55), channel_id=1, source_target_pairs={{0,16},{4,20},{8,24},{12,28},{16,0},{20,4},{24,8},{28,12},{32,48},... | collective-permute-start | bytes 393224 | tf_op jit(solution)/shard_map/ppermute | solution.py:249
  38.2 1.2 %dots_first.1.f_2_ = f32[4096,128]{1,0:T(8,128)S(1)} custom-call(bf16[128,512]{1,0:T(8,128)(2,1)S(1)} %get-tuple-element.57.j.f_1_, bf16[4096,2048]{1,0:T(8,128)(2,1)S(1)} %copy-done), custom_call_target="tpu_custom_call" | custom-call | flops 536870912 | bytes 1048576 | tf_op jit(solution)/shard_map/dots_first/pallas_call | solution.py:36
  39.5 1.2 %collective-permute-done.20.f_0_.f_2_ = bf16[128,512]{1,0:T(8,128)(2,1)S(1)} collective-permute-done((bf16[128,512]{1,0:T(8,128)(2,1)S(1)}, bf16[128,512]{1,0:T(8,128)(2,1)S(1)}, u32[]{:S(2)}, u32[]{:S(2)}) %collective-permute-start.20) | collective-permute-done | bytes 131104 | tf_op jit(solution)/shard_map/ppermute | solution.py:249
  40.7 1.4 %dots_next1.1.f_4_ = f32[4096,128]{1,0:T(8,128)S(1)} custom-call(bf16[128,512]{1,0:T(8,128)(2,1)S(1)} %collective-permute-done.20.f_0_.f_2_, bf16[4096,2048]{1,0:T(8,128)(2,1)S(1)} %copy-done, f32[4096,128]{1,0:T(8,128)S(1)} %dots_first.1.f_2_), custom_call_target="tpu_custom_call", output_to_operand_aliasing={{}: (2, {})} | custom-call | flops 536870912 | bytes 1048576 | tf_op jit(solution)/shard_map/dots_next1/pallas_call | solution.py:36
  42.0 0.0 collective-permute-done.19.f_0_
  42.0 1.4 %dots_next3.1 = (f32[4096,128]{1,0:T(8,128)S(1)}, f32[128,128]{1,0:T(8,128)S(1)}) custom-call(bf16[128,512]{1,0:T(8,128)(2,1)S(1)} %collective-permute-done.19.f_0_, bf16[128,512]{1,0:T(8,128)(2,1)S(1)} %get-tuple-element.57.j.f_1_, bf16[128,512]{1,0:T(8,128)(2,1)S(1)} %collective-permute-done.20.f_0_.f_2_, ...), custom_call_target="tpu_custom_call", output_to_operand_aliasing={{0}: (4, {})} | custom-call | flops 536870912 | bytes 1048576 | tf_op jit(solution)/shard_map/dots_next3/pallas_call | solution.py:36
  43.4 0.9 %collective-permute-done.18.f_0_ = bf16[128,512]{1,0:T(8,128)(2,1)S(1)} collective-permute-done((bf16[128,512]{1,0:T(8,128)(2,1)S(1)}, bf16[128,512]{1,0:T(8,128)(2,1)S(1)}, u32[]{:S(2)}, u32[]{:S(2)}) %collective-permute-start.18) | collective-permute-done | bytes 131104 | tf_op jit(solution)/shard_map/ppermute | solution.py:249
  44.3 1.4 %dots_last.1 = (f32[32,4096]{1,0:T(8,128)S(1)}, f32[32,128]{1,0:T(8,128)S(1)}, f32[32,128]{1,0:T(8,128)S(1)}, bf16[32,4352]{1,0:T(8,128)(2,1)S(1)}, bf16[32,4352...) custom-call(bf16[128,512]{1,0:T(8,128)(2,1)S(1)} %collective-permute-done.18.f_0_, f32[128,128]{1,0:T(8,128)S(1)} %get-tuple-element.58.f_1_, ...), custom_call_target="tpu_custom_call" | custom-call | flops 536870912 | bytes 1048576 | tf_op jit(solution)/shard_map/dots_last/pallas_call | solution.py:36
  45.7 3.6 %collective-permute-start.21 = (bf16[32,4352]{1,0:T(8,128)(2,1)S(1)}, bf16[32,4352]{1,0:T(8,128)(2,1)S(1)}, u32[]{:S(2)}, u32[]{:S(2)}) collective-permute-start(bf16[32,4352]{1,0:T(8,128)(2,1)S(1)} %get-tuple-element.63), channel_id=1, source_target_pairs={{0,1},{1,2},{2,3},{3,0},{4,6},{5,7},{6,4},{7,5},{8,9},{9,10},{10,1... | collective-permute-start | bytes 835592 | tf_op jit(solution)/shard_map/ppermute | solution.py:257
  49.3 0.7 %collective-permute-start.22 = (bf16[32,4352]{1,0:T(8,128)(2,1)S(1)}, bf16[32,4352]{1,0:T(8,128)(2,1)S(1)}, u32[]{:S(2)}, u32[]{:S(2)}) collective-permute-start(bf16[32,4352]{1,0:T(8,128)(2,1)S(1)} %get-tuple-element.64), channel_id=1, source_target_pairs={{0,3},{1,0},{2,1},{3,2},{4,5},{5,6},{6,7},{7,4},{8,11},{9,8},{10,9... | collective-permute-start | bytes 835592 | tf_op jit(solution)/shard_map/ppermute | solution.py:257
  50.1 1.9 %collective-permute-start.23 = (bf16[32,4352]{1,0:T(8,128)(2,1)S(1)}, bf16[32,4352]{1,0:T(8,128)(2,1)S(1)}, u32[]{:S(2)}, u32[]{:S(2)}) collective-permute-start(bf16[32,4352]{1,0:T(8,128)(2,1)S(1)} %get-tuple-element.68), channel_id=1, source_target_pairs={{0,2},{1,3},{2,0},{3,1},{4,7},{5,4},{6,5},{7,6},{8,10},{9,11},{10,... | collective-permute-start | bytes 835592 | tf_op jit(solution)/shard_map/ppermute | solution.py:257
  52.0 3.7 %collective-permute-done.21.z1 = bf16[32,4352]{1,0:T(8,128)(2,1)S(1)} collective-permute-done((bf16[32,4352]{1,0:T(8,128)(2,1)S(1)}, bf16[32,4352]{1,0:T(8,128)(2,1)S(1)}, u32[]{:S(2)}, u32[]{:S(2)}) %collective-permute-start.21) | collective-permute-done | bytes 278560 | tf_op jit(solution)/shard_map/ppermute | solution.py:257
  55.7 5.7 %collective-permute-done.22.z3 = bf16[32,4352]{1,0:T(8,128)(2,1)S(1)} collective-permute-done((bf16[32,4352]{1,0:T(8,128)(2,1)S(1)}, bf16[32,4352]{1,0:T(8,128)(2,1)S(1)}, u32[]{:S(2)}, u32[]{:S(2)}) %collective-permute-start.22) | collective-permute-done | bytes 278560 | tf_op jit(solution)/shard_map/ppermute | solution.py:257
  61.4 0.3 finish_first.1
  61.7 0.9 %collective-permute-done.23.z2 = bf16[32,4352]{1,0:T(8,128)(2,1)S(1)} collective-permute-done((bf16[32,4352]{1,0:T(8,128)(2,1)S(1)}, bf16[32,4352]{1,0:T(8,128)(2,1)S(1)}, u32[]{:S(2)}, u32[]{:S(2)}) %collective-permute-start.23) | collective-permute-done | bytes 278560 | tf_op jit(solution)/shard_map/ppermute | solution.py:257
  62.6 1.0 %finish_last.1 = f32[32,4096]{1,0:T(8,128)} custom-call(f32[32,4096]{1,0:T(8,128)S(1)} %get-tuple-element.65.t, f32[32,128]{1,0:T(8,128)S(1)} %get-tuple-element.66.g, f32[32,128]{1,0:T(8,128)S(1)} %get-tuple-element.67.q, bf16[32,4352]{1,0:T(8,128)(2,1)S(1)} %collective-permute-done.23.z2), custom_call_target="tpu_custom_call" | custom-call | tf_op jit(solution)/shard_map/finish_last/pallas_call | solution.py:315
  (5 shorter events, 0.2 us)
Async XLA Ops:
  0.0 3.2 %collective-permute-start = (bf16[128,2048]{1,0:T(8,128)(2,1)}, bf16[128,2048]{1,0:T(8,128)(2,1)S(1)}, u32[]{:S(2)}, u32[]{:S(2)}) collective-permute-start(bf16[128,2048]{1,0:T(8,128)(2,1)} %bitcast.3), channel_id=1, source_target_pairs={{0,4},{4,0},{8,12},{12,8},{16,20},{20,16},{24,28},{28,24},{32,36},... | collective-permute-start | bytes 1572872 | tf_op jit(solution)/shard_map/ppermute | solution.py:249
  1.4 20.1 %collective-permute-start.7 = (bf16[64,2048]{1,0:T(8,128)(2,1)}, bf16[64,2048]{1,0:T(8,128)(2,1)S(1)}, u32[]{:S(2)}, u32[]{:S(2)}) collective-permute-start(bf16[64,2048]{1,0:T(8,128)(2,1)} %bitcast.5), channel_id=1, source_target_pairs={{0,4},{4,0},{8,12},{12,8},{16,20},{20,16},{24,28},{28,24},{32,36},... | collective-permute-start | bytes 786440 | tf_op jit(solution)/shard_map/ppermute | solution.py:249
  3.2 23.0 %copy-start = (bf16[4096,2048]{1,0:T(8,128)(2,1)S(1)}, bf16[4096,2048]{1,0:T(8,128)(2,1)}, u32[]{:S(2)}) copy-start(bf16[4096,2048]{1,0:T(8,128)(2,1)} %f_2_.1) | copy-start | bytes 50331652
  3.3 6.4 %collective-permute-start.1 = (bf16[64,512]{1,0:T(8,128)(2,1)S(1)}, bf16[64,512]{1,0:T(8,128)(2,1)S(1)}, u32[]{:S(2)}, u32[]{:S(2)}) collective-permute-start(bf16[64,512]{1,0:T(8,128)(2,1)S(1)} %get-tuple-element.40), channel_id=1, source_target_pairs={{0,32},{4,36},{8,40},{12,44},{16,48},{20,52},{24,56},{28,60},{32,6... | collective-permute-start | bytes 196616 | tf_op jit(solution)/shard_map/ppermute | solution.py:249
  4.7 7.6 %collective-permute-start.2 = (bf16[64,512]{1,0:T(8,128)(2,1)S(1)}, bf16[64,512]{1,0:T(8,128)(2,1)S(1)}, u32[]{:S(2)}, u32[]{:S(2)}) collective-permute-start(bf16[64,512]{1,0:T(8,128)(2,1)S(1)} %get-tuple-element.41), channel_id=1, source_target_pairs={{0,64},{4,68},{8,72},{12,76},{16,80},{20,84},{24,88},{28,92},{32,9... | collective-permute-start | bytes 196616 | tf_op jit(solution)/shard_map/ppermute | solution.py:249
  7.1 6.2 %collective-permute-start.3 = (bf16[64,512]{1,0:T(8,128)(2,1)S(1)}, bf16[64,512]{1,0:T(8,128)(2,1)S(1)}, u32[]{:S(2)}, u32[]{:S(2)}) collective-permute-start(bf16[64,512]{1,0:T(8,128)(2,1)S(1)} %get-tuple-element.42), channel_id=1, source_target_pairs={{0,96},{4,100},{8,104},{12,108},{16,112},{20,116},{24,120},{28,124... | collective-permute-start | bytes 196616 | tf_op jit(solution)/shard_map/ppermute | solution.py:249
  8.3 5.4 %collective-permute-start.8 = (bf16[64,512]{1,0:T(8,128)(2,1)S(1)}, bf16[64,512]{1,0:T(8,128)(2,1)S(1)}, u32[]{:S(2)}, u32[]{:S(2)}) collective-permute-start(bf16[64,512]{1,0:T(8,128)(2,1)S(1)} %get-tuple-element.48), channel_id=1, source_target_pairs={{0,8},{4,12},{8,16},{12,20},{16,24},{20,28},{24,0},{28,4},{32,40},... | collective-permute-start | bytes 196616 | tf_op jit(solution)/shard_map/ppermute | solution.py:249
  9.7 6.6 %collective-permute-start.9 = (bf16[64,512]{1,0:T(8,128)(2,1)S(1)}, bf16[64,512]{1,0:T(8,128)(2,1)S(1)}, u32[]{:S(2)}, u32[]{:S(2)}) collective-permute-start(bf16[64,512]{1,0:T(8,128)(2,1)S(1)} %get-tuple-element.49), channel_id=1, source_target_pairs={{0,16},{4,20},{8,24},{12,28},{16,0},{20,4},{24,8},{28,12},{32,48},... | collective-permute-start | bytes 196616 | tf_op jit(solution)/shard_map/ppermute | solution.py:249
  12.3 4.0 %collective-permute-start.10 = (bf16[64,512]{1,0:T(8,128)(2,1)S(1)}, bf16[64,512]{1,0:T(8,128)(2,1)S(1)}, u32[]{:S(2)}, u32[]{:S(2)}) collective-permute-start(bf16[64,512]{1,0:T(8,128)(2,1)S(1)} %get-tuple-element.50), channel_id=1, source_target_pairs={{0,24},{4,28},{8,0},{12,4},{16,8},{20,12},{24,16},{28,20},{32,56},... | collective-permute-start | bytes 196616 | tf_op jit(solution)/shard_map/ppermute | solution.py:249
  13.4 5.6 %collective-permute-start.5 = (bf16[64,512]{1,0:T(8,128)(2,1)S(1)}, bf16[64,512]{1,0:T(8,128)(2,1)S(1)}, u32[]{:S(2)}, u32[]{:S(2)}) collective-permute-start(bf16[64,512]{1,0:T(8,128)(2,1)S(1)} %get-tuple-element.44), channel_id=1, source_target_pairs={{0,16},{4,20},{8,24},{12,28},{16,0},{20,4},{24,8},{28,12},{32,48},... | collective-permute-start | bytes 196616 | tf_op jit(solution)/shard_map/ppermute | solution.py:249
  13.7 7.7 %collective-permute-start.6 = (bf16[64,512]{1,0:T(8,128)(2,1)S(1)}, bf16[64,512]{1,0:T(8,128)(2,1)S(1)}, u32[]{:S(2)}, u32[]{:S(2)}) collective-permute-start(bf16[64,512]{1,0:T(8,128)(2,1)S(1)} %get-tuple-element.45), channel_id=1, source_target_pairs={{0,24},{4,28},{8,0},{12,4},{16,8},{20,12},{24,16},{28,20},{32,56},... | collective-permute-start | bytes 196616 | tf_op jit(solution)/shard_map/ppermute | solution.py:249
  16.3 5.1 %collective-permute-start.4 = (bf16[64,512]{1,0:T(8,128)(2,1)S(1)}, bf16[64,512]{1,0:T(8,128)(2,1)S(1)}, u32[]{:S(2)}, u32[]{:S(2)}) collective-permute-start(bf16[64,512]{1,0:T(8,128)(2,1)S(1)} %get-tuple-element.43.r), channel_id=1, source_target_pairs={{0,8},{4,12},{8,16},{12,20},{16,24},{20,28},{24,0},{28,4},{32,40},... | collective-permute-start | bytes 196616 | tf_op jit(solution)/shard_map/ppermute | solution.py:249
  16.3 5.2 %collective-permute-start.11 = (bf16[64,512]{1,0:T(8,128)(2,1)S(1)}, bf16[64,512]{1,0:T(8,128)(2,1)S(1)}, u32[]{:S(2)}, u32[]{:S(2)}) collective-permute-start(bf16[64,512]{1,0:T(8,128)(2,1)S(1)} %collective-permute-done.8.b1), channel_id=1, source_target_pairs={{0,4},{4,0},{8,12},{12,8},{16,20},{20,16},{24,28},{28,24},{32,36},... | collective-permute-start | bytes 196616 | tf_op jit(solution)/shard_map/ppermute | solution.py:249
  19.0 3.3 %collective-permute-start.12 = (bf16[64,512]{1,0:T(8,128)(2,1)S(1)}, bf16[64,512]{1,0:T(8,128)(2,1)S(1)}, u32[]{:S(2)}, u32[]{:S(2)}) collective-permute-start(bf16[64,512]{1,0:T(8,128)(2,1)S(1)} %collective-permute-done.9.b2), channel_id=1, source_target_pairs={{0,4},{4,0},{8,12},{12,8},{16,20},{20,16},{24,28},{28,24},{32,36},... | collective-permute-start | bytes 196616 | tf_op jit(solution)/shard_map/ppermute | solution.py:249
  21.4 1.3 %collective-permute-start.13 = (bf16[64,512]{1,0:T(8,128)(2,1)S(1)}, bf16[64,512]{1,0:T(8,128)(2,1)S(1)}, u32[]{:S(2)}, u32[]{:S(2)}) collective-permute-start(bf16[64,512]{1,0:T(8,128)(2,1)S(1)} %collective-permute-done.10.b3), channel_id=1, source_target_pairs={{0,4},{4,0},{8,12},{12,8},{16,20},{20,16},{24,28},{28,24},{32,36},... | collective-permute-start | bytes 196616 | tf_op jit(solution)/shard_map/ppermute | solution.py:249
  23.0 6.7 %collective-permute-start.14 = (f32[64,512]{1,0:T(8,128)S(1)}, f32[64,512]{1,0:T(8,128)S(1)}, u32[]{:S(2)}, u32[]{:S(2)}) collective-permute-start(f32[64,512]{1,0:T(8,128)S(1)} %get-tuple-element.52), channel_id=1, source_target_pairs={{0,32},{4,36},{8,40},{12,44},{16,48},{20,52},{24,56},{28,60},{32,6... | collective-permute-start | bytes 393224 | tf_op jit(solution)/shard_map/ppermute | solution.py:249
  23.4 6.4 %collective-permute-start.15 = (f32[64,512]{1,0:T(8,128)S(1)}, f32[64,512]{1,0:T(8,128)S(1)}, u32[]{:S(2)}, u32[]{:S(2)}) collective-permute-start(f32[64,512]{1,0:T(8,128)S(1)} %get-tuple-element.53), channel_id=1, source_target_pairs={{0,64},{4,68},{8,72},{12,76},{16,80},{20,84},{24,88},{28,92},{32,9... | collective-permute-start | bytes 393224 | tf_op jit(solution)/shard_map/ppermute | solution.py:249
  24.7 5.8 %collective-permute-start.16 = (f32[64,512]{1,0:T(8,128)S(1)}, f32[64,512]{1,0:T(8,128)S(1)}, u32[]{:S(2)}, u32[]{:S(2)}) collective-permute-start(f32[64,512]{1,0:T(8,128)S(1)} %get-tuple-element.54), channel_id=1, source_target_pairs={{0,96},{4,100},{8,104},{12,108},{16,112},{20,116},{24,120},{28,124... | collective-permute-start | bytes 393224 | tf_op jit(solution)/shard_map/ppermute | solution.py:249
  30.6 4.0 %collective-permute-start.17 = (bf16[64,512]{1,0:T(8,128)(2,1)S(1)}, bf16[64,512]{1,0:T(8,128)(2,1)S(1)}, u32[]{:S(2)}, u32[]{:S(2)}) collective-permute-start(bf16[64,512]{1,0:T(8,128)(2,1)S(1)} %round_sum.1.h), channel_id=1, source_target_pairs={{0,4},{4,0},{8,12},{12,8},{16,20},{20,16},{24,28},{28,24},{32,36},... | collective-permute-start | bytes 196616 | tf_op jit(solution)/shard_map/ppermute | solution.py:249
  34.7 6.0 %collective-permute-start.20 = (bf16[128,512]{1,0:T(8,128)(2,1)S(1)}, bf16[128,512]{1,0:T(8,128)(2,1)S(1)}, u32[]{:S(2)}, u32[]{:S(2)}) collective-permute-start(bf16[128,512]{1,0:T(8,128)(2,1)S(1)} %get-tuple-element.57.j.f_1_), channel_id=1, source_target_pairs={{0,8},{4,12},{8,16},{12,20},{16,24},{20,28},{24,0},{28,4},{32,40},... | collective-permute-start | bytes 393224 | tf_op jit(solution)/shard_map/ppermute | solution.py:249
  35.0 7.0 %collective-permute-start.19 = (bf16[128,512]{1,0:T(8,128)(2,1)S(1)}, bf16[128,512]{1,0:T(8,128)(2,1)S(1)}, u32[]{:S(2)}, u32[]{:S(2)}) collective-permute-start(bf16[128,512]{1,0:T(8,128)(2,1)S(1)} %get-tuple-element.56), channel_id=1, source_target_pairs={{0,24},{4,28},{8,0},{12,4},{16,8},{20,12},{24,16},{28,20},{32,56},... | collective-permute-start | bytes 393224 | tf_op jit(solution)/shard_map/ppermute | solution.py:249
  37.4 6.9 %collective-permute-start.18 = (bf16[128,512]{1,0:T(8,128)(2,1)S(1)}, bf16[128,512]{1,0:T(8,128)(2,1)S(1)}, u32[]{:S(2)}, u32[]{:S(2)}) collective-permute-start(bf16[128,512]{1,0:T(8,128)(2,1)S(1)} %get-tuple-element.55), channel_id=1, source_target_pairs={{0,16},{4,20},{8,24},{12,28},{16,0},{20,4},{24,8},{28,12},{32,48},... | collective-permute-start | bytes 393224 | tf_op jit(solution)/shard_map/ppermute | solution.py:249
  45.7 10.0 %collective-permute-start.21 = (bf16[32,4352]{1,0:T(8,128)(2,1)S(1)}, bf16[32,4352]{1,0:T(8,128)(2,1)S(1)}, u32[]{:S(2)}, u32[]{:S(2)}) collective-permute-start(bf16[32,4352]{1,0:T(8,128)(2,1)S(1)} %get-tuple-element.63), channel_id=1, source_target_pairs={{0,1},{1,2},{2,3},{3,0},{4,6},{5,7},{6,4},{7,5},{8,9},{9,10},{10,1... | collective-permute-start | bytes 835592 | tf_op jit(solution)/shard_map/ppermute | solution.py:257
  49.3 12.1 %collective-permute-start.22 = (bf16[32,4352]{1,0:T(8,128)(2,1)S(1)}, bf16[32,4352]{1,0:T(8,128)(2,1)S(1)}, u32[]{:S(2)}, u32[]{:S(2)}) collective-permute-start(bf16[32,4352]{1,0:T(8,128)(2,1)S(1)} %get-tuple-element.64), channel_id=1, source_target_pairs={{0,3},{1,0},{2,1},{3,2},{4,5},{5,6},{6,7},{7,4},{8,11},{9,8},{10,9... | collective-permute-start | bytes 835592 | tf_op jit(solution)/shard_map/ppermute | solution.py:257
  50.1 12.6 %collective-permute-start.23 = (bf16[32,4352]{1,0:T(8,128)(2,1)S(1)}, bf16[32,4352]{1,0:T(8,128)(2,1)S(1)}, u32[]{:S(2)}, u32[]{:S(2)}) collective-permute-start(bf16[32,4352]{1,0:T(8,128)(2,1)S(1)} %get-tuple-element.68), channel_id=1, source_target_pairs={{0,2},{1,3},{2,0},{3,1},{4,7},{5,4},{6,5},{7,6},{8,10},{9,11},{10,... | collective-permute-start | bytes 835592 | tf_op jit(solution)/shard_map/ppermute | solution.py:257

commit v8 on v6

--- a/solution.py
+++ b/solution.py
@@ -120,7 +120,7 @@
     h[...] = total * jnp.asarray(0.5, BF16)
 
 
-WAYS = ((1, 3, 2), (2, 1, 3))
+WAYS = ((1, 3, 2), (2, 3, 1))
 
 
 def slot(ahead, c):

time: 63.9 us -> 64.1 us (level)
  waiting for transfers between devices: 16.3 us -> 17.6 us
  starting transfers between devices: 35.6 us -> 34.4 us
    ppermute x3, waiting for transfers between devices: 10.4 us -> 11.7 us  [send_layer(): return lax.ppermute(a, ('ex', 'layer'), pairs)]
    ppermute x3, starting transfers between devices: 6.32 us -> 5.12 us  [send_layer(): return lax.ppermute(a, ('ex', 'layer'), pairs)]
  transfers between devices with their start and end apart: 24 -> 24, of which waited for: 12 -> 11; matrix products, arithmetic and copies ran while one was open for 0% -> 0% of each run, Pallas kernels for 14% -> 14%
where the time goes in v8:
time: 64.1 us; the launch traced here: 63.9 us
  starting transfers between devices  34.4 us (54%)
  waiting for transfers between devices  17.6 us (27%)
  Pallas kernels  11.6 us (18%)
    ppermute x21, starting transfers between devices, send(): return lax.ppermute(a, 'ex', moved(dx, dy, dc))  29.3 us
    ppermute x3, waiting for transfers between devices, send_layer(): return lax.ppermute(a, ('ex', 'layer'), pairs)  11.7 us
    pallas_call x15, Pallas kernels, call(): pl.pallas_call(body, name=name, in_specs=[pl.BlockSpec(memory_space=space...  10.6 us
    ppermute x21, waiting for transfers between devices, send(): return lax.ppermute(a, 'ex', moved(dx, dy, dc))  5.91 us
    ppermute x3, starting transfers between devices, send_layer(): return lax.ppermute(a, ('ex', 'layer'), pairs)  5.12 us
  transfers between devices with their start and end apart: 24, of which 11 were waited for; matrix products, arithmetic and copies ran while one was open for 0% of the time, Pallas kernels for 14%

profile of v8, /device:TPU:1, one launch (start us, length us, event | category | flops | bytes accessed | tf_op | source)
XLA Modules:
  0.0 63.9 jit_solution(11557615219746588822)
XLA Ops:
  0.0 1.4 %collective-permute-start = (bf16[128,2048]{1,0:T(8,128)(2,1)}, bf16[128,2048]{1,0:T(8,128)(2,1)S(1)}, u32[]{:S(2)}, u32[]{:S(2)}) collective-permute-start(bf16[128,2048]{1,0:T(8,128)(2,1)} %bitcast.3), channel_id=1, source_target_pairs={{0,4},{4,0},{8,12},{12,8},{16,20},{20,16},{24,28},{28,24},{32,36},... | collective-permute-start | bytes 1572872 | tf_op jit(solution)/shard_map/ppermute | solution.py:239
  1.4 0.0 collective-permute-start.7
  1.4 1.1 %fetch.1 = (bf16[10,64,128]{2,1,0:T(8,128)(2,1)S(1)}, bf16[64,2048]{1,0:T(8,128)(2,1)S(1)}, bf16[64,2048]{1,0:T(8,128)(2,1)S(1)}) custom-call(s32[2]{0:T(128)} %owners.1, bf16[128,2048]{1,0:T(8,128)(2,1)} %bitcast.4, bf16[64,2048]{1,0:T(8,128)(2,1)} %bitcast.6), custom_call_target="tpu_custom_call" | custom-call | bytes 1048576 | tf_op jit(solution)/shard_map/fetch/pallas_call | solution.py:36
  2.5 0.7 %collective-permute-done.qo = bf16[128,2048]{1,0:T(8,128)(2,1)S(1)} collective-permute-done((bf16[128,2048]{1,0:T(8,128)(2,1)}, bf16[128,2048]{1,0:T(8,128)(2,1)S(1)}, u32[]{:S(2)}, u32[]{:S(2)}) %collective-permute-start) | collective-permute-done | bytes 524320 | tf_op jit(solution)/shard_map/ppermute | solution.py:239
  3.2 0.0 copy-start
  3.2 0.1 slices.1
  3.3 1.4 %collective-permute-start.1 = (bf16[64,512]{1,0:T(8,128)(2,1)S(1)}, bf16[64,512]{1,0:T(8,128)(2,1)S(1)}, u32[]{:S(2)}, u32[]{:S(2)}) collective-permute-start(bf16[64,512]{1,0:T(8,128)(2,1)S(1)} %get-tuple-element.38), channel_id=1, source_target_pairs={{0,32},{4,36},{8,40},{12,44},{16,48},{20,52},{24,56},{28,60},{32,6... | collective-permute-start | bytes 196616 | tf_op jit(solution)/shard_map/ppermute | solution.py:239
  4.7 2.5 %collective-permute-start.2 = (bf16[64,512]{1,0:T(8,128)(2,1)S(1)}, bf16[64,512]{1,0:T(8,128)(2,1)S(1)}, u32[]{:S(2)}, u32[]{:S(2)}) collective-permute-start(bf16[64,512]{1,0:T(8,128)(2,1)S(1)} %get-tuple-element.39), channel_id=1, source_target_pairs={{0,64},{4,68},{8,72},{12,76},{16,80},{20,84},{24,88},{28,92},{32,9... | collective-permute-start | bytes 196616 | tf_op jit(solution)/shard_map/ppermute | solution.py:239
  7.1 1.2 %collective-permute-start.3 = (bf16[64,512]{1,0:T(8,128)(2,1)S(1)}, bf16[64,512]{1,0:T(8,128)(2,1)S(1)}, u32[]{:S(2)}, u32[]{:S(2)}) collective-permute-start(bf16[64,512]{1,0:T(8,128)(2,1)S(1)} %get-tuple-element.40), channel_id=1, source_target_pairs={{0,96},{4,100},{8,104},{12,108},{16,112},{20,116},{24,120},{28,124... | collective-permute-start | bytes 196616 | tf_op jit(solution)/shard_map/ppermute | solution.py:239
  8.3 1.4 %collective-permute-start.8 = (bf16[64,512]{1,0:T(8,128)(2,1)S(1)}, bf16[64,512]{1,0:T(8,128)(2,1)S(1)}, u32[]{:S(2)}, u32[]{:S(2)}) collective-permute-start(bf16[64,512]{1,0:T(8,128)(2,1)S(1)} %get-tuple-element.46), channel_id=1, source_target_pairs={{0,8},{4,12},{8,16},{12,20},{16,24},{20,28},{24,0},{28,4},{32,40},... | collective-permute-start | bytes 196616 | tf_op jit(solution)/shard_map/ppermute | solution.py:239
  9.7 0.0 collective-permute-done.1.a1
  9.7 2.6 %collective-permute-start.9 = (bf16[64,512]{1,0:T(8,128)(2,1)S(1)}, bf16[64,512]{1,0:T(8,128)(2,1)S(1)}, u32[]{:S(2)}, u32[]{:S(2)}) collective-permute-start(bf16[64,512]{1,0:T(8,128)(2,1)S(1)} %get-tuple-element.47), channel_id=1, source_target_pairs={{0,16},{4,20},{8,24},{12,28},{16,0},{20,4},{24,8},{28,12},{32,48},... | collective-permute-start | bytes 196616 | tf_op jit(solution)/shard_map/ppermute | solution.py:239
  12.3 0.0 collective-permute-done.2.a2
  12.3 1.1 %collective-permute-start.10 = (bf16[64,512]{1,0:T(8,128)(2,1)S(1)}, bf16[64,512]{1,0:T(8,128)(2,1)S(1)}, u32[]{:S(2)}, u32[]{:S(2)}) collective-permute-start(bf16[64,512]{1,0:T(8,128)(2,1)S(1)} %get-tuple-element.48), channel_id=1, source_target_pairs={{0,24},{4,28},{8,0},{12,4},{16,8},{20,12},{24,16},{28,20},{32,56},... | collective-permute-start | bytes 196616 | tf_op jit(solution)/shard_map/ppermute | solution.py:239
  13.4 0.0 collective-permute-done.3.a3
  13.4 0.3 collective-permute-start.5
  13.7 0.0 collective-permute-done.8.b1
  13.7 2.6 %collective-permute-start.6 = (bf16[64,512]{1,0:T(8,128)(2,1)S(1)}, bf16[64,512]{1,0:T(8,128)(2,1)S(1)}, u32[]{:S(2)}, u32[]{:S(2)}) collective-permute-start(bf16[64,512]{1,0:T(8,128)(2,1)S(1)} %get-tuple-element.43), channel_id=1, source_target_pairs={{0,24},{4,28},{8,0},{12,4},{16,8},{20,12},{24,16},{28,20},{32,56},... | collective-permute-start | bytes 196616 | tf_op jit(solution)/shard_map/ppermute | solution.py:239
  16.3 0.0 collective-permute-done.9.b2
  16.3 0.0 collective-permute-start.4
  16.3 0.0 collective-permute-done.10.b3
  16.3 2.7 %collective-permute-start.11 = (bf16[64,512]{1,0:T(8,128)(2,1)S(1)}, bf16[64,512]{1,0:T(8,128)(2,1)S(1)}, u32[]{:S(2)}, u32[]{:S(2)}) collective-permute-start(bf16[64,512]{1,0:T(8,128)(2,1)S(1)} %collective-permute-done.8.b1), channel_id=1, source_target_pairs={{0,4},{4,0},{8,12},{12,8},{16,20},{20,16},{24,28},{28,24},{32,36},... | collective-permute-start | bytes 196616 | tf_op jit(solution)/shard_map/ppermute | solution.py:239
  19.0 0.0 collective-permute-done.5.u2
  19.0 2.4 %collective-permute-start.12 = (bf16[64,512]{1,0:T(8,128)(2,1)S(1)}, bf16[64,512]{1,0:T(8,128)(2,1)S(1)}, u32[]{:S(2)}, u32[]{:S(2)}) collective-permute-start(bf16[64,512]{1,0:T(8,128)(2,1)S(1)} %collective-permute-done.9.b2), channel_id=1, source_target_pairs={{0,4},{4,0},{8,12},{12,8},{16,20},{20,16},{24,28},{28,24},{32,36},... | collective-permute-start | bytes 196616 | tf_op jit(solution)/shard_map/ppermute | solution.py:239
  21.4 0.0 collective-permute-done.6.u3
  21.4 0.0 collective-permute-start.13
  21.4 0.0 collective-permute-done.4.u1
  21.5 0.0 collective-permute-done.7.po
  21.5 0.0 collective-permute-done.11.o1
  21.5 0.8 %collective-permute-done.12.o2 = bf16[64,512]{1,0:T(8,128)(2,1)S(1)} collective-permute-done((bf16[64,512]{1,0:T(8,128)(2,1)S(1)}, bf16[64,512]{1,0:T(8,128)(2,1)S(1)}, u32[]{:S(2)}, u32[]{:S(2)}) %collective-permute-start.12) | collective-permute-done | bytes 65568 | tf_op jit(solution)/shard_map/ppermute | solution.py:239
  22.3 0.4 collective-permute-done.13.o3
  22.7 0.3 product.1
  23.0 0.4 collective-permute-start.14
  23.4 1.4 %collective-permute-start.15 = (f32[64,512]{1,0:T(8,128)S(1)}, f32[64,512]{1,0:T(8,128)S(1)}, u32[]{:S(2)}, u32[]{:S(2)}) collective-permute-start(f32[64,512]{1,0:T(8,128)S(1)} %get-tuple-element.51), channel_id=1, source_target_pairs={{0,64},{4,68},{8,72},{12,76},{16,80},{20,84},{24,88},{28,92},{32,9... | collective-permute-start | bytes 393224 | tf_op jit(solution)/shard_map/ppermute | solution.py:239
  24.7 1.4 %collective-permute-start.16 = (f32[64,512]{1,0:T(8,128)S(1)}, f32[64,512]{1,0:T(8,128)S(1)}, u32[]{:S(2)}, u32[]{:S(2)}) collective-permute-start(f32[64,512]{1,0:T(8,128)S(1)} %get-tuple-element.52), channel_id=1, source_target_pairs={{0,96},{4,100},{8,104},{12,108},{16,112},{20,116},{24,120},{28,124... | collective-permute-start | bytes 393224 | tf_op jit(solution)/shard_map/ppermute | solution.py:239
  26.2 0.0 copy-done
  26.2 1.7 %norms1.1.__.f_7_ = f32[16,128]{1,0:T(8,128)S(1)} custom-call(bf16[4096,2048]{1,0:T(8,128)(2,1)S(1)} %copy-done, f32[64,512]{1,0:T(8,128)S(1)} %get-tuple-element.49.refs_1_.s0), custom_call_target="tpu_custom_call" | custom-call | flops 12582912 | bytes 8388608 | tf_op jit(solution)/shard_map/norms1/pallas_call | solution.py:36
  27.9 1.7 %norms0.1._.f_6_ = f32[16,128]{1,0:T(8,128)S(1)} custom-call(bf16[4096,2048]{1,0:T(8,128)(2,1)S(1)} %copy-done, f32[64,512]{1,0:T(8,128)S(1)} %get-tuple-element.49.refs_1_.s0), custom_call_target="tpu_custom_call" | custom-call | flops 12582912 | bytes 8388608 | tf_op jit(solution)/shard_map/norms0/pallas_call | solution.py:36
  29.6 0.1 collective-permute-done.14.s1
  29.7 0.1 collective-permute-done.15.s2
  29.7 0.8 %collective-permute-done.16.s3 = f32[64,512]{1,0:T(8,128)S(1)} collective-permute-done((f32[64,512]{1,0:T(8,128)S(1)}, f32[64,512]{1,0:T(8,128)S(1)}, u32[]{:S(2)}, u32[]{:S(2)}) %collective-permute-start.16) | collective-permute-done | bytes 131104 | tf_op jit(solution)/shard_map/ppermute | solution.py:239
  30.6 3.1 %collective-permute-start.17 = (bf16[64,512]{1,0:T(8,128)(2,1)S(1)}, bf16[64,512]{1,0:T(8,128)(2,1)S(1)}, u32[]{:S(2)}, u32[]{:S(2)}) collective-permute-start(bf16[64,512]{1,0:T(8,128)(2,1)S(1)} %round_sum.1.h), channel_id=1, source_target_pairs={{0,4},{4,0},{8,12},{12,8},{16,20},{20,16},{24,28},{28,24},{32,36},... | collective-permute-start | bytes 196616 | tf_op jit(solution)/shard_map/ppermute | solution.py:239
  33.7 0.9 %collective-permute-done.17.o = bf16[64,512]{1,0:T(8,128)(2,1)S(1)} collective-permute-done((bf16[64,512]{1,0:T(8,128)(2,1)S(1)}, bf16[64,512]{1,0:T(8,128)(2,1)S(1)}, u32[]{:S(2)}, u32[]{:S(2)}) %collective-permute-start.17) | collective-permute-done | bytes 65568 | tf_op jit(solution)/shard_map/ppermute | solution.py:239
  34.7 0.4 collective-permute-start.19
  35.0 2.4 %collective-permute-start.20 = (bf16[128,512]{1,0:T(8,128)(2,1)S(1)}, bf16[128,512]{1,0:T(8,128)(2,1)S(1)}, u32[]{:S(2)}, u32[]{:S(2)}) collective-permute-start(bf16[128,512]{1,0:T(8,128)(2,1)S(1)} %get-tuple-element.55), channel_id=1, source_target_pairs={{0,24},{4,28},{8,0},{12,4},{16,8},{20,12},{24,16},{28,20},{32,56},... | collective-permute-start | bytes 393224 | tf_op jit(solution)/shard_map/ppermute | solution.py:239
  37.4 0.8 %collective-permute-start.18 = (bf16[128,512]{1,0:T(8,128)(2,1)S(1)}, bf16[128,512]{1,0:T(8,128)(2,1)S(1)}, u32[]{:S(2)}, u32[]{:S(2)}) collective-permute-start(bf16[128,512]{1,0:T(8,128)(2,1)S(1)} %get-tuple-element.53), channel_id=1, source_target_pairs={{0,16},{4,20},{8,24},{12,28},{16,0},{20,4},{24,8},{28,12},{32,48},... | collective-permute-start | bytes 393224 | tf_op jit(solution)/shard_map/ppermute | solution.py:239
  38.2 1.2 %dots_first.1.f_2_ = f32[4096,128]{1,0:T(8,128)S(1)} custom-call(bf16[128,512]{1,0:T(8,128)(2,1)S(1)} %get-tuple-element.54.j.f_1_, bf16[4096,2048]{1,0:T(8,128)(2,1)S(1)} %copy-done), custom_call_target="tpu_custom_call" | custom-call | flops 536870912 | bytes 1048576 | tf_op jit(solution)/shard_map/dots_first/pallas_call | solution.py:36
  39.5 1.2 %collective-permute-done.19.f_0_.f_2_ = bf16[128,512]{1,0:T(8,128)(2,1)S(1)} collective-permute-done((bf16[128,512]{1,0:T(8,128)(2,1)S(1)}, bf16[128,512]{1,0:T(8,128)(2,1)S(1)}, u32[]{:S(2)}, u32[]{:S(2)}) %collective-permute-start.19) | collective-permute-done | bytes 131104 | tf_op jit(solution)/shard_map/ppermute | solution.py:239
  40.7 1.4 %dots_next1.1.f_2_ = f32[4096,128]{1,0:T(8,128)S(1)} custom-call(bf16[128,512]{1,0:T(8,128)(2,1)S(1)} %collective-permute-done.19.f_0_.f_2_, bf16[4096,2048]{1,0:T(8,128)(2,1)S(1)} %copy-done, f32[4096,128]{1,0:T(8,128)S(1)} %dots_first.1.f_2_), custom_call_target="tpu_custom_call", output_to_operand_aliasing={{}: (2, {})} | custom-call | flops 536870912 | bytes 1048576 | tf_op jit(solution)/shard_map/dots_next1/pallas_call | solution.py:36
  42.0 0.0 collective-permute-done.20.f_0_.f_3_
  42.0 1.4 %dots_next3.1.f_5_ = f32[4096,128]{1,0:T(8,128)S(1)} custom-call(bf16[128,512]{1,0:T(8,128)(2,1)S(1)} %collective-permute-done.20.f_0_.f_3_, bf16[4096,2048]{1,0:T(8,128)(2,1)S(1)} %copy-done, f32[4096,128]{1,0:T(8,128)S(1)} %dots_next1.1.f_2_), custom_call_target="tpu_custom_call", output_to_operand_aliasing={{}: (2, {})} | custom-call | flops 536870912 | bytes 1048576 | tf_op jit(solution)/shard_map/dots_next3/pallas_call | solution.py:36
  43.4 0.9 %collective-permute-done.18.f_0_ = bf16[128,512]{1,0:T(8,128)(2,1)S(1)} collective-permute-done((bf16[128,512]{1,0:T(8,128)(2,1)S(1)}, bf16[128,512]{1,0:T(8,128)(2,1)S(1)}, u32[]{:S(2)}, u32[]{:S(2)}) %collective-permute-start.18) | collective-permute-done | bytes 131104 | tf_op jit(solution)/shard_map/ppermute | solution.py:239
  44.3 1.4 %dots_last.1 = (f32[32,4096]{1,0:T(8,128)S(1)}, f32[32,128]{1,0:T(8,128)S(1)}, f32[32,128]{1,0:T(8,128)S(1)}, bf16[32,4352]{1,0:T(8,128)(2,1)S(1)}, bf16[32,4352...) custom-call(bf16[128,512]{1,0:T(8,128)(2,1)S(1)} %collective-permute-done.18.f_0_, ...), custom_call_target="tpu_custom_call" | custom-call | flops 536870912 | bytes 1048576 | tf_op jit(solution)/shard_map/dots_last/pallas_call | solution.py:36
  45.7 3.7 %collective-permute-start.21 = (bf16[32,4352]{1,0:T(8,128)(2,1)S(1)}, bf16[32,4352]{1,0:T(8,128)(2,1)S(1)}, u32[]{:S(2)}, u32[]{:S(2)}) collective-permute-start(bf16[32,4352]{1,0:T(8,128)(2,1)S(1)} %get-tuple-element.59), channel_id=1, source_target_pairs={{0,1},{1,2},{2,3},{3,0},{4,6},{5,7},{6,4},{7,5},{8,9},{9,10},{10,1... | collective-permute-start | bytes 835592 | tf_op jit(solution)/shard_map/ppermute | solution.py:247
  49.4 0.4 collective-permute-start.22
  49.8 1.0 %collective-permute-start.23 = (bf16[32,4352]{1,0:T(8,128)(2,1)S(1)}, bf16[32,4352]{1,0:T(8,128)(2,1)S(1)}, u32[]{:S(2)}, u32[]{:S(2)}) collective-permute-start(bf16[32,4352]{1,0:T(8,128)(2,1)S(1)} %get-tuple-element.64), channel_id=1, source_target_pairs={{0,2},{1,3},{2,0},{3,1},{4,5},{5,6},{6,7},{7,4},{8,10},{9,11},{10,... | collective-permute-start | bytes 835592 | tf_op jit(solution)/shard_map/ppermute | solution.py:247
  50.8 4.9 %collective-permute-done.21.z1 = bf16[32,4352]{1,0:T(8,128)(2,1)S(1)} collective-permute-done((bf16[32,4352]{1,0:T(8,128)(2,1)S(1)}, bf16[32,4352]{1,0:T(8,128)(2,1)S(1)}, u32[]{:S(2)}, u32[]{:S(2)}) %collective-permute-start.21) | collective-permute-done | bytes 278560 | tf_op jit(solution)/shard_map/ppermute | solution.py:247
  55.7 6.8 %collective-permute-done.22.z3 = bf16[32,4352]{1,0:T(8,128)(2,1)S(1)} collective-permute-done((bf16[32,4352]{1,0:T(8,128)(2,1)S(1)}, bf16[32,4352]{1,0:T(8,128)(2,1)S(1)}, u32[]{:S(2)}, u32[]{:S(2)}) %collective-permute-start.22) | collective-permute-done | bytes 278560 | tf_op jit(solution)/shard_map/ppermute | solution.py:247
  62.5 0.3 finish_first.1
  62.8 0.0 collective-permute-done.23.z2
  62.8 1.0 %finish_last.1 = f32[32,4096]{1,0:T(8,128)} custom-call(f32[32,4096]{1,0:T(8,128)S(1)} %get-tuple-element.61.t, f32[32,128]{1,0:T(8,128)S(1)} %get-tuple-element.62.g, f32[32,128]{1,0:T(8,128)S(1)} %get-tuple-element.63.q, bf16[32,4352]{1,0:T(8,128)(2,1)S(1)} %collective-permute-done.23.z2), custom_call_target="tpu_custom_call" | custom-call | tf_op jit(solution)/shard_map/finish_last/pallas_call | solution.py:302
  (5 shorter events, 0.2 us)
Async XLA Ops:
  0.0 3.2 %collective-permute-start = (bf16[128,2048]{1,0:T(8,128)(2,1)}, bf16[128,2048]{1,0:T(8,128)(2,1)S(1)}, u32[]{:S(2)}, u32[]{:S(2)}) collective-permute-start(bf16[128,2048]{1,0:T(8,128)(2,1)} %bitcast.3), channel_id=1, source_target_pairs={{0,4},{4,0},{8,12},{12,8},{16,20},{20,16},{24,28},{28,24},{32,36},... | collective-permute-start | bytes 1572872 | tf_op jit(solution)/shard_map/ppermute | solution.py:239
  1.4 20.1 %collective-permute-start.7 = (bf16[64,2048]{1,0:T(8,128)(2,1)}, bf16[64,2048]{1,0:T(8,128)(2,1)S(1)}, u32[]{:S(2)}, u32[]{:S(2)}) collective-permute-start(bf16[64,2048]{1,0:T(8,128)(2,1)} %bitcast.5), channel_id=1, source_target_pairs={{0,4},{4,0},{8,12},{12,8},{16,20},{20,16},{24,28},{28,24},{32,36},... | collective-permute-start | bytes 786440 | tf_op jit(solution)/shard_map/ppermute | solution.py:239
  3.2 23.0 %copy-start = (bf16[4096,2048]{1,0:T(8,128)(2,1)S(1)}, bf16[4096,2048]{1,0:T(8,128)(2,1)}, u32[]{:S(2)}) copy-start(bf16[4096,2048]{1,0:T(8,128)(2,1)} %f_4_.1) | copy-start | bytes 50331652
  3.3 6.4 %collective-permute-start.1 = (bf16[64,512]{1,0:T(8,128)(2,1)S(1)}, bf16[64,512]{1,0:T(8,128)(2,1)S(1)}, u32[]{:S(2)}, u32[]{:S(2)}) collective-permute-start(bf16[64,512]{1,0:T(8,128)(2,1)S(1)} %get-tuple-element.38), channel_id=1, source_target_pairs={{0,32},{4,36},{8,40},{12,44},{16,48},{20,52},{24,56},{28,60},{32,6... | collective-permute-start | bytes 196616 | tf_op jit(solution)/shard_map/ppermute | solution.py:239
  4.7 7.6 %collective-permute-start.2 = (bf16[64,512]{1,0:T(8,128)(2,1)S(1)}, bf16[64,512]{1,0:T(8,128)(2,1)S(1)}, u32[]{:S(2)}, u32[]{:S(2)}) collective-permute-start(bf16[64,512]{1,0:T(8,128)(2,1)S(1)} %get-tuple-element.39), channel_id=1, source_target_pairs={{0,64},{4,68},{8,72},{12,76},{16,80},{20,84},{24,88},{28,92},{32,9... | collective-permute-start | bytes 196616 | tf_op jit(solution)/shard_map/ppermute | solution.py:239
  7.1 6.2 %collective-permute-start.3 = (bf16[64,512]{1,0:T(8,128)(2,1)S(1)}, bf16[64,512]{1,0:T(8,128)(2,1)S(1)}, u32[]{:S(2)}, u32[]{:S(2)}) collective-permute-start(bf16[64,512]{1,0:T(8,128)(2,1)S(1)} %get-tuple-element.40), channel_id=1, source_target_pairs={{0,96},{4,100},{8,104},{12,108},{16,112},{20,116},{24,120},{28,124... | collective-permute-start | bytes 196616 | tf_op jit(solution)/shard_map/ppermute | solution.py:239
  8.3 5.4 %collective-permute-start.8 = (bf16[64,512]{1,0:T(8,128)(2,1)S(1)}, bf16[64,512]{1,0:T(8,128)(2,1)S(1)}, u32[]{:S(2)}, u32[]{:S(2)}) collective-permute-start(bf16[64,512]{1,0:T(8,128)(2,1)S(1)} %get-tuple-element.46), channel_id=1, source_target_pairs={{0,8},{4,12},{8,16},{12,20},{16,24},{20,28},{24,0},{28,4},{32,40},... | collective-permute-start | bytes 196616 | tf_op jit(solution)/shard_map/ppermute | solution.py:239
  9.7 6.6 %collective-permute-start.9 = (bf16[64,512]{1,0:T(8,128)(2,1)S(1)}, bf16[64,512]{1,0:T(8,128)(2,1)S(1)}, u32[]{:S(2)}, u32[]{:S(2)}) collective-permute-start(bf16[64,512]{1,0:T(8,128)(2,1)S(1)} %get-tuple-element.47), channel_id=1, source_target_pairs={{0,16},{4,20},{8,24},{12,28},{16,0},{20,4},{24,8},{28,12},{32,48},... | collective-permute-start | bytes 196616 | tf_op jit(solution)/shard_map/ppermute | solution.py:239
  12.3 4.0 %collective-permute-start.10 = (bf16[64,512]{1,0:T(8,128)(2,1)S(1)}, bf16[64,512]{1,0:T(8,128)(2,1)S(1)}, u32[]{:S(2)}, u32[]{:S(2)}) collective-permute-start(bf16[64,512]{1,0:T(8,128)(2,1)S(1)} %get-tuple-element.48), channel_id=1, source_target_pairs={{0,24},{4,28},{8,0},{12,4},{16,8},{20,12},{24,16},{28,20},{32,56},... | collective-permute-start | bytes 196616 | tf_op jit(solution)/shard_map/ppermute | solution.py:239
  13.4 5.6 %collective-permute-start.5 = (bf16[64,512]{1,0:T(8,128)(2,1)S(1)}, bf16[64,512]{1,0:T(8,128)(2,1)S(1)}, u32[]{:S(2)}, u32[]{:S(2)}) collective-permute-start(bf16[64,512]{1,0:T(8,128)(2,1)S(1)} %get-tuple-element.42), channel_id=1, source_target_pairs={{0,16},{4,20},{8,24},{12,28},{16,0},{20,4},{24,8},{28,12},{32,48},... | collective-permute-start | bytes 196616 | tf_op jit(solution)/shard_map/ppermute | solution.py:239
  13.7 7.7 %collective-permute-start.6 = (bf16[64,512]{1,0:T(8,128)(2,1)S(1)}, bf16[64,512]{1,0:T(8,128)(2,1)S(1)}, u32[]{:S(2)}, u32[]{:S(2)}) collective-permute-start(bf16[64,512]{1,0:T(8,128)(2,1)S(1)} %get-tuple-element.43), channel_id=1, source_target_pairs={{0,24},{4,28},{8,0},{12,4},{16,8},{20,12},{24,16},{28,20},{32,56},... | collective-permute-start | bytes 196616 | tf_op jit(solution)/shard_map/ppermute | solution.py:239
  16.3 5.1 %collective-permute-start.4 = (bf16[64,512]{1,0:T(8,128)(2,1)S(1)}, bf16[64,512]{1,0:T(8,128)(2,1)S(1)}, u32[]{:S(2)}, u32[]{:S(2)}) collective-permute-start(bf16[64,512]{1,0:T(8,128)(2,1)S(1)} %get-tuple-element.41.r), channel_id=1, source_target_pairs={{0,8},{4,12},{8,16},{12,20},{16,24},{20,28},{24,0},{28,4},{32,40},... | collective-permute-start | bytes 196616 | tf_op jit(solution)/shard_map/ppermute | solution.py:239
  16.3 5.2 %collective-permute-start.11 = (bf16[64,512]{1,0:T(8,128)(2,1)S(1)}, bf16[64,512]{1,0:T(8,128)(2,1)S(1)}, u32[]{:S(2)}, u32[]{:S(2)}) collective-permute-start(bf16[64,512]{1,0:T(8,128)(2,1)S(1)} %collective-permute-done.8.b1), channel_id=1, source_target_pairs={{0,4},{4,0},{8,12},{12,8},{16,20},{20,16},{24,28},{28,24},{32,36},... | collective-permute-start | bytes 196616 | tf_op jit(solution)/shard_map/ppermute | solution.py:239
  19.0 3.3 %collective-permute-start.12 = (bf16[64,512]{1,0:T(8,128)(2,1)S(1)}, bf16[64,512]{1,0:T(8,128)(2,1)S(1)}, u32[]{:S(2)}, u32[]{:S(2)}) collective-permute-start(bf16[64,512]{1,0:T(8,128)(2,1)S(1)} %collective-permute-done.9.b2), channel_id=1, source_target_pairs={{0,4},{4,0},{8,12},{12,8},{16,20},{20,16},{24,28},{28,24},{32,36},... | collective-permute-start | bytes 196616 | tf_op jit(solution)/shard_map/ppermute | solution.py:239
  21.4 1.3 %collective-permute-start.13 = (bf16[64,512]{1,0:T(8,128)(2,1)S(1)}, bf16[64,512]{1,0:T(8,128)(2,1)S(1)}, u32[]{:S(2)}, u32[]{:S(2)}) collective-permute-start(bf16[64,512]{1,0:T(8,128)(2,1)S(1)} %collective-permute-done.10.b3), channel_id=1, source_target_pairs={{0,4},{4,0},{8,12},{12,8},{16,20},{20,16},{24,28},{28,24},{32,36},... | collective-permute-start | bytes 196616 | tf_op jit(solution)/shard_map/ppermute | solution.py:239
  23.0 6.7 %collective-permute-start.14 = (f32[64,512]{1,0:T(8,128)S(1)}, f32[64,512]{1,0:T(8,128)S(1)}, u32[]{:S(2)}, u32[]{:S(2)}) collective-permute-start(f32[64,512]{1,0:T(8,128)S(1)} %get-tuple-element.50), channel_id=1, source_target_pairs={{0,32},{4,36},{8,40},{12,44},{16,48},{20,52},{24,56},{28,60},{32,6... | collective-permute-start | bytes 393224 | tf_op jit(solution)/shard_map/ppermute | solution.py:239
  23.4 6.4 %collective-permute-start.15 = (f32[64,512]{1,0:T(8,128)S(1)}, f32[64,512]{1,0:T(8,128)S(1)}, u32[]{:S(2)}, u32[]{:S(2)}) collective-permute-start(f32[64,512]{1,0:T(8,128)S(1)} %get-tuple-element.51), channel_id=1, source_target_pairs={{0,64},{4,68},{8,72},{12,76},{16,80},{20,84},{24,88},{28,92},{32,9... | collective-permute-start | bytes 393224 | tf_op jit(solution)/shard_map/ppermute | solution.py:239
  24.7 5.8 %collective-permute-start.16 = (f32[64,512]{1,0:T(8,128)S(1)}, f32[64,512]{1,0:T(8,128)S(1)}, u32[]{:S(2)}, u32[]{:S(2)}) collective-permute-start(f32[64,512]{1,0:T(8,128)S(1)} %get-tuple-element.52), channel_id=1, source_target_pairs={{0,96},{4,100},{8,104},{12,108},{16,112},{20,116},{24,120},{28,124... | collective-permute-start | bytes 393224 | tf_op jit(solution)/shard_map/ppermute | solution.py:239
  30.6 4.0 %collective-permute-start.17 = (bf16[64,512]{1,0:T(8,128)(2,1)S(1)}, bf16[64,512]{1,0:T(8,128)(2,1)S(1)}, u32[]{:S(2)}, u32[]{:S(2)}) collective-permute-start(bf16[64,512]{1,0:T(8,128)(2,1)S(1)} %round_sum.1.h), channel_id=1, source_target_pairs={{0,4},{4,0},{8,12},{12,8},{16,20},{20,16},{24,28},{28,24},{32,36},... | collective-permute-start | bytes 196616 | tf_op jit(solution)/shard_map/ppermute | solution.py:239
  34.7 6.0 %collective-permute-start.19 = (bf16[128,512]{1,0:T(8,128)(2,1)S(1)}, bf16[128,512]{1,0:T(8,128)(2,1)S(1)}, u32[]{:S(2)}, u32[]{:S(2)}) collective-permute-start(bf16[128,512]{1,0:T(8,128)(2,1)S(1)} %get-tuple-element.54.j.f_1_), channel_id=1, source_target_pairs={{0,8},{4,12},{8,16},{12,20},{16,24},{20,28},{24,0},{28,4},{32,40},... | collective-permute-start | bytes 393224 | tf_op jit(solution)/shard_map/ppermute | solution.py:239
  35.0 7.0 %collective-permute-start.20 = (bf16[128,512]{1,0:T(8,128)(2,1)S(1)}, bf16[128,512]{1,0:T(8,128)(2,1)S(1)}, u32[]{:S(2)}, u32[]{:S(2)}) collective-permute-start(bf16[128,512]{1,0:T(8,128)(2,1)S(1)} %get-tuple-element.55), channel_id=1, source_target_pairs={{0,24},{4,28},{8,0},{12,4},{16,8},{20,12},{24,16},{28,20},{32,56},... | collective-permute-start | bytes 393224 | tf_op jit(solution)/shard_map/ppermute | solution.py:239
  37.4 6.9 %collective-permute-start.18 = (bf16[128,512]{1,0:T(8,128)(2,1)S(1)}, bf16[128,512]{1,0:T(8,128)(2,1)S(1)}, u32[]{:S(2)}, u32[]{:S(2)}) collective-permute-start(bf16[128,512]{1,0:T(8,128)(2,1)S(1)} %get-tuple-element.53), channel_id=1, source_target_pairs={{0,16},{4,20},{8,24},{12,28},{16,0},{20,4},{24,8},{28,12},{32,48},... | collective-permute-start | bytes 393224 | tf_op jit(solution)/shard_map/ppermute | solution.py:239
  45.7 10.0 %collective-permute-start.21 = (bf16[32,4352]{1,0:T(8,128)(2,1)S(1)}, bf16[32,4352]{1,0:T(8,128)(2,1)S(1)}, u32[]{:S(2)}, u32[]{:S(2)}) collective-permute-start(bf16[32,4352]{1,0:T(8,128)(2,1)S(1)} %get-tuple-element.59), channel_id=1, source_target_pairs={{0,1},{1,2},{2,3},{3,0},{4,6},{5,7},{6,4},{7,5},{8,9},{9,10},{10,1... | collective-permute-start | bytes 835592 | tf_op jit(solution)/shard_map/ppermute | solution.py:247
  49.4 13.2 %collective-permute-start.22 = (bf16[32,4352]{1,0:T(8,128)(2,1)S(1)}, bf16[32,4352]{1,0:T(8,128)(2,1)S(1)}, u32[]{:S(2)}, u32[]{:S(2)}) collective-permute-start(bf16[32,4352]{1,0:T(8,128)(2,1)S(1)} %get-tuple-element.60), channel_id=1, source_target_pairs={{0,3},{1,0},{2,1},{3,2},{4,7},{5,4},{6,5},{7,6},{8,11},{9,8},{10,9... | collective-permute-start | bytes 835592 | tf_op jit(solution)/shard_map/ppermute | solution.py:247
  49.8 13.0 %collective-permute-start.23 = (bf16[32,4352]{1,0:T(8,128)(2,1)S(1)}, bf16[32,4352]{1,0:T(8,128)(2,1)S(1)}, u32[]{:S(2)}, u32[]{:S(2)}) collective-permute-start(bf16[32,4352]{1,0:T(8,128)(2,1)S(1)} %get-tuple-element.64), channel_id=1, source_target_pairs={{0,2},{1,3},{2,0},{3,1},{4,5},{5,6},{6,7},{7,4},{8,10},{9,11},{10,... | collective-permute-start | bytes 835592 | tf_op jit(solution)/shard_map/ppermute | solution.py:247
